TPU v7x, 32 devices: a whole 2x2x4 slice. The times are simulated.
32 devices in a mesh: row: 8 (over y, x, core), col: 4 (over z).
Axes of the slice: x: 2, y: 2, z: 4, core: 2. Of those that a mesh axis runs over, the one named last changes fastest.
Arguments:
- layer_in: bfloat16 [2, 1024, 2048], P(None, 'row', 'col'), may hold values from -6 to 6
- out_grad: bfloat16 [2, 1024, 2048], P(None, 'row', 'col'), may hold values from -6 to 6
- lengths: int32 [2, 4], replicated, may hold values from 1 to 682, 1024 in all within a row
- token_order: int32 [2, 1024], replicated, may hold values from 0 to 1023, each once within a row
- choices: int32 [2, 1024, 8], P(None, 'row'), may hold values from 0 to 15, all different within a row
- norm_gain: float32 [2048], replicated, may hold values from 0.5 to 1.5
- w_query: bfloat16 [2048, 4096], P('row', 'col'), may hold values from -0.125 to 0.125
- w_key: bfloat16 [2048, 512], P('row', 'col'), may hold values from -0.125 to 0.125
- w_value: bfloat16 [2048, 512], P('row', 'col'), may hold values from -0.125 to 0.125
- query_gain: float32 [128], replicated, may hold values from 0.5 to 1.5
- key_gain: float32 [128], replicated, may hold values from 0.5 to 1.5
- w_out: bfloat16 [2048, 4096], P('row', 'col'), may hold values from -0.75 to 0.75
- ffn_gain: float32 [2048], replicated, may hold values from 0.5 to 1.5
- w_router: bfloat16 [2048, 16], P('row'), may hold values from -0.0625 to 0.0625
- w_gate: bfloat16 [2048, 12288], P('row', 'col'), may hold values from -0.125 to 0.125
- w_up: bfloat16 [2048, 12288], P('row', 'col'), may hold values from -0.125 to 0.125
- w_down: bfloat16 [2048, 12288], P('row', 'col'), may hold values from -0.875 to 0.875
Outputs:
- layer_out: bfloat16 [2, 1024, 2048], P(None, 'row', 'col')
- input_grad: bfloat16 [2, 1024, 2048], P(None, 'row', 'col')
- grad_norm_gain: float32 [2048], replicated
- grad_w_query: float32 [2048, 4096], P('row', 'col')
- grad_w_key: float32 [2048, 512], P('row', 'col')
- grad_w_value: float32 [2048, 512], P('row', 'col')
- grad_query_gain: float32 [128], replicated
- grad_key_gain: float32 [128], replicated
- grad_w_out: float32 [2048, 4096], P('row', 'col')
- grad_ffn_gain: float32 [2048], replicated
- grad_w_router: float32 [2048, 16], P('row')
- grad_w_gate: float32 [2048, 12288], P('row', 'col')
- grad_w_up: float32 [2048, 12288], P('row', 'col')
- grad_w_down: float32 [2048, 12288], P('row', 'col')
Inputs may be any that keep to these rules, and one draw needn't show every extreme that they name: `lengths`: each row sums to 1024 and its largest entry is 682. `token_order`: each row holds every number from 0 to 1023 once. `choices`: the 8 entries of a token are distinct.
All inputs are finite; a program needn't handle non-finite values.
Results may differ from a plain program's by a relative error of at most 0.015.
Values may be sent and summed in bfloat16 or wider, within the bound.
No kernel may reach another device: no remote copies, remote signals or barrier semaphores. Data moves between devices by JAX's collectives and lax.ppermute only.
A program may use at most 576 MiB of HBM per device.

v0:
```python
import math

import jax
import jax.numpy as jnp
from jax import lax
from jax.sharding import PartitionSpec as P

EPS = 1e-06
THETA = 1000000.0
NEGATIVE = -1e30


def normed(tensor, gain_row):
    return tensor * lax.rsqrt(jnp.mean(tensor * tensor, axis=-1, keepdims=True) + EPS) * gain_row


def rotated(tensor, places):
    half_size = tensor.shape[-1] // 2
    frequency = jnp.exp(
        jnp.arange(half_size, dtype=jnp.float32) * (-2.0 * math.log(THETA) / tensor.shape[-1])
    )
    angles = places.astype(jnp.float32)[:, None] * frequency[None, :]
    cosine = jnp.cos(angles)[:, None, :]
    sine_part = jnp.sin(angles)[:, None, :]
    first_half = tensor[..., :half_size]
    second = tensor[..., half_size:]
    return jnp.concatenate(
        [first_half * cosine - second * sine_part, second * cosine + first_half * sine_part],
        axis=-1,
    )


def token_places(lengths, token_order):
    seq_ends = jnp.cumsum(lengths)
    passed = token_order[:, None] >= seq_ends[None, :]
    seq_of = jnp.sum(passed.astype(jnp.int32), axis=1)
    start_of = jnp.sum(jnp.where(passed, lengths[None, :], 0), axis=1)
    return (seq_of, token_order - start_of)


def contract(tokens, weight):
    return jnp.dot(tokens, weight, preferred_element_type=jnp.float32)


def col_total(tensor):
    return lax.psum(tensor, "col")


def feature_gather(tensor):
    return lax.all_gather(tensor, "col", axis=1, tiled=True)


def branch_total(tensor):
    return lax.psum_scatter(tensor, "col", scatter_dimension=1, tiled=True)


def stash_fold(tokens, members, pieces):
    buffers = tuple((piece for piece in pieces))
    partial_value = tuple((contract(tokens, pieces[member]) for member in members))
    return (buffers, partial_value)


def fetch_attention(weights, tokens, members):
    return stash_fold(
        tokens,
        members,
        (
            lax.all_gather(weights[0], "row", axis=0, tiled=True),
            lax.all_gather(weights[1], "row", axis=0, tiled=True),
            lax.all_gather(weights[2], "row", axis=0, tiled=True),
            lax.all_gather(weights[3], "row", axis=0, tiled=True),
        ),
    )


def fetch_experts(weights, tokens, members):
    return stash_fold(
        tokens,
        members,
        (
            lax.all_gather(weights[0], "row", axis=0, tiled=True),
            lax.all_gather(weights[1], "row", axis=0, tiled=True),
            lax.all_gather(weights[2], "row", axis=0, tiled=True),
            lax.all_gather(weights[3], "row", axis=0, tiled=True),
        ),
    )


def reduce_terms(kept):
    summed = None
    for entry in kept:
        (
            normed_one,
            dq_low,
            dk_low,
            dv_low,
            grad_feats,
            attended,
            normed_two,
            logit_low,
            d_gate,
            d_up,
            out_feats,
            weighted,
        ) = entry
        pieces = [
            jnp.einsum("td,th->dh", normed_one, dq_low, preferred_element_type=jnp.float32),
            jnp.einsum("td,th->dh", normed_one, dk_low, preferred_element_type=jnp.float32),
            jnp.einsum("td,th->dh", normed_one, dv_low, preferred_element_type=jnp.float32),
            jnp.einsum("td,th->dh", grad_feats, attended, preferred_element_type=jnp.float32),
            jnp.einsum("td,te->de", normed_two, logit_low, preferred_element_type=jnp.float32),
            jnp.einsum("td,tc->dc", normed_two, d_gate, preferred_element_type=jnp.float32),
            jnp.einsum("td,tc->dc", normed_two, d_up, preferred_element_type=jnp.float32),
            jnp.einsum("td,tc->dc", out_feats, weighted, preferred_element_type=jnp.float32),
        ]
        joined = jnp.concatenate(pieces, axis=1)
        summed = joined
    return lax.psum_scatter(summed, "row", scatter_dimension=0, tiled=True)


def per_device(
    layer_in,
    out_grad,
    lengths,
    token_order,
    choices,
    norm_gain,
    w_query,
    w_key,
    w_value,
    query_gain,
    key_gain,
    w_out,
    ffn_gain,
    w_router,
    w_gate,
    w_up,
    w_down,
):
    micro_count = layer_in.shape[0]
    tok_rows = layer_in.shape[1]
    width_part = layer_in.shape[2]
    width = width_part * lax.axis_size("col")
    col_at = lax.axis_index("col")
    row_at = lax.axis_index("row")
    head_size = query_gain.shape[0]
    local_heads = w_query.shape[1] // head_size
    local_kv = w_key.shape[1] // head_size
    half_group = local_heads // local_kv // 2
    expert_count = w_router.shape[1]
    expert_cols = w_gate.shape[1]
    unit_count = expert_cols // expert_count
    score_scale = 1.0 / math.sqrt(head_size)
    gain_one = lax.dynamic_slice_in_dim(norm_gain, col_at * width_part, width_part)
    gain_two = lax.dynamic_slice_in_dim(ffn_gain, col_at * width_part, width_part)
    attn_set = (w_query, w_key, w_value, w_out)
    expert_set = (w_router, w_gate, w_up, w_down)

    def to_blocks(tensor):
        split = tensor.reshape(tok_rows, local_kv, 2, half_group, head_size)
        return split.transpose(1, 2, 3, 0, 4).reshape(local_kv * 2, half_group, tok_rows, head_size)

    def from_blocks(tensor):
        split = tensor.reshape(local_kv, 2, half_group, tok_rows, head_size)
        return split.transpose(3, 0, 1, 2, 4).reshape(tok_rows, local_heads * head_size)

    def key_blocks(tensor):
        split = tensor.reshape(tensor.shape[0], local_kv, head_size).transpose(1, 0, 2)
        return jnp.repeat(split, 2, axis=0)

    gain_grad_one = jnp.zeros((width_part,), jnp.float32)
    gain_grad_two = jnp.zeros((width_part,), jnp.float32)
    qgain_grad = jnp.zeros((head_size,), jnp.float32)
    kgain_grad = jnp.zeros((head_size,), jnp.float32)
    grad_totals = None
    kept = []
    layer_outs = []
    input_grads = []
    for batch_index in range(micro_count):
        local_in = layer_in[batch_index].astype(jnp.float32)
        dealt = token_order[batch_index]
        seq_of, places = token_places(lengths[batch_index], dealt)
        own_order = lax.dynamic_slice_in_dim(dealt, row_at * tok_rows, tok_rows)
        own_seq = lax.dynamic_slice_in_dim(seq_of, row_at * tok_rows, tok_rows)
        own_places = lax.dynamic_slice_in_dim(places, row_at * tok_rows, tok_rows)
        allowed = (own_seq[:, None] == seq_of[None, :]) & (dealt[None, :] <= own_order[:, None])
        chosen = jnp.any(
            choices[batch_index][:, :, None]
            == jnp.arange(expert_count, dtype=jnp.int32)[None, None, :],
            axis=1,
        )
        scale_one = lax.rsqrt(col_total(jnp.sum(local_in * local_in, axis=1)) / width + EPS)[
            :, None
        ]
        normed_one = feature_gather((local_in * scale_one * gain_one).astype(jnp.bfloat16))
        attn_now, projected = fetch_attention(attn_set, normed_one, (0, 1, 2))
        query_pre, key_pre, value_pre = projected

        def shape_heads(projection, gain_row):
            split = projection.reshape(tok_rows, -1, head_size)
            return rotated(normed(split, gain_row), own_places)

        queries, query_back = jax.vjp(shape_heads, query_pre, query_gain)
        key_now, key_back = jax.vjp(shape_heads, key_pre, key_gain)
        queries = queries.astype(jnp.bfloat16)
        key_now = key_now.astype(jnp.bfloat16).reshape(tok_rows, -1)
        value_now = value_pre.astype(jnp.bfloat16)
        key_all, value_all = (
            lax.all_gather(key_now, "row", axis=0, tiled=True),
            lax.all_gather(value_now, "row", axis=0, tiled=True),
        )
        query_blocks = to_blocks(queries)
        key_block_all = key_blocks(key_all)
        value_block_all = key_blocks(value_all)

        def forward_block(pieces):
            query_block, key_block, value_block = pieces
            scores = (
                jnp.einsum(
                    "gqd,kd->gqk", query_block, key_block, preferred_element_type=jnp.float32
                )
                * score_scale
            )
            scores = jnp.where(allowed[None], scores, NEGATIVE)
            peak = jnp.max(scores, axis=-1, keepdims=True)
            log_total = peak + jnp.log(jnp.sum(jnp.exp(scores - peak), axis=-1, keepdims=True))
            probs = jnp.exp(scores - log_total).astype(jnp.bfloat16)
            return (
                jnp.einsum("gqk,kd->gqd", probs, value_block, preferred_element_type=jnp.float32),
                log_total,
            )

        mixed, log_totals = lax.map(forward_block, (query_blocks, key_block_all, value_block_all))
        attended = from_blocks(mixed).astype(jnp.bfloat16)
        attn_part = branch_total(
            jnp.einsum("th,dh->td", attended, attn_now[3], preferred_element_type=jnp.float32)
        )
        residual = local_in + attn_part
        scale_two = lax.rsqrt(col_total(jnp.sum(residual * residual, axis=1)) / width + EPS)[
            :, None
        ]
        normed_two = feature_gather((residual * scale_two * gain_two).astype(jnp.bfloat16))
        expert_now, routed = fetch_experts(expert_set, normed_two, (0, 1, 2))
        logits, gate_pre, up_pre = routed
        gate_probs = jax.nn.softmax(jnp.where(chosen, logits, NEGATIVE), axis=-1)
        probs_wide = jnp.tile(gate_probs, (1, unit_count))
        sigmoid_gate = jax.nn.sigmoid(gate_pre)
        swish = gate_pre * sigmoid_gate
        active = swish * up_pre
        weighted = (probs_wide * active).astype(jnp.bfloat16)
        expert_part = branch_total(
            jnp.einsum("tc,dc->td", weighted, expert_now[3], preferred_element_type=jnp.float32)
        )
        layer_outs.append((residual + expert_part).astype(jnp.bfloat16))
        out_feats = feature_gather(out_grad[batch_index])
        expert_now, (back_weighted,) = fetch_experts(expert_set, out_feats, (3,))
        gate_grad = col_total(
            jnp.sum((active * back_weighted).reshape(tok_rows, unit_count, expert_count), axis=1)
        )
        logit_grad = gate_probs * (
            gate_grad - jnp.sum(gate_probs * gate_grad, axis=-1, keepdims=True)
        )
        logit_low = logit_grad.astype(jnp.bfloat16)
        back_active = probs_wide * back_weighted
        d_gate = (
            back_active * up_pre * sigmoid_gate * (1.0 + gate_pre * (1.0 - sigmoid_gate))
        ).astype(jnp.bfloat16)
        d_up = (back_active * swish).astype(jnp.bfloat16)
        router_term = jnp.einsum(
            "te,de->td", logit_low, expert_now[0], preferred_element_type=jnp.float32
        )
        spread_two = jnp.einsum(
            "tc,dc->td", d_gate, expert_now[1], preferred_element_type=jnp.float32
        )
        spread_two = spread_two + jnp.einsum(
            "tc,dc->td", d_up, expert_now[2], preferred_element_type=jnp.float32
        )
        spread_two = spread_two + jnp.where(col_at == 0, router_term, 0.0)
        grad_normed_two = branch_total(spread_two)
        scaled_two = grad_normed_two * gain_two
        inner_two = col_total(jnp.sum(scaled_two * residual, axis=1))[:, None]
        grad_residual = (
            out_grad[batch_index].astype(jnp.float32)
            + scale_two * scaled_two
            - residual * scale_two**3 * inner_two / width
        )
        gain_grad_two = gain_grad_two + jnp.sum(grad_normed_two * residual * scale_two, axis=0)
        grad_feats = feature_gather(grad_residual.astype(jnp.bfloat16))
        attn_now, (back_attended,) = fetch_attention(attn_set, grad_feats, (3,))
        grad_blocks = to_blocks(back_attended.astype(jnp.bfloat16))

        def backward_block(pieces):
            query_block, key_block, value_block, total_block, grad_block = pieces
            scores = (
                jnp.einsum(
                    "gqd,kd->gqk", query_block, key_block, preferred_element_type=jnp.float32
                )
                * score_scale
            )
            scores = jnp.where(allowed[None], scores, NEGATIVE)
            probs = jnp.exp(scores - total_block)
            prob_low = probs.astype(jnp.bfloat16)
            grad_probs = jnp.einsum(
                "gqd,kd->gqk", grad_block, value_block, preferred_element_type=jnp.float32
            )
            centre = jnp.sum(probs * grad_probs, axis=-1, keepdims=True)
            grad_scores = (probs * (grad_probs - centre)).astype(jnp.bfloat16)
            grad_query = (
                jnp.einsum(
                    "gqk,kd->gqd", grad_scores, key_block, preferred_element_type=jnp.float32
                )
                * score_scale
            )
            grad_key = (
                jnp.einsum(
                    "gqk,gqd->kd", grad_scores, query_block, preferred_element_type=jnp.float32
                )
                * score_scale
            )
            grad_value = jnp.einsum(
                "gqk,gqd->kd", prob_low, grad_block, preferred_element_type=jnp.float32
            )
            return (grad_query, grad_key, grad_value)

        grad_query, grad_key, grad_value = lax.map(
            backward_block, (query_blocks, key_block_all, value_block_all, log_totals, grad_blocks)
        )
        seq_total = grad_key.shape[1]
        grad_key = (
            grad_key.reshape(local_kv, 2, seq_total, head_size)
            .sum(axis=1)
            .transpose(1, 0, 2)
            .reshape(seq_total, -1)
        )
        grad_value = (
            grad_value.reshape(local_kv, 2, seq_total, head_size)
            .sum(axis=1)
            .transpose(1, 0, 2)
            .reshape(seq_total, -1)
        )
        own_key_grad, own_value_grad = (
            lax.psum_scatter(grad_key, "row", scatter_dimension=0, tiled=True),
            lax.psum_scatter(grad_value, "row", scatter_dimension=0, tiled=True),
        )
        query_pre_grad, query_gain_part = query_back(
            from_blocks(grad_query).reshape(tok_rows, local_heads, head_size)
        )
        key_pre_grad, key_gain_part = key_back(own_key_grad.reshape(tok_rows, local_kv, head_size))
        qgain_grad = qgain_grad + query_gain_part
        kgain_grad = kgain_grad + key_gain_part
        dq_low = query_pre_grad.astype(jnp.bfloat16)
        dk_low = key_pre_grad.astype(jnp.bfloat16)
        dv_low = own_value_grad.astype(jnp.bfloat16)
        spread_one = jnp.einsum(
            "th,dh->td", dq_low, attn_now[0], preferred_element_type=jnp.float32
        )
        spread_one = spread_one + jnp.einsum(
            "th,dh->td", dk_low, attn_now[1], preferred_element_type=jnp.float32
        )
        spread_one = spread_one + jnp.einsum(
            "th,dh->td", dv_low, attn_now[2], preferred_element_type=jnp.float32
        )
        grad_normed_one = branch_total(spread_one)
        scaled_one = grad_normed_one * gain_one
        inner_one = col_total(jnp.sum(scaled_one * local_in, axis=1))[:, None]
        grad_in = (
            grad_residual + scale_one * scaled_one - local_in * scale_one**3 * inner_one / width
        )
        input_grads.append(grad_in.astype(jnp.bfloat16))
        gain_grad_one = gain_grad_one + jnp.sum(grad_normed_one * local_in * scale_one, axis=0)
        kept.append(
            (
                normed_one,
                dq_low,
                dk_low,
                dv_low,
                grad_feats,
                attended,
                normed_two,
                logit_low,
                d_gate,
                d_up,
                out_feats,
                weighted,
            )
        )
        reduced = reduce_terms(kept[-1:])
        grad_totals = reduced if grad_totals is None else grad_totals + reduced
    widths = [
        w_query.shape[1],
        w_key.shape[1],
        w_value.shape[1],
        w_out.shape[1],
        expert_count,
        expert_cols,
        expert_cols,
        expert_cols,
    ]
    split_grads = []
    offset = 0
    for size_cols in widths:
        split_grads.append(grad_totals[:, offset : offset + size_cols])
        offset = offset + size_cols
    spread_gain_one = lax.dynamic_update_slice_in_dim(
        jnp.zeros((width,), jnp.float32), gain_grad_one, col_at * width_part, 0
    )
    spread_gain_two = lax.dynamic_update_slice_in_dim(
        jnp.zeros((width,), jnp.float32), gain_grad_two, col_at * width_part, 0
    )
    grad_norm_gain, grad_ffn_gain, grad_query_gain, grad_key_gain = lax.psum(
        (spread_gain_one, spread_gain_two, qgain_grad, kgain_grad), ("row", "col")
    )
    return (
        jnp.stack(layer_outs),
        jnp.stack(input_grads),
        grad_norm_gain,
        split_grads[0],
        split_grads[1],
        split_grads[2],
        grad_query_gain,
        grad_key_gain,
        split_grads[3],
        grad_ffn_gain,
        split_grads[4],
        split_grads[5],
        split_grads[6],
        split_grads[7],
    )


def solution(mesh):
    placed = (
        P(None, "row", "col"),
        P(None, "row", "col"),
        P(),
        P(),
        P(None, "row", None),
        P(),
        P("row", "col"),
        P("row", "col"),
        P("row", "col"),
        P(),
        P(),
        P("row", "col"),
        P(),
        P("row", None),
        P("row", "col"),
        P("row", "col"),
        P("row", "col"),
    )
    return jax.shard_map(
        per_device,
        mesh=mesh,
        in_specs=placed,
        out_specs=(
            P(None, "row", "col"),
            P(None, "row", "col"),
            P(),
            P("row", "col"),
            P("row", "col"),
            P("row", "col"),
            P(),
            P(),
            P("row", "col"),
            P(),
            P("row", None),
            P("row", "col"),
            P("row", "col"),
            P("row", "col"),
        ),
        check_vma=False,
    )
```

profile of v0, /device:TPU:0, one launch (start us, length us, event | category | flops | bytes accessed | tf_op | source)
XLA Modules:
  0.0 2273.4 jit_solution(16585445238262980628)
XLA Ops:
  10.6 13.4 all-reduce.14
  25.8 14.8 all_gather.40
  52.3 16.1 all_gather.96
  157.7 17.4 all-gather.1
  175.2 22.5 all-gather
  211.1 15.1 all_gather.91
  226.5 15.8 all_gather.99
  242.6 29.9 %all-gather.14.cloned.1.call-done = bf16[2048,3072]{1,0:T(8,128)(2,1)} async-done(((bf16[256,3072]{1,0:T(8,128)(2,1)}), bf16[2048,3072]{1,0:T(8,128)(2,1)}) %all-gather.14.cloned.1.call-update) | async-done | bytes 12582928 | tf_op jit(solution)/shard_map/all_gather | solution.py:83
  279.9 66.4 %all-gather.12.cloned.1.call-done = bf16[2048,3072]{1,0:T(8,128)(2,1)} async-done(((bf16[256,3072]{1,0:T(8,128)(2,1)}), bf16[2048,3072]{1,0:T(8,128)(2,1)}) %all-gather.12.cloned.1.call-update) | async-done | bytes 12582928 | tf_op jit(solution)/shard_map/all_gather | solution.py:82
  353.8 66.5 %all-gather.16.cloned.1.call-done = bf16[2048,3072]{1,0:T(8,128)(2,1)} async-done(((bf16[256,3072]{1,0:T(8,128)(2,1)}), bf16[2048,3072]{1,0:T(8,128)(2,1)}) %all-gather.16.cloned.1.call-update) | async-done | bytes 12582928 | tf_op jit(solution)/shard_map/all_gather | solution.py:84
  457.0 18.7 all-reduce.12
  578.3 11.5 fusion.229
  590.1 13.2 convolution_bitcast_fusion.7
  630.5 16.1 all_gather.101
  662.2 15.5 all_gather.103
  721.4 33.2 %reduce-scatter.31.cloned.1.call-done = f32[128,128]{0,1:T(8,128)} async-done(((f32[1024,128]{0,1:T(8,128)}), f32[128,128]{0,1:T(8,128)}) %reduce-scatter.31.cloned.1.call-update) | async-done | bytes 65552 | tf_op jit(solution)/shard_map/reduce_scatter | solution.py:342
  759.1 32.5 %reduce-scatter.25.cloned.1.call-done = f32[128,128]{1,0:T(8,128)} async-done(((f32[1024,128]{1,0:T(8,128)}), f32[128,128]{1,0:T(8,128)}) %reduce-scatter.25.cloned.1.call-update) | async-done | bytes 65552 | tf_op jit(solution)/shard_map/reduce_scatter | solution.py:343
  815.3 13.7 reduce-scatter.33.cloned.1.call-done
  847.1 124.5 %concatenate.70 = f32[2048,11536]{1,0:T(8,128)} concatenate(f32[2048,1024]{1,0:T(8,128)} %fusion.120, f32[2048,128]{1,0:T(8,128)S(1)} %fusion.221, f32[2048,128]{1,0:T(8,128)} %fusion.179, f32[2048,1024]{1,0:T(8,128)} %fusion.222, f32[2048,16]{1,0:T(8,128)S(1)} %copy-done.33, f32[2048,3072]{1,0:T(8,128)} %fusion.224, f32[2048,3072]{1,0:T(8,128)} %fusion.225, ...), dimensions={1} | concatenate | bytes 189005824 | tf_op jit(solution)/shard_map/concatenate | solution.py:116
  973.2 122.7 %concatenate.71 = f32[2048,11536]{1,0:T(8,128)} concatenate(f32[2048,1024]{1,0:T(8,128)} %fusion.116, f32[2048,128]{1,0:T(8,128)S(1)} %fusion.226, f32[2048,128]{1,0:T(8,128)} %fusion.176, f32[2048,1024]{1,0:T(8,128)} %fusion.227, f32[2048,16]{1,0:T(8,128)S(1)} %copy-done.32, f32[2048,3072]{1,0:T(8,128)} %fusion.229, f32[2048,3072]{1,0:T(8,128)} %fusion.230, ...), dimensions={1} | concatenate | bytes 189005824 | tf_op jit(solution)/shard_map/concatenate | solution.py:116
  1095.9 91.5 %add.314 = f32[2048,11536]{1,0:T(8,128)} add(f32[2048,11536]{1,0:T(8,128)} %concatenate.70, f32[2048,11536]{1,0:T(8,128)} %concatenate.71) | non-fusion elementwise | flops 23625728 | bytes 283508736 | tf_op jit(solution)/shard_map/add | solution.py:388
  1191.5 11.7 all-reduce.10
  1203.5 38.7 %all-reduce.9 = (f32[2048]{0:T(1024)}, f32[128]{0:T(128)}, f32[128]{0:T(128)}, f32[2048]{0:T(1024)}) all-reduce(f32[2048]{0:T(1024)S(1)} %add_dynamic-update-slice_fusion.1, f32[128]{0:T(128)S(1)} %add.311, f32[128]{0:T(128)S(1)} %add.312, f32[2048]{0:T(1024)S(1)} %add_dynamic-update-slice_fusion), channel_id=1, replica_groups=mesh['row'=8,'col'=4] {'row','col'}, use_global_device_ids=true, to_apply=%region_74.75 | all-reduce | flops 4352 | bytes 34816 | tf_op jit(solution)/shard_map/psum | solution.py:410
  1244.2 1005.2 %all-reduce.17.cloned.1.call-done = f32[2048,11536]{1,0:T(8,128)} async-done(((f32[2048,11536]{1,0:T(8,128)}), f32[2048,11536]{1,0:T(8,128)}) %all-reduce.17.cloned.1.call-update) | async-done | bytes 94502928
  (603 shorter events, 457.4 us)
Async XLA Ops:
  7.2 112.3 %all-gather.8.cloned.1.call-start = ((), (), s32[]{:S(2)}) async-start(), calls=%async_computation.12 | async-start | bytes 4718592 | tf_op jit(solution)/shard_map/all_gather | solution.py:68
  7.9 123.9 %all-gather.10.cloned.1.call-start = ((), (), s32[]{:S(2)}) async-start(), calls=%async_computation.13 | async-start | bytes 4718592 | tf_op jit(solution)/shard_map/all_gather | solution.py:71
  8.7 189.0 %reduce-scatter.13.cloned.1.call-start = ((), (), s32[]{:S(2)}) async-start(), calls=%async_computation.14 | async-start | bytes 1310720 | tf_op jit(solution)/shard_map/reduce_scatter | solution.py:54
  8.8 109.8 %copy-start.117 = (f32[64]{0:T(128)}, f32[64]{0:T(128)S(1)}, u32[]{:S(2)}) copy-start(f32[64]{0:T(128)S(1)} %multiply_exponential_fusion) | copy-start | bytes 772
  40.6 79.0 %copy-start.3 = (bf16[128,2048]{1,0:T(8,128)(2,1)}, bf16[128,2048]{1,0:T(8,128)(2,1)S(1)}, u32[]{:S(2)}) copy-start(bf16[128,2048]{1,0:T(8,128)(2,1)S(1)} %all_gather.40) | copy-start | bytes 1572868
  52.3 66.3 %copy-start.102 = (f32[128]{0:T(128)}, f32[128]{0:T(128)S(1)}, u32[]{:S(2)}) copy-start(f32[128]{0:T(128)S(1)} %get-tuple-element.663) | copy-start | bytes 1540
  52.3 66.3 %copy-start.104 = (f32[128]{0:T(128)}, f32[128]{0:T(128)S(1)}, u32[]{:S(2)}) copy-start(f32[128]{0:T(128)S(1)} %get-tuple-element.664) | copy-start | bytes 1540
  136.7 63.1 %reduce-scatter.17.cloned.1.call-start = ((), (), s32[]{:S(2)}) async-start(), calls=%async_computation.19 | async-start | bytes 1310720 | tf_op jit(solution)/shard_map/reduce_scatter | solution.py:54
  146.7 125.7 %all-gather.14.cloned.1.call-start = ((), (), s32[]{:S(2)}) async-start(), calls=%async_computation.16 | async-start | bytes 14155776 | tf_op jit(solution)/shard_map/all_gather | solution.py:83
  147.3 199.0 %all-gather.12.cloned.1.call-start = ((), (), s32[]{:S(2)}) async-start(), calls=%async_computation.15 | async-start | bytes 14155776 | tf_op jit(solution)/shard_map/all_gather | solution.py:82
  147.9 272.5 %all-gather.16.cloned.1.call-start = ((), (), s32[]{:S(2)}) async-start(), calls=%async_computation.17 | async-start | bytes 14155776 | tf_op jit(solution)/shard_map/all_gather | solution.py:84
  148.6 464.9 %reduce-scatter.21.cloned.1.call-start = ((), (), s32[]{:S(2)}) async-start(), calls=%async_computation.21 | async-start | bytes 1310720 | tf_op jit(solution)/shard_map/reduce_scatter | solution.py:54
  505.1 108.4 %reduce-scatter.29.cloned.1.call-start = ((), (), s32[]{:S(2)}) async-start(), calls=%async_computation.25 | async-start | bytes 1310720 | tf_op jit(solution)/shard_map/reduce_scatter | solution.py:54
  546.0 78.0 %reduce-scatter.19.cloned.1.call-start = ((), (), s32[]{:S(2)}) async-start(), calls=%async_computation.20 | async-start | bytes 1310720 | tf_op jit(solution)/shard_map/reduce_scatter | solution.py:54
  568.1 60.0 %reduce-scatter.15.cloned.1.call-start = ((), (), s32[]{:S(2)}) async-start(), calls=%async_computation.18 | async-start | bytes 1310720 | tf_op jit(solution)/shard_map/reduce_scatter | solution.py:54
  589.8 131.5 %reduce-scatter.23.cloned.1.call-start = ((), (), s32[]{:S(2)}) async-start(), calls=%async_computation.22 | async-start | bytes 589824 | tf_op jit(solution)/shard_map/reduce_scatter | solution.py:342
  684.9 69.7 %reduce-scatter.31.cloned.1.call-start = ((), (), s32[]{:S(2)}) async-start(), calls=%async_computation.26 | async-start | bytes 589824 | tf_op jit(solution)/shard_map/reduce_scatter | solution.py:342
  702.5 89.2 %reduce-scatter.25.cloned.1.call-start = ((), (), s32[]{:S(2)}) async-start(), calls=%async_computation.23 | async-start | bytes 589824 | tf_op jit(solution)/shard_map/reduce_scatter | solution.py:343
  707.0 122.0 %reduce-scatter.33.cloned.1.call-start = ((), (), s32[]{:S(2)}) async-start(), calls=%async_computation.27 | async-start | bytes 589824 | tf_op jit(solution)/shard_map/reduce_scatter | solution.py:343
  716.5 473.7 %reduce-scatter.27.cloned.1.call-start = ((), (), s32[]{:S(2)}) async-start(), calls=%async_computation.24 | async-start | bytes 1310720 | tf_op jit(solution)/shard_map/reduce_scatter | solution.py:54
  721.4 70.3 %copy-start.18 = (bf16[2048,128]{1,0:T(8,128)(2,1)S(1)}, bf16[2048,128]{1,0:T(8,128)(2,1)}, u32[]{:S(2)}) copy-start(bf16[2048,128]{1,0:T(8,128)(2,1)} %copy-done.17) | copy-start | bytes 1572868
  794.2 396.0 %reduce-scatter.35.cloned.1.call-start = ((), (), s32[]{:S(2)}) async-start(), calls=%async_computation.28 | async-start | bytes 1310720 | tf_op jit(solution)/shard_map/reduce_scatter | solution.py:54
  831.6 1417.8 %all-reduce.17.cloned.1.call-start = ((), (), s32[]{:S(2)}) async-start(), calls=%async_computation.29 | async-start | bytes 190840832
  847.1 124.8 %copy-start.83 = (f32[128,128]{1,0:T(8,128)S(1)}, f32[128,128]{1,0:T(8,128)}, u32[]{:S(2)}) copy-start(f32[128,128]{1,0:T(8,128)} %reduce-scatter.33.cloned.1.call-done) | copy-start | bytes 196612
  (150 other events, 1726.8 us)
Sparse Core Ops, SparseCore 0:
  9.9 40.1 all-gather.7
  52.0 39.5 all-gather.9
  136.8 25.3 reduce-scatter.12
  165.0 34.7 reduce-scatter.16
  201.5 70.8 all-gather.13
  274.2 72.1 all-gather.11
  348.2 72.1 all-gather.15
  505.2 24.3 reduce-scatter.20
  546.1 24.3 reduce-scatter.28
  573.3 25.7 reduce-scatter.18
  602.1 26.0 reduce-scatter.14
  685.0 32.0 reduce-scatter.22
  720.4 34.1 reduce-scatter.30
  757.5 34.1 reduce-scatter.24
  794.9 34.0 reduce-scatter.32
  831.7 27.1 reduce-scatter.26
  861.7 25.7 reduce-scatter.34
  1187.7 1061.6 all-reduce.16
where the time goes:
time: 2290 us; the launch traced here: 2270 us
  waiting for transfers between devices  1260 us (55%)
  local copies, waits for them, and re-layouts  305 us (13%)
  blocking collectives  301 us (13%)
  matrix products  248 us (11%)
  other arithmetic  142 us (6%)
    unnamed x19, waiting for transfers between devices  1010 us
    concatenate x2, local copies, waits for them, and re-layouts, reduce_terms(): joined = jnp.concatenate(pieces, axis=1)  247 us
    all_gather x8, blocking collectives, feature_gather(): return lax.all_gather(tensor, 'col', axis=1, tiled=True)  133 us
    add x1, other arithmetic, per_device(): grad_totals = reduced if grad_totals is None else grad_totals + reduced  91.5 us
    all_gather x1, waiting for transfers between devices, fetch_experts(): lax.all_gather(weights[3], 'row', axis=0, tiled=True)  66.5 us
    all_gather x1, waiting for transfers between devices, fetch_experts(): lax.all_gather(weights[1], 'row', axis=0, tiled=True)  66.4 us
    psum x5, blocking collectives, col_total(): return lax.psum(tensor, 'col')  62.5 us
    dot_general x16, matrix products, contract(): return jnp.dot(tokens, weight, preferred_element_type=jnp.float32)  55.8 us
  transfers between devices with their start and end apart: 18, of which 9 were waited for; matrix products, arithmetic and copies ran while one was open for 25% of the time, Pallas kernels for 0%

commit v1 on v0

v1 whole, which is shorter than its diff:
```python
import functools
import math

import jax
import jax.numpy as jnp
from jax import lax
from jax.experimental import pallas as pl
from jax.experimental.pallas import tpu as pltpu
from jax.sharding import Mesh
from jax.sharding import PartitionSpec as P

EPS = 1e-06
THETA = 1000000.0
NEGATIVE = -1e30
F32 = jnp.float32
BF16 = jnp.bfloat16
VMEM_BYTES = 56 * 1024 * 1024
LANES = 128
ROW = ("outer", "core")


def angles_of(places, head_size):
    half_size = head_size // 2
    frequency = jnp.exp(jnp.arange(half_size, dtype=F32) * (-2.0 * math.log(THETA) / head_size))
    angles = places.astype(F32)[:, None] * frequency[None, :]
    cosine, sine = jnp.cos(angles), jnp.sin(angles)
    return jnp.concatenate([cosine, cosine], axis=1), jnp.concatenate([-sine, sine], axis=1)


def token_places(lengths, token_order):
    seq_ends = jnp.cumsum(lengths)
    passed = token_order[:, None] >= seq_ends[None, :]
    seq_of = jnp.sum(passed.astype(jnp.int32), axis=1)
    start_of = jnp.sum(jnp.where(passed, lengths[None, :], 0), axis=1)
    return (seq_of, token_order - start_of)


def dot(a, b):
    return jnp.dot(a, b, preferred_element_type=F32)


def dot_bt(a, b):
    return lax.dot_general(a, b, (((1,), (1,)), ((), ())), preferred_element_type=F32)


def dot_at(a, b):
    return lax.dot_general(a, b, (((0,), (0,)), ((), ())), preferred_element_type=F32)


def two_parts(a):
    high = a.astype(BF16)
    return high, (a - high.astype(F32)).astype(BF16)


ANY = pl.BlockSpec(memory_space=pl.ANY)
SMEM = pl.BlockSpec(memory_space=pltpu.SMEM)


def whole(shape):
    return pl.BlockSpec(shape, lambda *_: (0,) * len(shape))


def params(steps=1):
    return pltpu.CompilerParams(
        dimension_semantics=("arbitrary",) * steps, vmem_limit_bytes=VMEM_BYTES
    )


def cost(flops, moved):
    return pl.CostEstimate(flops=int(flops), bytes_accessed=int(moved), transcendentals=0)


def nbytes(arrays):
    return sum(math.prod(a.shape) * a.dtype.itemsize for a in arrays)


def struct(shape, dtype):
    return jax.ShapeDtypeStruct(shape, dtype)


def weight_copies(at, pairs, fulls, sems, firsts=None):
    copies = []
    for i, ((own, other), full) in enumerate(zip(pairs, fulls)):
        cols, half = own.shape[0], own.shape[1]
        first = firsts[i] if firsts else 0
        for k in range(cols):
            for h, source in enumerate((own, other)):
                copies.append(
                    pltpu.make_async_copy(
                        source.at[at ^ k, :, pl.ds(first, full.shape[1])],
                        full.at[pl.ds((2 * k + h) * half, half)],
                        sems.at[len(copies)],
                    )
                )
    return copies


def load_weights(at, pairs, fulls, sems, firsts=None):
    copies = weight_copies(at, pairs, fulls, sems, firsts)
    for copy in copies:
        copy.start()
    for copy in copies:
        copy.wait()


def full_weight(pair, n=None):
    cols, half, _ = pair[0].shape
    n = n or pair[0].shape[2]
    return pltpu.VMEM((2 * cols * half, n), BF16)


def weight_sems(*pairs):
    return pltpu.SemaphoreType.DMA((sum(2 * pair[0].shape[0] for pair in pairs),))


def rms_scale(pieces, width):
    total = sum(jnp.sum(piece * piece, axis=1, keepdims=True) for piece in pieces)
    return lax.rsqrt(total / width + EPS)


def project(at, pieces, gain, pair, query_gain, key_gain, cosine, sine, heads, kv_heads):
    parts = len(pieces)
    tokens, part = pieces[0].shape
    width = parts * part
    n = pair[0].shape[2]
    size = query_gain.shape[1]

    def kernel(at_ref, *refs):
        ins, refs = refs[:parts], refs[parts:]
        gain_ref, own, other, qg, kg, cos_ref, sin_ref, normed, pre, ready, full, sems = refs
        copies = weight_copies(at_ref[0], [(own, other)], [full], sems)
        for copy in copies:
            copy.start()
        values = [ref[...].astype(F32) for ref in ins]
        scale = rms_scale(values, width)
        for k, value in enumerate(values):
            cut = slice(k * part, (k + 1) * part)
            normed[:, cut] = (value * scale * gain_ref[:, cut]).astype(BF16)
        for copy in copies:
            copy.wait()
        pre[...] = dot(normed[...], full[...])
        cosine, sine = cos_ref[...], sin_ref[...]
        for i in range(n // size):
            cut = slice(i * size, (i + 1) * size)
            head = pre[:, cut]
            if i < heads + kv_heads:
                head_gain = qg[...] if i < heads else kg[...]
                head = (
                    head
                    * lax.rsqrt(jnp.mean(head * head, axis=1, keepdims=True) + EPS)
                    * head_gain
                )
                head = head * cosine + pltpu.roll(head, size // 2, 1) * sine
            ready[:, cut] = head.astype(BF16)

    outs = (
        struct((tokens, width), BF16),
        struct((tokens, n), F32),
        struct((tokens, n), BF16),
    )
    ins = (*pieces, gain, *pair, query_gain, key_gain, cosine, sine)
    return pl.pallas_call(
        kernel,
        out_shape=outs,
        in_specs=[SMEM]
        + [whole(a.shape) for a in pieces]
        + [whole(gain.shape), ANY, ANY]
        + [whole(a.shape) for a in (query_gain, key_gain, cosine, sine)],
        out_specs=[whole(o.shape) for o in outs],
        scratch_shapes=[full_weight(pair), weight_sems(pair)],
        grid=(1,),
        compiler_params=params(),
        cost_estimate=cost(2 * tokens * width * n, nbytes(ins + outs)),
        name="project",
    )(at, *ins)


def attend(ready, own, other, bias, heads, kv_heads, size):
    micro, keys, tok = bias.shape
    group = heads // kv_heads
    outer = own.shape[0]
    scale = 1.0 / math.sqrt(size)

    def kernel(q_ref, k0, k1, v0, v1, bias_ref, out_ref, lse_ref):
        key = jnp.concatenate([r[...].reshape(outer * tok, size) for r in (k0, k1)], axis=0)
        value = jnp.concatenate([r[...].reshape(outer * tok, size) for r in (v0, v1)], axis=0)
        scores = dot_bt(key, q_ref[...]) * scale + bias_ref[0]
        peak = jnp.max(scores, axis=0, keepdims=True)
        powers = jnp.exp(scores - peak)
        total = jnp.sum(powers, axis=0, keepdims=True)
        probs = (powers * (1.0 / total)).astype(BF16)
        out_ref[...] = dot_at(probs, value).astype(BF16)
        lse_ref[0, 0] = peak + jnp.log(total)

    def kv_spec(first):
        return pl.BlockSpec((outer, tok, size), lambda m, h: (0, m, first + h // group))

    outs = (struct((micro * tok, heads * size), BF16), struct((micro, heads, 1, tok), F32))
    return pl.pallas_call(
        kernel,
        out_shape=outs,
        grid=(micro, heads),
        in_specs=[
            pl.BlockSpec((tok, size), lambda m, h: (m, h)),
            kv_spec(0),
            kv_spec(0),
            kv_spec(kv_heads),
            kv_spec(kv_heads),
            pl.BlockSpec((1, keys, tok), lambda m, h: (m, 0, 0)),
        ],
        out_specs=[
            pl.BlockSpec((tok, size), lambda m, h: (m, h)),
            pl.BlockSpec((1, 1, 1, tok), lambda m, h: (m, h, 0, 0)),
        ],
        compiler_params=params(2),
        cost_estimate=cost(4 * micro * heads * keys * tok * size, nbytes((ready, own, other, bias))),
        name="attend",
    )(ready, own, other, own, other, bias)


def attend_back(ready, own, other, bias, lse, grad, heads, kv_heads, size):
    micro, keys, tok = bias.shape
    group = heads // kv_heads
    outer = own.shape[0]
    scale = 1.0 / math.sqrt(size)
    mid = keys // 2

    def kernel(q_ref, k0, k1, v0, v1, bias_ref, lse_ref, g_ref, gq, gk0, gk1, gv0, gv1):
        first = pl.program_id(1) % group == 0
        key = jnp.concatenate([r[...].reshape(outer * tok, size) for r in (k0, k1)], axis=0)
        value = jnp.concatenate([r[...].reshape(outer * tok, size) for r in (v0, v1)], axis=0)
        query, out_grad = q_ref[...], g_ref[...]
        scores = dot_bt(key, query) * scale + bias_ref[0]
        probs = jnp.exp(scores - lse_ref[0, 0])
        back = dot_bt(value, out_grad)
        centre = jnp.sum(probs * back, axis=0, keepdims=True)
        slope = (probs * (back - centre)).astype(BF16)
        gq[...] = dot_at(slope, key) * scale
        key_part = dot(slope, query) * scale
        value_part = dot(probs.astype(BF16), out_grad)
        for ref, part in (
            (gk0, key_part[:mid]),
            (gk1, key_part[mid:]),
            (gv0, value_part[:mid]),
            (gv1, value_part[mid:]),
        ):
            part = part.reshape(outer, tok, size)
            before = jnp.where(first, 0.0, ref[...])
            ref[...] = before + part

    def kv_spec(start):
        return pl.BlockSpec((outer, tok, size), lambda m, h: (0, m, start + h // group))

    head_spec = pl.BlockSpec((tok, size), lambda m, h: (m, h))
    kv_shape = struct((outer, micro * tok, kv_heads * size), F32)
    outs = (struct((micro * tok, heads * size), F32), kv_shape, kv_shape, kv_shape, kv_shape)
    return pl.pallas_call(
        kernel,
        out_shape=outs,
        grid=(micro, heads),
        in_specs=[
            head_spec,
            kv_spec(0),
            kv_spec(0),
            kv_spec(kv_heads),
            kv_spec(kv_heads),
            pl.BlockSpec((1, keys, tok), lambda m, h: (m, 0, 0)),
            pl.BlockSpec((1, 1, 1, tok), lambda m, h: (m, h, 0, 0)),
            head_spec,
        ],
        out_specs=[head_spec] + [kv_spec(0)] * 4,
        compiler_params=params(2),
        cost_estimate=cost(
            10 * micro * heads * keys * tok * size, nbytes((ready, own, other, bias) + outs)
        ),
        name="attend_back",
    )(ready, own, other, own, other, bias, lse, grad)


def expand(at, a, pair, part):
    tokens, n = a.shape
    cols = pair[0].shape[0]
    outs = [struct((tokens, part), F32 if k == 0 else BF16) for k in range(cols)]

    def kernel(at_ref, a_ref, own, other, *refs):
        outs, (full, sems) = refs[:cols], refs[cols:]
        load_weights(at_ref[0], [(own, other)], [full], sems)
        for k, out in enumerate(outs):
            out[...] = dot_bt(a_ref[...], full[k * part : (k + 1) * part]).astype(out.dtype)

    return pl.pallas_call(
        kernel,
        out_shape=outs,
        in_specs=[SMEM, whole(a.shape), ANY, ANY],
        out_specs=[whole(o.shape) for o in outs],
        scratch_shapes=[full_weight(pair, n), weight_sems(pair)],
        grid=(1,),
        compiler_params=params(),
        cost_estimate=cost(2 * tokens * n * part * cols, nbytes((a, *pair))),
        name="expand",
    )(at, a, *pair)


def contract(at, pieces, pair, n):
    parts = len(pieces)
    tokens, part = pieces[0].shape
    outs = struct((tokens, n), BF16)

    def kernel(at_ref, *refs):
        ins, (own, other, out, full, sems) = refs[:parts], refs[parts:]
        load_weights(at_ref[0], [(own, other)], [full], sems)
        joined = jnp.concatenate([ref[...] for ref in ins], axis=1)
        out[...] = dot(joined, full[...]).astype(BF16)

    return pl.pallas_call(
        kernel,
        out_shape=outs,
        in_specs=[SMEM] + [whole(a.shape) for a in pieces] + [ANY, ANY],
        out_specs=whole(outs.shape),
        scratch_shapes=[full_weight(pair, n), weight_sems(pair)],
        grid=(1,),
        compiler_params=params(),
        cost_estimate=cost(2 * tokens * n * part * parts, nbytes((*pieces, *pair))),
        name="contract",
    )(at, *pieces, *pair)


def second_norm(pieces, gain):
    parts = len(pieces)
    tokens, part = pieces[0].shape
    width = parts * part
    out = struct((tokens, width), BF16)

    def kernel(*refs):
        ins, (gain_ref, out_ref) = refs[:parts], refs[parts:]
        values = [ref[...].astype(F32) for ref in ins]
        scale = rms_scale(values, width)
        for k, value in enumerate(values):
            cut = slice(k * part, (k + 1) * part)
            out_ref[:, cut] = (value * scale * gain_ref[:, cut]).astype(BF16)

    return pl.pallas_call(
        kernel,
        out_shape=out,
        in_specs=[whole(a.shape) for a in pieces] + [whole(gain.shape)],
        out_specs=whole(out.shape),
        grid=(1,),
        compiler_params=params(),
        cost_estimate=cost(tokens * width * 4, nbytes((*pieces, out))),
        name="second_norm",
    )(*pieces, gain)


def run_experts(at, first, tokens_in, grads, spread, high, low, router, router_at, before):
    count = len(tokens_in)
    tokens, width = tokens_in[0].shape
    hidden = low[0].shape[2]
    parts = low[0].shape[0]
    part = width // parts

    def kernel(at_ref, g_ref, c_ref, s_ref, *refs):
        x_refs, refs = refs[:count], refs[count:]
        pairs, refs = [refs[:2], refs[2:4], refs[4:6]], refs[6 + len(before) :]
        weighted, d_high, logit, dx, lo, full_high, full_low, r_ref, x_now, sems, x_sems = refs
        step = pl.program_id(0)
        fulls = [full_high, full_low, r_ref]
        copies = weight_copies(at_ref[0], pairs, fulls, sems, (0, 0, router_at))
        arrivals = [
            pltpu.make_async_copy(ref, x_now.at[i % 2], x_sems.at[i % 2])
            for i, ref in enumerate(x_refs)
        ]

        @pl.when(step == 0)
        def _():
            arrivals[0].start()
            for k in range(parts):
                for i in range(3):
                    for h in range(2):
                        copies[2 * parts * i + 2 * k + h].start()

        for i in range(count):

            @pl.when(step == i)
            def _(i=i):
                arrivals[i].wait()
                if i + 1 < count:
                    arrivals[i + 1].start()

        slot = lax.rem(step, 2)
        pre, back, logits = 0.0, 0.0, 0.0
        for k in range(parts):

            @pl.when(step == 0)
            def _(k=k):
                for i in range(3):
                    for h in range(2):
                        copies[2 * parts * i + 2 * k + h].wait()

            cut = slice(k * part, (k + 1) * part)
            x = x_now[slot, :, cut]
            pre = pre + dot(x, full_high[cut])
            back = back + dot(g_ref[0, :, cut], full_low[cut])
            logits = logits + dot(x, r_ref[cut])
        logits = jnp.where(c_ref[0] > 0, logits, NEGATIVE)
        peak = jnp.max(logits, axis=1, keepdims=True)
        powers = jnp.exp(logits - peak)
        gate_probs = powers / jnp.sum(powers, axis=1, keepdims=True)
        spread = s_ref[...]
        one, two = two_parts(gate_probs)
        probs_wide = dot(one, spread) + dot(two, spread)
        gate_pre, up_pre = pre[:, :hidden], pre[:, hidden:]
        sigmoid = 0.5 + 0.5 * jnp.tanh(0.5 * gate_pre)
        swish = gate_pre * sigmoid
        active = swish * up_pre
        weighted_now = (probs_wide * active).astype(BF16)
        weighted[...] = weighted_now
        gate_grad = dot_bt((active * back).astype(BF16), spread)
        logit_low = (
            gate_probs * (gate_grad - jnp.sum(gate_probs * gate_grad, axis=1, keepdims=True))
        ).astype(BF16)
        logit[...] = logit_low
        back = probs_wide * back
        d_high[:, :hidden] = (back * up_pre * (sigmoid + swish * (1.0 - sigmoid))).astype(BF16)
        d_high[:, hidden:] = (back * swish).astype(BF16)
        dx[0] = (dot_bt(d_high[...], full_high[...]) + dot_bt(logit_low, r_ref[...])).astype(BF16)
        lo[0] = dot_bt(weighted_now, full_low[...]).astype(BF16)

    def rows(n):
        return pl.BlockSpec((tokens, n), lambda i, at_ref: (i, 0))

    def owner(n, lane):
        return pl.BlockSpec(
            (1, tokens, n), lambda i, at_ref: (at_ref[1] ^ (i + first), 0, lane)
        )

    outs = [struct((count * tokens, n), BF16) for n in (hidden, 2 * hidden, LANES)]
    outs += [struct((grads.shape[0], tokens, width), BF16)] * 2
    ins = (grads, grads, spread, *tokens_in, *high, *low, *router, *before)
    return pl.pallas_call(
        kernel,
        out_shape=outs,
        grid_spec=pltpu.PrefetchScalarGridSpec(
            num_scalar_prefetch=1,
            grid=(count,),
            in_specs=[owner(width, 0), owner(LANES, width // LANES), whole(spread.shape)]
            + [ANY] * (count + 6 + len(before)),
            out_specs=[rows(hidden), rows(2 * hidden), rows(LANES)] + [owner(width, 0)] * 2,
            scratch_shapes=[
                full_weight(high),
                full_weight(low),
                full_weight(router, LANES),
                pltpu.VMEM((2, tokens, width), BF16),
                weight_sems(high, low, router),
                pltpu.SemaphoreType.DMA((2,)),
            ],
        ),
        input_output_aliases={len(ins) - 1: 3, len(ins): 4} if before else {},
        compiler_params=params(),
        cost_estimate=cost(12 * count * tokens * width * hidden, nbytes([*high, *low, *outs])),
        name="run_experts",
    )(at, *ins)


def weight_grads(at, half_at, lefts, rights, cols, add=None):
    flat = [r for group in rights for stack in group for r in stack]
    lefts = [[a] * a.shape[0] if not isinstance(a, list) else a for a in lefts]
    left_flat = [a for group in lefts for a in group]
    stacks = [stack for group in rights for stack in group]
    tokens = sum(r.shape[0] for r in stacks[0])
    by_part = [group[0].shape[0] == tokens and len(group) > 1 for group in lefts]
    width = lefts[0][0].shape[1] * (cols if by_part[0] else 1)
    half = width // cols // 2
    n = sum(stack[0].shape[1] for stack in stacks)
    apart = add is None
    outs = [struct((half, n), BF16)] * cols if apart else struct((cols, half, n), BF16)
    joins = [stack for stack in stacks if len(stack) > 1]
    extra = [] if apart else list(add)

    def kernel(at_ref, *refs):
        left_refs, refs = refs[: len(left_flat)], refs[len(left_flat) :]
        right_refs, refs = refs[: len(flat)], refs[len(flat) :]
        added, refs = refs[: len(extra)], refs[len(extra) :]
        out_refs, joined = refs[: cols if apart else 1], refs[cols if apart else 1 :]
        step = pl.program_id(0)
        stacked = []
        for stack in stacks:
            stack_refs, right_refs = right_refs[: len(stack)], right_refs[len(stack) :]
            if len(stack) == 1:
                stacked.append(stack_refs[0])
            else:
                full, joined = joined[0], joined[1:]
                stacked.append(full)

                @pl.when(step == 0)
                def _(full=full, stack_refs=stack_refs):
                    row = 0
                    for ref in stack_refs:
                        full[row : row + ref.shape[0]] = ref[...]
                        row += ref.shape[0]

        def write(k):
            column, group_lefts, rest = 0, left_refs, stacked
            for group, is_part, group_rights in zip(lefts, by_part, rights):
                group_refs, group_lefts = group_lefts[: len(group)], group_lefts[len(group) :]
                now, rest = rest[: len(group_rights)], rest[len(group_rights) :]
                if is_part:
                    left = group_refs[k][...]
                else:
                    blocks = [ref[...] if len(ref.shape) == 2 else ref[0] for ref in group_refs]
                    left = jnp.concatenate(blocks, axis=0)
                left = left.T
                for right in now:
                    cut = slice(column, column + right.shape[1])
                    value = dot(left, right[...])
                    if apart:
                        out_refs[k][:, cut] = value.astype(BF16)
                    else:
                        out_refs[0][0, :, cut] = (value + added[k][:, cut].astype(F32)).astype(BF16)
                    column = cut.stop

        for k in range(cols):
            pl.when(step == k)(functools.partial(write, k))

    def left_spec(a, i, is_part):
        if a.ndim == 3:
            return pl.BlockSpec(
                (1, a.shape[1], half), lambda k, at_ref: (at_ref[1] ^ i, 0, 2 * k + half_at)
            )
        shape = (a.shape[0], half)
        if is_part:
            return pl.BlockSpec(shape, lambda k, at_ref: (0, half_at))
        return pl.BlockSpec(shape, lambda k, at_ref: (0, 2 * k + half_at))

    ins = (*left_flat, *flat, *extra)
    return pl.pallas_call(
        kernel,
        out_shape=outs,
        grid_spec=pltpu.PrefetchScalarGridSpec(
            num_scalar_prefetch=1,
            grid=(cols,),
            in_specs=[
                left_spec(a, i, p) for group, p in zip(lefts, by_part) for i, a in enumerate(group)
            ]
            + [whole(a.shape) for a in flat + extra],
            out_specs=[whole((half, n))] * cols
            if apart
            else pl.BlockSpec((1, half, n), lambda k, at_ref: (at_ref[0] ^ k, 0, 0)),
            scratch_shapes=[pltpu.VMEM((tokens, stack[0].shape[1]), BF16) for stack in joins],
        ),
        compiler_params=params(),
        cost_estimate=cost(2 * tokens * cols * half * n, nbytes(ins)),
        name="weight_grads",
    )(at, *ins)


def by_owner(weights, outer):
    unit, hidden = weights[0].shape[0], weights[0].shape[1] // outer
    if hidden % LANES:
        return jnp.concatenate(
            [w.reshape(unit, outer, hidden).transpose(1, 0, 2) for w in weights], axis=2
        )

    def kernel(*refs):
        for i, ref in enumerate(refs[:-1]):
            refs[-1][0, :, i * hidden : (i + 1) * hidden] = ref[...]

    out = struct((outer, unit, hidden * len(weights)), BF16)
    return pl.pallas_call(
        kernel,
        out_shape=out,
        grid=(outer,),
        in_specs=[pl.BlockSpec((unit, hidden), lambda i: (0, i)) for _ in weights],
        out_specs=pl.BlockSpec((1,) + out.shape[1:], lambda i: (i, 0, 0)),
        compiler_params=params(),
        cost_estimate=cost(1, 1),
        name="by_owner",
    )(*weights)


def by_columns(grads, hidden):
    outer, unit, n = grads.shape
    starts = (0, hidden, 2 * hidden + LANES)
    if hidden % LANES:
        return [
            grads[:, :, start : start + hidden]
            .transpose(1, 0, 2)
            .reshape(unit, outer * hidden)
            .astype(F32)
            for start in starts
        ] + [jnp.sum(grads[:, :, 2 * hidden : 2 * hidden + LANES].astype(F32), axis=0)]

    def kernel(ref, *outs):
        for start, out in zip(starts, outs):
            out[...] = ref[0, :, start : start + hidden].astype(F32)
        rest = ref[0, :, 2 * hidden : 2 * hidden + LANES].astype(F32)
        before = jnp.where(pl.program_id(0) == 0, 0.0, outs[-1][...])
        outs[-1][...] = before + rest

    outs = [struct((unit, outer * hidden), F32) for _ in starts] + [struct((unit, LANES), F32)]
    return pl.pallas_call(
        kernel,
        out_shape=outs,
        grid=(outer,),
        in_specs=[pl.BlockSpec((1, unit, n), lambda i: (i, 0, 0))],
        out_specs=[pl.BlockSpec((unit, hidden), lambda i: (0, i)) for _ in starts]
        + [whole((unit, LANES))],
        compiler_params=params(),
        cost_estimate=cost(0, nbytes([grads, *outs])),
        name="by_columns",
    )(grads)


def norm_back(values, pieces, scale, gain, gain_grad, outs, width):
    part = pieces[0].shape[1]
    cuts = [slice(k * part, (k + 1) * part) for k in range(len(pieces))]
    inner = 0.0
    for value, piece, cut in zip(values, pieces, cuts):
        gain_grad[:, cut] = jnp.sum(value * (piece * scale), axis=0, keepdims=True)
        inner = inner + jnp.sum(value * gain[:, cut] * piece, axis=1, keepdims=True)
    inner = inner * (scale * scale * scale / width)
    for value, piece, cut, out in zip(values, pieces, cuts, outs):
        out[...] = (value * gain[:, cut] * scale - piece * inner).astype(out.dtype)


def second_norm_back(received, pieces, gain):
    parts = len(pieces)
    blocks, tokens, width = received.shape
    part = width // parts
    outs = [struct((tokens, part), F32 if k == 0 else BF16) for k in range(parts)]
    outs.append(struct((1, width), F32))

    def kernel(*refs):
        got, *refs = refs
        ins, (gain_ref, *outs, gain_grad) = refs[:parts], refs[parts:]
        values = []
        for k in range(parts):
            cut = slice(k * part, (k + 1) * part)
            values.append(sum(got[i, :, cut].astype(F32) for i in range(blocks)))
        pieces = [ref[...].astype(F32) for ref in ins]
        scale = rms_scale(pieces, width)
        norm_back(values, pieces, scale, gain_ref, gain_grad, outs, width)

    ins = (received, *pieces, gain)
    return pl.pallas_call(
        kernel,
        out_shape=outs,
        in_specs=[whole(a.shape) for a in ins],
        out_specs=[whole(o.shape) for o in outs],
        grid=(1,),
        compiler_params=params(),
        cost_estimate=cost(tokens * width * 20, nbytes(ins)),
        name="second_norm_back",
    )(*ins)


def project_back(
    at, grad_q, grad_kv, pre, pieces, gain, pair, query_gain, key_gain, cosine, sine, heads, kv_heads
):
    parts = len(pieces)
    tokens, part = pieces[0].shape
    width = parts * part
    n = pair[0].shape[2]
    size = query_gain.shape[1]
    blocks = len(grad_kv)
    outs = [struct((tokens, part), F32 if k == 0 else BF16) for k in range(parts)]
    outs += [struct((1, width), F32), struct((tokens, n), BF16), struct((2, size), F32)]

    def kernel(at_ref, gq, pre_ref, *refs):
        gkv, refs = refs[:blocks], refs[blocks:]
        ins, refs = refs[:parts], refs[parts:]
        gain_ref, own, other, qg, kg, cos_ref, sin_ref, *refs = refs
        outs, (gain_grad, d_wide, head_gain, full, sems) = refs[:parts], refs[parts:]
        copies = weight_copies(at_ref[0], [(own, other)], [full], sems)
        for copy in copies:
            copy.start()
        cosine, sine = cos_ref[...], sin_ref[...]
        totals = [jnp.zeros((1, size), F32), jnp.zeros((1, size), F32)]
        for i in range(n // size):
            cut = slice(i * size, (i + 1) * size)
            if i < heads:
                grad = gq[:, cut]
            else:
                kv_cut = slice((i - heads) * size, (i - heads + 1) * size)
                grad = sum(ref[:, kv_cut].astype(F32) for ref in gkv)
            if i < heads + kv_heads:
                which = 0 if i < heads else 1
                gain_row = (qg, kg)[which][...]
                grad = grad * cosine + pltpu.roll(grad * sine, size // 2, 1)
                head = pre_ref[:, cut]
                scale = lax.rsqrt(jnp.mean(head * head, axis=1, keepdims=True) + EPS)
                unit = head * scale
                totals[which] = totals[which] + jnp.sum(grad * unit, axis=0, keepdims=True)
                grad = grad * gain_row
                grad = scale * (grad - unit * jnp.mean(grad * unit, axis=1, keepdims=True))
            d_wide[:, cut] = grad.astype(BF16)
        head_gain[0:1] = totals[0]
        head_gain[1:2] = totals[1]
        for copy in copies:
            copy.wait()
        values = [
            dot_bt(d_wide[...], full[k * part : (k + 1) * part]) for k in range(parts)
        ]
        pieces = [ref[...].astype(F32) for ref in ins]
        scale = rms_scale(pieces, width)
        norm_back(values, pieces, scale, gain_ref, gain_grad, outs, width)

    ins = (grad_q, pre, *grad_kv, *pieces, gain, *pair, query_gain, key_gain, cosine, sine)
    return pl.pallas_call(
        kernel,
        out_shape=outs,
        in_specs=[SMEM]
        + [whole(a.shape) for a in (grad_q, pre, *grad_kv, *pieces, gain)]
        + [ANY, ANY]
        + [whole(a.shape) for a in (query_gain, key_gain, cosine, sine)],
        out_specs=[whole(o.shape) for o in outs],
        scratch_shapes=[full_weight(pair), weight_sems(pair)],
        grid=(1,),
        compiler_params=params(),
        cost_estimate=cost(2 * tokens * width * n, nbytes(ins)),
        name="project_back",
    )(at, *ins)


def per_device(
    layer_in,
    out_grad,
    lengths,
    token_order,
    choices,
    norm_gain,
    w_query,
    w_key,
    w_value,
    query_gain,
    key_gain,
    w_out,
    ffn_gain,
    w_router,
    w_gate,
    w_up,
    w_down,
):
    micro, tok, part = layer_in.shape
    outer, cols = lax.axis_size("outer"), lax.axis_size("col")
    rows = 2 * outer
    tokens = micro * tok
    width = part * cols
    outer_at, core_at, col_at = (lax.axis_index(name) for name in ("outer", "core", "col"))
    row_at = outer_at * 2 + core_at
    at = jnp.stack([col_at, outer_at]).astype(jnp.int32)
    low = outer // cols
    unit = width // rows
    half = part // 2
    size = query_gain.shape[0]
    heads = w_query.shape[1] // size
    kv_heads = w_key.shape[1] // size
    experts = w_router.shape[1]
    hidden = w_gate.shape[1] // outer
    repeats = hidden // experts

    def core_swap(a):
        return lax.ppermute(a, "core", [(0, 1), (1, 0)])

    def col_swap(a, mask):
        return lax.ppermute(a, "col", [(i, i ^ mask) for i in range(cols)])

    def exchange(a):
        return lax.all_to_all(a, "outer", 0, 0, tiled=True)

    def after(a, b):
        return lax.optimization_barrier((a, b))[0]

    def spread_out(a):
        return exchange(jnp.broadcast_to(a[None], (outer,) + a.shape))

    def to_halves(a):
        blocks = a.reshape(a.shape[:-1] + (low, 2, unit))
        first = blocks[..., 0, :].reshape(a.shape[:-1] + (half,))
        second = blocks[..., 1, :].reshape(a.shape[:-1] + (half,))
        even = core_at == 0
        return jnp.concatenate(
            [jnp.where(even, first, second), jnp.where(even, second, first)], axis=-1
        )

    def from_halves(a):
        even = core_at == 0
        first = jnp.where(even, a[..., :half], a[..., half:]).reshape(a.shape[:-1] + (low, unit))
        second = jnp.where(even, a[..., half:], a[..., :half]).reshape(a.shape[:-1] + (low, unit))
        return jnp.stack([first, second], axis=-2).reshape(a.shape)

    def relative(a):
        return jnp.stack(
            [lax.dynamic_index_in_dim(a, col_at ^ k, 0, keepdims=False) for k in range(cols)]
        )

    def order_rows(a):
        blocks = relative(a.reshape((cols, low, 2, unit) + a.shape[1:]))
        blocks = jnp.where(core_at == 0, blocks, blocks[:, :, ::-1])
        return jnp.moveaxis(blocks, 2, 1).reshape(a.shape)

    def unorder_rows(a):
        blocks = jnp.moveaxis(a.reshape((cols, 2, low, unit) + a.shape[1:]), 1, 2)
        blocks = jnp.where(core_at == 0, blocks, blocks[:, :, ::-1])
        return relative(blocks).reshape(a.shape)

    def col_gather(a):
        return [a] + [col_swap(a, k) for k in range(1, cols)]

    def col_total(pieces):
        total = pieces[0]
        for k in range(1, cols):
            total = total + col_swap(pieces[k], k).astype(F32)
        return total

    def both_cores(a):
        own = a.reshape(cols, half, a.shape[-1])
        return own, core_swap(own)

    def swap(a, mask):
        return lax.ppermute(a, "outer", [(i, i ^ mask) for i in range(outer)])

    def gather(a):
        return [a] + [swap(a, j) for j in range(1, outer)]

    def scatter(blocks):
        return [blocks[0]] + [swap(blocks[j], j) for j in range(1, outer)]

    own_in = to_halves(layer_in).reshape(tokens, part)
    own_grad = to_halves(out_grad).reshape(tokens, part)
    w_in = spread_out(jnp.concatenate([w_query, w_key, w_value], axis=1))
    full_in = col_gather(own_in)
    chosen = jnp.any(
        choices.reshape(tokens, -1)[..., None] == jnp.arange(LANES, dtype=jnp.int32), axis=1
    ).astype(BF16)
    own_grads = col_gather(own_grad)
    back_now = jnp.concatenate([w_out, jnp.pad(w_router, ((0, 0), (0, LANES - experts)))], axis=1)
    back_now = jnp.broadcast_to(back_now[None], (outer,) + back_now.shape)
    low_now, high_now = by_owner([w_down], outer), by_owner([w_gate, w_up], outer)
    grads = jnp.concatenate(own_grads + [chosen], axis=1)
    grads = jnp.broadcast_to(grads[None], (outer,) + grads.shape)
    gain_one = order_rows(norm_gain)[None, :]
    gain_two = order_rows(ffn_gain)[None, :]
    q_gain, k_gain = query_gain[None, :], key_gain[None, :]
    spread = (
        jnp.arange(hidden)[None, :] % experts == jnp.arange(LANES)[:, None]
    ).astype(BF16)

    biases, cosines, sines = [], [], []
    for b in range(micro):
        dealt = token_order[b]
        seq_of, places = token_places(lengths[b], dealt)
        own_order = lax.dynamic_slice_in_dim(dealt, row_at * tok, tok)
        own_seq = lax.dynamic_slice_in_dim(seq_of, row_at * tok, tok)
        own_places = lax.dynamic_slice_in_dim(places, row_at * tok, tok)

        def by_core(a):
            blocks = a.reshape(outer, 2, tok)
            blocks = jnp.where(core_at == 0, blocks, blocks[:, ::-1])
            blocks = jnp.stack(
                [
                    lax.dynamic_index_in_dim(blocks, outer_at ^ j, 0, keepdims=False)
                    for j in range(outer)
                ]
            )
            return blocks.transpose(1, 0, 2).reshape(-1)

        allowed = (own_seq[None, :] == by_core(seq_of)[:, None]) & (
            by_core(dealt)[:, None] <= own_order[None, :]
        )
        biases.append(jnp.where(allowed, 0.0, NEGATIVE))
        cosine, sine = angles_of(own_places, size)
        cosines.append(cosine)
        sines.append(sine)
    bias = jnp.stack(biases)
    cosine, sine = jnp.concatenate(cosines), jnp.concatenate(sines)

    w_in, *_ = lax.optimization_barrier(
        (w_in, full_in, grads, back_now, low_now, high_now, bias, cosine, sine, gain_one, gain_two, spread)
    )
    w_back = exchange(after(back_now, w_in))
    w_in = both_cores(w_in)
    normed_one, pre, ready = project(
        at, full_in, gain_one, w_in, q_gain, k_gain, cosine, sine, heads, kv_heads
    )
    kv_own = jnp.stack(gather(ready[:, heads * size :]))
    kv_other = core_swap(kv_own)
    kv_other, w_back = lax.optimization_barrier((kv_other, w_back))
    w_low = exchange(after(low_now, w_back))
    w_back = both_cores(w_back)
    attended, lse = attend(ready, kv_own, kv_other, bias, heads, kv_heads, size)
    attended, w_low = lax.optimization_barrier((attended, w_low))
    w_high = exchange(after(high_now, w_low))
    attn_parts = expand(at, attended, w_back, part)
    residual = own_in.astype(F32) + col_total(attn_parts)
    residual, w_high = lax.optimization_barrier((residual, w_high))
    grads = exchange(after(grads, w_high))
    w_low = both_cores(w_low)
    full_res = col_gather(residual.astype(BF16))

    full_res, grads = lax.optimization_barrier((full_res, grads))
    normed_two = second_norm(full_res, gain_two)
    expert_in = gather(normed_two)
    w_high = both_cores(w_high)
    weights = (spread, w_high, w_low, w_back, w_out.shape[1])
    weighted_0, d_high_0, logit_0, *before = run_experts(
        at, 0, expert_in[:1], grads, *weights, ()
    )
    weighted, d_high, logit_low, dx, lo = run_experts(
        at, 1, expert_in[1:], grads, *weights, before
    )
    weighted, d_high, logit_low = [weighted_0, weighted], [d_high_0, d_high], [logit_0, logit_low]
    dx = exchange(dx)

    def both_halves(lefts, rights):
        other = weight_grads(at, 1, lefts, rights, cols)
        own = weight_grads(at, 0, lefts, rights, cols, [core_swap(a) for a in other])
        return own.reshape(outer, unit, own.shape[-1])

    expert_grads = both_halves([expert_in, grads], [[d_high, logit_low], [weighted]])
    dx, expert_grads = lax.optimization_barrier((dx, expert_grads))
    expert_grads = exchange(expert_grads)
    *spread_two, gain_grad_two = second_norm_back(dx, full_res, gain_two)
    grad_residual = own_grad.astype(F32) + col_total(spread_two)
    grad_feats = col_gather(grad_residual.astype(BF16))

    grad_feats, expert_grads = lax.optimization_barrier((grad_feats, expert_grads))
    lo = exchange(after(lo, expert_grads))
    back_attended = contract(at, grad_feats, w_back, heads * size)
    grad_q, *kv_grads = attend_back(
        ready, kv_own, kv_other, bias, lse, back_attended, heads, kv_heads, size
    )
    kv_mine = jnp.concatenate([kv_grads[0], kv_grads[2]], axis=2)
    kv_theirs = jnp.concatenate([kv_grads[1], kv_grads[3]], axis=2).astype(BF16)
    kv_mine = (kv_mine + core_swap(kv_theirs).astype(F32)).astype(BF16)
    grad_kv = scatter([kv_mine[j] for j in range(outer)])
    out_grads = both_halves([grad_feats], [[[attended]]])
    grad_kv, out_grads, lo = lax.optimization_barrier((grad_kv, out_grads, lo))
    out_grads = exchange(out_grads)
    *spread_one, gain_grad_one, d_wide, head_gains = project_back(
        at, grad_q, grad_kv, pre, full_in, gain_one, w_in, q_gain, k_gain, cosine, sine, heads, kv_heads
    )
    sums = jnp.concatenate(
        [unorder_rows(gain_grad_one[0]), unorder_rows(gain_grad_two[0]), head_gains.reshape(-1)]
    ).reshape(-1, LANES)
    sums = sums + sum(col_swap(sums, k) for k in range(1, cols))
    sums = sums + core_swap(sums)
    wide_grads = both_halves([[normed_one]], [[[d_wide]]])
    out_grads, wide_grads, sums = lax.optimization_barrier((out_grads, wide_grads, sums))
    wide_grads = exchange(wide_grads)
    sums = sum(gather(sums)).reshape(-1)
    expert_grads, lo = lax.optimization_barrier((expert_grads, lo, out_grads))[:2]
    layer_sum = jnp.sum(lo.astype(F32), axis=0)
    layer_out = residual + col_total(
        [
            layer_sum[:, k * part : (k + 1) * part].astype(F32 if k == 0 else BF16)
            for k in range(cols)
        ]
    )
    input_grad = grad_residual + col_total(spread_one)
    grad_gate_w, grad_up_w, grad_down_w, router_part = by_columns(expert_grads, hidden)
    grad_router = router_part
    for k in range(1, cols):
        grad_router = grad_router + col_swap(router_part, k)
    grad_out_w = jnp.sum(out_grads.astype(F32), axis=0)
    wide_grads, input_grad, layer_out, grad_out_w, sums, grad_router, grad_gate_w = (
        lax.optimization_barrier(
            (wide_grads, input_grad, layer_out, grad_out_w, sums, grad_router, grad_gate_w)
        )
    )
    grad_wide = jnp.sum(wide_grads.astype(F32), axis=0)
    query_cols, key_cols = w_query.shape[1], w_key.shape[1]
    return (
        from_halves(layer_out.astype(BF16)).reshape(micro, tok, part),
        from_halves(input_grad.astype(BF16)).reshape(micro, tok, part),
        sums[:width],
        grad_wide[:, :query_cols],
        grad_wide[:, query_cols : query_cols + key_cols],
        grad_wide[:, query_cols + key_cols :],
        sums[2 * width : 2 * width + size],
        sums[2 * width + size :],
        grad_out_w,
        sums[width : 2 * width],
        grad_router[:, :experts],
        grad_gate_w,
        grad_up_w,
        grad_down_w,
    )


def solution(mesh):
    rows, cols = mesh.devices.shape
    split = Mesh(mesh.devices.reshape(rows // 2, 2, cols), ("outer", "core", "col"))
    tokens_placed = P(None, ROW, "col")
    weight_placed = P(ROW, "col")
    return jax.shard_map(
        per_device,
        mesh=split,
        in_specs=(
            tokens_placed,
            tokens_placed,
            P(),
            P(),
            P(None, ROW, None),
            P(),
            weight_placed,
            weight_placed,
            weight_placed,
            P(),
            P(),
            weight_placed,
            P(),
            P(ROW, None),
            weight_placed,
            weight_placed,
            weight_placed,
        ),
        out_specs=(
            tokens_placed,
            tokens_placed,
            P(),
            weight_placed,
            weight_placed,
            weight_placed,
            P(),
            P(),
            weight_placed,
            P(),
            P(ROW, None),
            weight_placed,
            weight_placed,
            weight_placed,
        ),
        check_vma=False,
    )
```

time: 2290 us -> 592 us (0.26)
  waiting for transfers between devices: 1260 us -> 236 us
  blocking collectives: 301 us -> 0 us
  local copies, waits for them, and re-layouts: 305 us -> 29.3 us
  matrix products: 248 us -> 0 us
  Pallas kernels: 0 us -> 172 us
  other arithmetic: 142 us -> 23 us
  starting transfers between devices: 2.13 us -> 120 us
    unnamed x19 -> x0, waiting for transfers between devices: 1010 us -> none
    dot_general x76 -> x0, matrix products: 248 us -> none  [the longest x16 55.8 us: contract(): return jnp.dot(tokens, weight, preferred_element_type=jnp.float32)]
    concatenate x2 -> x0, local copies, waits for them, and re-layouts: 247 us -> none  [reduce_terms(): joined = jnp.concatenate(pieces, axis=1)]
    all_gather x15 -> x0, blocking collectives: 200 us -> none  [the longest x8 133 us: feature_gather(): return lax.all_gather(tensor, 'col', axis=1, tiled=True)]
    ppermute x0 -> x61, waiting for transfers between devices: none -> 191 us  [the longest x30 120 us: col_swap(): return lax.ppermute(a, 'col', [(i, i ^ mask) for i in range(cols)])]
    pallas_call x0 -> x19, Pallas kernels: none -> 172 us  [the longest x6 47.3 us: weight_grads(): pl.pallas_call(kernel, out_shape=outs, grid_spec=pltpu.PrefetchScalarGrid...]
    all_gather x5 -> x0, waiting for transfers between devices: 163 us -> none  [the longest x1 66.5 us: fetch_experts(): lax.all_gather(weights[3], 'row', axis=0, tiled=True)]
    psum x6 -> x0, blocking collectives: 101 us -> none  [the longest x5 62.5 us: col_total(): return lax.psum(tensor, 'col')]
  transfers between devices with their start and end apart: 18 -> 71, of which waited for: 9 -> 37; matrix products, arithmetic and copies ran while one was open for 25% -> 5% of each run, Pallas kernels for 0% -> 24%
where the time goes in v1:
time: 592 us; the launch traced here: 582 us
  waiting for transfers between devices  236 us (40%)
  Pallas kernels  172 us (29%)
  starting transfers between devices  120 us (20%)
  local copies, waits for them, and re-layouts  29.3 us (5%)
  other arithmetic  23 us (4%)
    ppermute x30, waiting for transfers between devices, col_swap(): return lax.ppermute(a, 'col', [(i, i ^ mask) for i in range(cols)])  120 us
    ppermute x12, waiting for transfers between devices, swap(): return lax.ppermute(a, 'outer', [(i, i ^ mask) for i in range(outer)])  60.3 us
    ppermute x30, starting transfers between devices, col_swap(): return lax.ppermute(a, 'col', [(i, i ^ mask) for i in range(cols)])  55.3 us
    pallas_call x6, Pallas kernels, weight_grads(): pl.pallas_call(kernel, out_shape=outs, grid_spec=pltpu.PrefetchScalarGrid...  47.3 us
    all_to_all x10, starting transfers between devices, exchange(): return lax.all_to_all(a, 'outer', 0, 0, tiled=True)  46 us
    all_to_all x10, waiting for transfers between devices, exchange(): return lax.all_to_all(a, 'outer', 0, 0, tiled=True)  44.7 us
    pallas_call x2, Pallas kernels, run_experts(): pl.pallas_call(kernel, out_shape=outs, grid_spec=pltpu.PrefetchScalarGrid...  43.9 us
    pallas_call x1, Pallas kernels, attend_back(): pl.pallas_call(kernel, out_shape=outs, grid=(micro, heads), in_specs=[hea...  16.9 us
  transfers between devices with their start and end apart: 71, of which 37 were waited for; matrix products, arithmetic and copies ran while one was open for 5% of the time, Pallas kernels for 24%

profile of v1, /device:TPU:0, one launch (start us, length us, event | category | flops | bytes accessed | tf_op | source)
XLA Modules:
  0.0 582.1 jit_solution(5964513531605241286)
XLA Ops:
  58.6 6.7 %project.1 = (bf16[256,2048]{1,0:T(8,128)(2,1)}, f32[256,1280]{1,0:T(8,128)}, bf16[256,1280]{1,0:T(8,128)(2,1)}) custom-call(s32[2]{0:T(128)} %pad_add_fusion.at_ref, bf16[256,512]{1,0:T(8,128)(2,1)} %copy-done.7, bf16[256,512]{1,0:T(8,128)(2,1)} %copy-done.15, bf16[256,512]{1,0:T(8,128)(2,1)} %copy-done.16, bf16[256,512]{1,0:T(8,128)(2,1)} %copy-done.17, ...), custom_call_target="tpu_custom_call" | custom-call | flops 1342177280 | bytes 9577472 | tf_op jit(solution)/shard_map/project/pallas_call | solution.py:162
  69.9 19.9 %collective-permute-done.9 = bf16[256,256]{1,0:T(8,128)(2,1)S(1)} collective-permute-done((bf16[256,256]{1,0:T(8,128)(2,1)S(1)}, bf16[256,256]{1,0:T(8,128)(2,1)S(1)}, u32[]{:S(2)}, u32[]{:S(2)}) %collective-permute-start.9) | collective-permute-done | bytes 131104 | tf_op jit(solution)/shard_map/ppermute | solution.py:820
  98.0 16.0 %attend.1 = (bf16[256,1024]{1,0:T(8,128)(2,1)}, f32[2,8,1,128]{3,2,1,0:T(1,128)}) custom-call(bf16[256,1280]{1,0:T(8,128)(2,1)} %get-tuple-element.109.q_ref, bf16[4,256,256]{2,1,0:T(8,128)(2,1)} %copy-done.34, bf16[4,256,256]{2,1,0:T(8,128)(2,1)} %collective-permute-done.10.k1.v1, bf16[4,256,256]{2,1,0:T(8,128)(2,1)} %copy-done.34, ...), custom_call_target="tpu_custom_call" | custom-call | flops 1073741824 | bytes 2752512 | tf_op jit(solution)/shard_map/attend/pallas_call | solution.py:199
  138.1 16.0 %collective-permute-done.13 = bf16[256,512]{1,0:T(8,128)(2,1)S(1)} collective-permute-done((bf16[256,512]{1,0:T(8,128)(2,1)}, bf16[256,512]{1,0:T(8,128)(2,1)S(1)}, u32[]{:S(2)}, u32[]{:S(2)}) %collective-permute-start.13) | collective-permute-done | bytes 262176 | tf_op jit(solution)/shard_map/ppermute | solution.py:765
  172.0 9.1 %collective-permute-done.15.refs_1_.refs_2_ = bf16[256,512]{1,0:T(8,128)(2,1)S(1)} collective-permute-done((bf16[256,512]{1,0:T(8,128)(2,1)S(1)}, bf16[256,512]{1,0:T(8,128)(2,1)S(1)}, u32[]{:S(2)}, u32[]{:S(2)}) %collective-permute-start.15) | collective-permute-done | bytes 262176 | tf_op jit(solution)/shard_map/ppermute | solution.py:765
  181.0 9.8 %collective-permute-done.16.refs_2_.refs_3_ = bf16[256,512]{1,0:T(8,128)(2,1)S(1)} collective-permute-done((bf16[256,512]{1,0:T(8,128)(2,1)S(1)}, bf16[256,512]{1,0:T(8,128)(2,1)S(1)}, u32[]{:S(2)}, u32[]{:S(2)}) %collective-permute-start.16) | collective-permute-done | bytes 262176 | tf_op jit(solution)/shard_map/ppermute | solution.py:765
  190.8 22.6 %all-to-all-done.4.g_ref.c_ref.refs_4_.refs_5_.refs_6_.refs_7_ = bf16[4,256,2176]{2,1,0:T(8,128)(2,1)} async-done(((bf16[4,256,2176]{2,1,0:T(8,128)(2,1)}), bf16[4,256,2176]{2,1,0:T(8,128)(2,1)}, u32[]{:S(2)}, u32[]{:S(2)}) %all-to-all-start.4) | async-done | bytes 4456480 | tf_op jit(solution)/shard_map/all_to_all | solution.py:768
  219.5 14.5 %run_experts.2 = (bf16[256,768]{1,0:T(8,128)(2,1)}, bf16[256,1536]{1,0:T(8,128)(2,1)}, bf16[256,128]{1,0:T(8,128)(2,1)}, bf16[4,256,2048]{2,1,0:T(8,128)(2,1)}, bf16[4,256,2048]{2,1,0:T(8,128)(2,1)}) custom-call(s32[2]{0:T(128)} %pad_add_fusion.at_ref, bf16[4,256,2176]{2,1,0:T(8,128)(2,1)} %all-to-all-done.4.g_ref.c_ref.refs_4_.refs_5_.refs_6_.refs_7_, ...), custom_call_target="tpu_custom_call" | custom-call | flops 4831838208 | bytes 19070976 | tf_op jit(solution)/shard_map/run_experts/pallas_call | solution.py:439
  234.1 8.3 %collective-permute-done.18.refs_0_.refs_1_ = bf16[256,2048]{1,0:T(8,128)(2,1)S(1)} collective-permute-done((bf16[256,2048]{1,0:T(8,128)(2,1)}, bf16[256,2048]{1,0:T(8,128)(2,1)S(1)}, u32[]{:S(2)}, u32[]{:S(2)}) %collective-permute-start.18) | collective-permute-done | bytes 1048608 | tf_op jit(solution)/shard_map/ppermute | solution.py:820
  242.3 20.7 %collective-permute-done.19.refs_1_.refs_2_ = bf16[256,2048]{1,0:T(8,128)(2,1)S(1)} collective-permute-done((bf16[256,2048]{1,0:T(8,128)(2,1)}, bf16[256,2048]{1,0:T(8,128)(2,1)S(1)}, u32[]{:S(2)}, u32[]{:S(2)}) %collective-permute-start.19) | collective-permute-done | bytes 1048608 | tf_op jit(solution)/shard_map/ppermute | solution.py:820
  264.3 29.3 %run_experts.3 = (bf16[768,768]{1,0:T(8,128)(2,1)}, bf16[768,1536]{1,0:T(8,128)(2,1)}, bf16[768,128]{1,0:T(8,128)(2,1)}, bf16[4,256,2048]{2,1,0:T(8,128)(2,1)}, bf16[4,256,2048]{2,1,0:T(8,128)(2,1)}) custom-call(s32[2]{0:T(128)} %pad_add_fusion.at_ref, ...), custom_call_target="tpu_custom_call", output_to_operand_aliasing={{3}: (13, {}), {4}: (14, {})} | custom-call | flops 14495514624 | bytes 21561344 | tf_op jit(solution)/shard_map/run_experts/pallas_call | solution.py:439
  298.7 12.7 %weight_grads.6 = (bf16[256,2432]{1,0:T(8,128)(2,1)}, bf16[256,2432]{1,0:T(8,128)(2,1)}, bf16[256,2432]{1,0:T(8,128)(2,1)}, bf16[256,2432]{1,0:T(8,128)(2,1)}) custom-call(s32[2]{0:T(128)} %pad_add_fusion.at_ref, bf16[256,2048]{1,0:T(8,128)(2,1)} %second_norm.1.refs_0_, bf16[256,2048]{1,0:T(8,128)(2,1)} %copy-done.3, bf16[256,2048]{1,0:T(8,128)(2,1)} %copy-done.4, ...), custom_call_target="tpu_custom_call" | custom-call | flops 5100273664 | bytes 27000832 | tf_op jit(solution)/shard_map/weight_grads/pallas_call | solution.py:535
  321.1 13.0 %weight_grads.7 = bf16[4,256,2432]{2,1,0:T(8,128)(2,1)} custom-call(s32[2]{0:T(128)} %pad_add_fusion.at_ref, bf16[256,2048]{1,0:T(8,128)(2,1)} %second_norm.1.refs_0_, bf16[256,2048]{1,0:T(8,128)(2,1)} %copy-done.3, bf16[256,2048]{1,0:T(8,128)(2,1)} %copy-done.4, bf16[256,2048]{1,0:T(8,128)(2,1)} %copy-done.5, ...), custom_call_target="tpu_custom_call" | custom-call | flops 5100273664 | bytes 31981568 | tf_op jit(solution)/shard_map/weight_grads/pallas_call | solution.py:535
  334.0 9.8 %all-to-all-done.5.refs_0_ = bf16[4,256,2048]{2,1,0:T(8,128)(2,1)} async-done(((bf16[4,256,2048]{2,1,0:T(8,128)(2,1)}), bf16[4,256,2048]{2,1,0:T(8,128)(2,1)}, u32[]{:S(2)}, u32[]{:S(2)}) %all-to-all-start.5) | async-done | bytes 4194336 | tf_op jit(solution)/shard_map/all_to_all | solution.py:768
  354.2 6.2 %collective-permute-start.28 = (bf16[256,512]{1,0:T(8,128)(2,1)}, bf16[256,512]{1,0:T(8,128)(2,1)S(1)}, u32[]{:S(2)}, u32[]{:S(2)}) collective-permute-start(bf16[256,512]{1,0:T(8,128)(2,1)} %get-tuple-element.147), channel_id=1, source_target_pairs={{0,2},{1,3},{2,0},{3,1},{4,6},{5,7},{6,4},{7,5},{8,10},{9,11},{10,... | collective-permute-start | bytes 786440 | tf_op jit(solution)/shard_map/ppermute | solution.py:765
  364.5 16.0 %collective-permute-done.28 = bf16[256,512]{1,0:T(8,128)(2,1)S(1)} collective-permute-done((bf16[256,512]{1,0:T(8,128)(2,1)}, bf16[256,512]{1,0:T(8,128)(2,1)S(1)}, u32[]{:S(2)}, u32[]{:S(2)}) %collective-permute-start.28) | collective-permute-done | bytes 262176 | tf_op jit(solution)/shard_map/ppermute | solution.py:765
  386.4 7.6 %collective-permute-done.30.refs_1_ = bf16[256,512]{1,0:T(8,128)(2,1)S(1)} collective-permute-done((bf16[256,512]{1,0:T(8,128)(2,1)S(1)}, bf16[256,512]{1,0:T(8,128)(2,1)S(1)}, u32[]{:S(2)}, u32[]{:S(2)}) %collective-permute-start.30) | collective-permute-done | bytes 262176 | tf_op jit(solution)/shard_map/ppermute | solution.py:765
  394.0 9.4 %collective-permute-done.31.refs_2_ = bf16[256,512]{1,0:T(8,128)(2,1)S(1)} collective-permute-done((bf16[256,512]{1,0:T(8,128)(2,1)S(1)}, bf16[256,512]{1,0:T(8,128)(2,1)S(1)}, u32[]{:S(2)}, u32[]{:S(2)}) %collective-permute-start.31) | collective-permute-done | bytes 262176 | tf_op jit(solution)/shard_map/ppermute | solution.py:765
  415.2 16.9 %attend_back.1 = (f32[256,1024]{1,0:T(8,128)}, f32[4,256,128]{2,1,0:T(8,128)}, f32[4,256,128]{2,1,0:T(8,128)}, f32[4,256,128]{2,1,0:T(8,128)}, f32[4,256,128]{2,1,0:T(8,128)}) custom-call(bf16[256,1280]{1,0:T(8,128)(2,1)} %get-tuple-element.109.q_ref, bf16[4,256,256]{2,1,0:T(8,128)(2,1)} %copy-done.34, bf16[4,256,256]{2,1,0:T(8,128)(2,1)} %collective-permute-done.10.k1.v1, ...), custom_call_target="tpu_custom_call" | custom-call | flops 2684354560 | bytes 5898240 | tf_op jit(solution)/shard_map/attend_back/pallas_call | solution.py:257
  453.1 7.6 %collective-permute-done.34.refs_1_ = bf16[256,256]{1,0:T(8,128)(2,1)S(1)} collective-permute-done((bf16[256,256]{1,0:T(8,128)(2,1)}, bf16[256,256]{1,0:T(8,128)(2,1)S(1)}, u32[]{:S(2)}, u32[]{:S(2)}) %collective-permute-start.34) | collective-permute-done | bytes 131104 | tf_op jit(solution)/shard_map/ppermute | solution.py:820
  467.6 8.5 %project_back.1 = (f32[256,512]{1,0:T(8,128)}, bf16[256,512]{1,0:T(8,128)(2,1)}, bf16[256,512]{1,0:T(8,128)(2,1)}, bf16[256,512]{1,0:T(8,128)(2,1)}, f32[1,2048]...) custom-call(s32[2]{0:T(128)} %pad_add_fusion.at_ref, f32[256,1024]{1,0:T(8,128)} %get-tuple-element.167.gq, ...), custom_call_target="tpu_custom_call" | custom-call | flops 1342177280 | bytes 9446400 | tf_op jit(solution)/shard_map/project_back/pallas_call | solution.py:708
  516.3 10.9 %collective-permute-done.50 = bf16[256,512]{1,0:T(8,128)(2,1)} collective-permute-done((bf16[256,512]{1,0:T(8,128)(2,1)}, bf16[256,512]{1,0:T(8,128)(2,1)}, u32[]{:S(2)}, u32[]{:S(2)}) %collective-permute-start.50) | collective-permute-done | bytes 262176 | tf_op jit(solution)/shard_map/ppermute | solution.py:765
  533.4 6.4 %by_columns.1 = (f32[256,3072]{1,0:T(8,128)}, f32[256,3072]{1,0:T(8,128)}, f32[256,3072]{1,0:T(8,128)}, f32[256,128]{1,0:T(8,128)}) custom-call(bf16[4,256,2432]{2,1,0:T(8,128)(2,1)} %all-to-all-done.6.ref), custom_call_target="tpu_custom_call" | custom-call | bytes 14548992 | tf_op jit(solution)/shard_map/by_columns/pallas_call | solution.py:600
  563.9 11.1 %collective-permute-done.53 = bf16[256,512]{1,0:T(8,128)(2,1)S(1)} collective-permute-done((bf16[256,512]{1,0:T(8,128)(2,1)S(1)}, bf16[256,512]{1,0:T(8,128)(2,1)S(1)}, u32[]{:S(2)}, u32[]{:S(2)}) %collective-permute-start.53) | collective-permute-done | bytes 262176 | tf_op jit(solution)/shard_map/ppermute | solution.py:765
  (370 shorter events, 270.8 us)
Async XLA Ops:
  2.7 37.8 %collective-permute-start = (bf16[256,512]{1,0:T(8,128)(2,1)S(1)}, bf16[256,512]{1,0:T(8,128)(2,1)S(1)}, u32[]{:S(2)}, u32[]{:S(2)}) collective-permute-start(bf16[256,512]{1,0:T(8,128)(2,1)S(1)} %pad_maximum_fusion.4.refs_0_.refs_4_), channel_id=1, source_target_pairs={{0,1},{1,0},{2,3},{3,2},{4,5},{5,4},{6,7},{7,6},{8,9},{9,8},{10,11... | collective-permute-start | bytes 786440 | tf_op jit(solution)/shard_map/ppermute | solution.py:765
  5.8 34.8 %collective-permute-start.1 = (bf16[256,512]{1,0:T(8,128)(2,1)S(1)}, bf16[256,512]{1,0:T(8,128)(2,1)S(1)}, u32[]{:S(2)}, u32[]{:S(2)}) collective-permute-start(bf16[256,512]{1,0:T(8,128)(2,1)S(1)} %pad_maximum_fusion.4.refs_0_.refs_4_), channel_id=1, source_target_pairs={{0,2},{1,3},{2,0},{3,1},{4,6},{5,7},{6,4},{7,5},{8,10},{9,11},{10,... | collective-permute-start | bytes 786440 | tf_op jit(solution)/shard_map/ppermute | solution.py:765
  9.1 27.4 %collective-permute-start.3 = (bf16[256,512]{1,0:T(8,128)(2,1)}, bf16[256,512]{1,0:T(8,128)(2,1)}, u32[]{:S(2)}, u32[]{:S(2)}) collective-permute-start(bf16[256,512]{1,0:T(8,128)(2,1)} %pad_maximum_fusion.5), channel_id=1, source_target_pairs={{0,1},{1,0},{2,3},{3,2},{4,5},{5,4},{6,7},{7,6},{8,9},{9,8},{10,11... | collective-permute-start | bytes 786440 | tf_op jit(solution)/shard_map/ppermute | solution.py:765
  9.6 29.0 %collective-permute-start.4 = (bf16[256,512]{1,0:T(8,128)(2,1)}, bf16[256,512]{1,0:T(8,128)(2,1)}, u32[]{:S(2)}, u32[]{:S(2)}) collective-permute-start(bf16[256,512]{1,0:T(8,128)(2,1)} %pad_maximum_fusion.5), channel_id=1, source_target_pairs={{0,2},{1,3},{2,0},{3,1},{4,6},{5,7},{6,4},{7,5},{8,10},{9,11},{10,... | collective-permute-start | bytes 786440 | tf_op jit(solution)/shard_map/ppermute | solution.py:765
  9.6 30.0 %collective-permute-start.5 = (bf16[256,512]{1,0:T(8,128)(2,1)}, bf16[256,512]{1,0:T(8,128)(2,1)}, u32[]{:S(2)}, u32[]{:S(2)}) collective-permute-start(bf16[256,512]{1,0:T(8,128)(2,1)} %pad_maximum_fusion.5), channel_id=1, source_target_pairs={{0,3},{1,2},{2,1},{3,0},{4,7},{5,6},{6,5},{7,4},{8,11},{9,10},{10,... | collective-permute-start | bytes 786440 | tf_op jit(solution)/shard_map/ppermute | solution.py:765
  15.3 34.1 %all-to-all-start = ((bf16[4,256,1280]{2,1,0:T(8,128)(2,1)}), bf16[4,256,1280]{2,1,0:T(8,128)(2,1)}, u32[]{:S(2)}, u32[]{:S(2)}) async-start(bf16[4,256,1280]{2,1,0:T(8,128)(2,1)} %broadcast_in_dim.69), calls=%async_computation | async-start | bytes 5242880 | tf_op jit(solution)/shard_map/all_to_all | solution.py:768
  53.4 38.1 %all-to-all-start.1 = ((bf16[4,256,1152]{2,1,0:T(8,128)(2,1)}), bf16[4,256,1152]{2,1,0:T(8,128)(2,1)S(1)}, u32[]{:S(2)}, u32[]{:S(2)}) async-start(bf16[4,256,1152]{2,1,0:T(8,128)(2,1)} %broadcast_in_dim.71), calls=%async_computation.1 | async-start | bytes 4718592 | tf_op jit(solution)/shard_map/all_to_all | solution.py:768
  93.5 24.3 %all-to-all-start.2 = ((bf16[4,256,768]{2,1,0:T(8,128)(2,1)}), bf16[4,256,768]{2,1,0:T(8,128)(2,1)}, u32[]{:S(2)}, u32[]{:S(2)}) async-start(bf16[4,256,768]{2,1,0:T(8,128)(2,1)} %by_owner.2), calls=%async_computation.2 | async-start | bytes 3145728 | tf_op jit(solution)/shard_map/all_to_all | solution.py:768
  97.8 24.6 %collective-permute-start.11 = (bf16[4,256,1152]{2,1,0:T(8,128)(2,1)S(1)}, bf16[4,256,1152]{2,1,0:T(8,128)(2,1)}, u32[]{:S(2)}, u32[]{:S(2)}) collective-permute-start(bf16[4,256,1152]{2,1,0:T(8,128)(2,1)S(1)} %all-to-all-done.1.own.refs_5_.refs_7_.refs_4_), channel_id=1, source_target_pairs={{0,4},{4,0},{1,5},{5,1},{2,6},{6,2},{3,7},{7,3},{8,12},{12,8},{9,1... | collective-permute-start | bytes 7077896 | tf_op jit(solution)/shard_map/ppermute | solution.py:762
  117.7 40.6 %all-to-all-start.3 = ((bf16[4,256,1536]{2,1,0:T(8,128)(2,1)}), bf16[4,256,1536]{2,1,0:T(8,128)(2,1)}, u32[]{:S(2)}, u32[]{:S(2)}) async-start(bf16[4,256,1536]{2,1,0:T(8,128)(2,1)} %by_owner.3), calls=%async_computation.3 | async-start | bytes 6291456 | tf_op jit(solution)/shard_map/all_to_all | solution.py:768
  128.1 26.1 %collective-permute-start.13 = (bf16[256,512]{1,0:T(8,128)(2,1)}, bf16[256,512]{1,0:T(8,128)(2,1)S(1)}, u32[]{:S(2)}, u32[]{:S(2)}) collective-permute-start(bf16[256,512]{1,0:T(8,128)(2,1)} %get-tuple-element.119), channel_id=1, source_target_pairs={{0,2},{1,3},{2,0},{3,1},{4,6},{5,7},{6,4},{7,5},{8,10},{9,11},{10,... | collective-permute-start | bytes 786440 | tf_op jit(solution)/shard_map/ppermute | solution.py:765
  158.3 55.1 %all-to-all-start.4 = ((bf16[4,256,2176]{2,1,0:T(8,128)(2,1)}), bf16[4,256,2176]{2,1,0:T(8,128)(2,1)}, u32[]{:S(2)}, u32[]{:S(2)}) async-start(bf16[4,256,2176]{2,1,0:T(8,128)(2,1)} %broadcast_in_dim.70), calls=%async_computation.4 | async-start | bytes 8912896 | tf_op jit(solution)/shard_map/all_to_all | solution.py:768
  163.8 55.7 %collective-permute-start.21 = (bf16[4,256,1536]{2,1,0:T(8,128)(2,1)}, bf16[4,256,1536]{2,1,0:T(8,128)(2,1)}, u32[]{:S(2)}, u32[]{:S(2)}) collective-permute-start(bf16[4,256,1536]{2,1,0:T(8,128)(2,1)} %all-to-all-done.3.refs_1_.refs_3_), channel_id=1, source_target_pairs={{0,4},{4,0},{1,5},{5,1},{2,6},{6,2},{3,7},{7,3},{8,12},{12,8},{9,1... | collective-permute-start | bytes 9437192 | tf_op jit(solution)/shard_map/ppermute | solution.py:762
  163.8 55.7 %collective-permute-start.22 = (bf16[4,256,768]{2,1,0:T(8,128)(2,1)}, bf16[4,256,768]{2,1,0:T(8,128)(2,1)}, u32[]{:S(2)}, u32[]{:S(2)}) collective-permute-start(bf16[4,256,768]{2,1,0:T(8,128)(2,1)} %all-to-all-done.2.refs_3_.refs_5_), channel_id=1, source_target_pairs={{0,4},{4,0},{1,5},{5,1},{2,6},{6,2},{3,7},{7,3},{8,12},{12,8},{9,1... | collective-permute-start | bytes 4718600 | tf_op jit(solution)/shard_map/ppermute | solution.py:762
  216.0 26.3 %collective-permute-start.18 = (bf16[256,2048]{1,0:T(8,128)(2,1)}, bf16[256,2048]{1,0:T(8,128)(2,1)S(1)}, u32[]{:S(2)}, u32[]{:S(2)}) collective-permute-start(bf16[256,2048]{1,0:T(8,128)(2,1)} %second_norm.1.refs_0_), channel_id=1, source_target_pairs={{0,8},{8,0},{16,24},{24,16},{1,9},{9,1},{17,25},{25,17},{2,10},{10... | collective-permute-start | bytes 3145736 | tf_op jit(solution)/shard_map/ppermute | solution.py:820
  217.5 45.5 %collective-permute-start.19 = (bf16[256,2048]{1,0:T(8,128)(2,1)}, bf16[256,2048]{1,0:T(8,128)(2,1)S(1)}, u32[]{:S(2)}, u32[]{:S(2)}) collective-permute-start(bf16[256,2048]{1,0:T(8,128)(2,1)} %second_norm.1.refs_0_), channel_id=1, source_target_pairs={{0,16},{8,24},{16,0},{24,8},{1,17},{9,25},{17,1},{25,9},{2,18},{10... | collective-permute-start | bytes 3145736 | tf_op jit(solution)/shard_map/ppermute | solution.py:820
  218.0 45.0 %collective-permute-start.20 = (bf16[256,2048]{1,0:T(8,128)(2,1)}, bf16[256,2048]{1,0:T(8,128)(2,1)S(1)}, u32[]{:S(2)}, u32[]{:S(2)}) collective-permute-start(bf16[256,2048]{1,0:T(8,128)(2,1)} %second_norm.1.refs_0_), channel_id=1, source_target_pairs={{0,24},{8,16},{16,8},{24,0},{1,25},{9,17},{17,9},{25,1},{2,26},{10... | collective-permute-start | bytes 3145736 | tf_op jit(solution)/shard_map/ppermute | solution.py:820
  293.6 50.1 %all-to-all-start.5 = ((bf16[4,256,2048]{2,1,0:T(8,128)(2,1)}), bf16[4,256,2048]{2,1,0:T(8,128)(2,1)}, u32[]{:S(2)}, u32[]{:S(2)}) async-start(bf16[4,256,2048]{2,1,0:T(8,128)(2,1)} %get-tuple-element.133), calls=%async_computation.5 | async-start | bytes 8388608 | tf_op jit(solution)/shard_map/all_to_all | solution.py:768
  343.8 61.0 %all-to-all-start.6 = ((bf16[4,256,2432]{2,1,0:T(8,128)(2,1)}), bf16[4,256,2432]{2,1,0:T(8,128)(2,1)}, u32[]{:S(2)}, u32[]{:S(2)}) async-start(bf16[4,256,2432]{2,1,0:T(8,128)(2,1)} %weight_grads.7), calls=%async_computation.6 | async-start | bytes 9961472 | tf_op jit(solution)/shard_map/all_to_all | solution.py:768
  354.2 26.3 %collective-permute-start.28 = (bf16[256,512]{1,0:T(8,128)(2,1)}, bf16[256,512]{1,0:T(8,128)(2,1)S(1)}, u32[]{:S(2)}, u32[]{:S(2)}) collective-permute-start(bf16[256,512]{1,0:T(8,128)(2,1)} %get-tuple-element.147), channel_id=1, source_target_pairs={{0,2},{1,3},{2,0},{3,1},{4,6},{5,7},{6,4},{7,5},{8,10},{9,11},{10,... | collective-permute-start | bytes 786440 | tf_op jit(solution)/shard_map/ppermute | solution.py:765
  404.9 58.2 %all-to-all-start.7 = ((bf16[4,256,2048]{2,1,0:T(8,128)(2,1)}), bf16[4,256,2048]{2,1,0:T(8,128)(2,1)}, u32[]{:S(2)}, u32[]{:S(2)}) async-start(bf16[4,256,2048]{2,1,0:T(8,128)(2,1)} %get-tuple-element.164), calls=%async_computation.7 | async-start | bytes 8388608 | tf_op jit(solution)/shard_map/all_to_all | solution.py:768
  463.7 47.1 %all-to-all-start.8 = ((bf16[4,256,1024]{2,1,0:T(8,128)(2,1)}), bf16[4,256,1024]{2,1,0:T(8,128)(2,1)S(1)}, u32[]{:S(2)}, u32[]{:S(2)}) async-start(bf16[4,256,1024]{2,1,0:T(8,128)(2,1)} %weight_grads.9), calls=%async_computation.8 | async-start | bytes 4194304 | tf_op jit(solution)/shard_map/all_to_all | solution.py:768
  502.7 24.5 %collective-permute-start.50 = (bf16[256,512]{1,0:T(8,128)(2,1)}, bf16[256,512]{1,0:T(8,128)(2,1)}, u32[]{:S(2)}, u32[]{:S(2)}) collective-permute-start(bf16[256,512]{1,0:T(8,128)(2,1)} %get-tuple-element.184), channel_id=1, source_target_pairs={{0,2},{1,3},{2,0},{3,1},{4,6},{5,7},{6,4},{7,5},{8,10},{9,11},{10,... | collective-permute-start | bytes 786440 | tf_op jit(solution)/shard_map/ppermute | solution.py:765
  512.2 63.1 %all-to-all-start.9 = ((bf16[4,256,1280]{2,1,0:T(8,128)(2,1)}), bf16[4,256,1280]{2,1,0:T(8,128)(2,1)S(1)}, u32[]{:S(2)}, u32[]{:S(2)}) async-start(bf16[4,256,1280]{2,1,0:T(8,128)(2,1)} %weight_grads.11), calls=%async_computation.9 | async-start | bytes 5242880 | tf_op jit(solution)/shard_map/all_to_all | solution.py:768
  (102 other events, 1210.1 us)

commit v2 on v1

v2 whole, which is shorter than its diff:
```python
import functools
import math

import jax
import jax.numpy as jnp
from jax import lax
from jax.experimental import pallas as pl
from jax.experimental.pallas import tpu as pltpu
from jax.sharding import Mesh
from jax.sharding import PartitionSpec as P

EPS = 1e-06
THETA = 1000000.0
NEGATIVE = -1e30
F32 = jnp.float32
BF16 = jnp.bfloat16
VMEM_BYTES = 56 * 1024 * 1024
LANES = 128
ROW = ("outer", "core")


def dot(a, b):
    return jnp.dot(a, b, preferred_element_type=F32)


def dot_bt(a, b):
    return lax.dot_general(a, b, (((1,), (1,)), ((), ())), preferred_element_type=F32)


def dot_at(a, b):
    return lax.dot_general(a, b, (((0,), (0,)), ((), ())), preferred_element_type=F32)


def two_parts(a):
    high = a.astype(BF16)
    return high, (a - high.astype(F32)).astype(BF16)


ANY = pl.BlockSpec(memory_space=pl.ANY)
SMEM = pl.BlockSpec(memory_space=pltpu.SMEM)


def whole(shape):
    return pl.BlockSpec(shape, lambda *_: (0,) * len(shape))


def params(steps=1):
    return pltpu.CompilerParams(
        dimension_semantics=("arbitrary",) * steps, vmem_limit_bytes=VMEM_BYTES
    )


def cost(flops, moved):
    return pl.CostEstimate(flops=int(flops) // 64, bytes_accessed=int(moved) // 64, transcendentals=0)


def nbytes(arrays):
    return sum(math.prod(a.shape) * a.dtype.itemsize for a in arrays)


def struct(shape, dtype):
    return jax.ShapeDtypeStruct(shape, dtype)


def block_count(pair):
    return len(pair[0]) if isinstance(pair[0], list) else pair[0].shape[0]


def weight_copies(at_ref, pairs, fulls, sems, parts, firsts=None):
    copies, base = [], 0
    for i, (pair, full) in enumerate(zip(pairs, fulls)):
        first = firsts[i] if firsts else 0
        blocks = block_count(pair)
        low = blocks // parts
        unit = full.shape[0] // blocks // 2
        for h, sources in enumerate(pair):
            listed = isinstance(sources, list)
            for j in range(blocks):
                to = at_ref[0 if listed else 2] ^ j
                source = sources[j] if listed else sources.at[j]
                row = (2 * (to // low) + h) * (low * unit) + lax.rem(to, low) * unit
                copies.append(
                    pltpu.make_async_copy(
                        source.at[:, pl.ds(first, full.shape[1])],
                        full.at[pl.ds(pl.multiple_of(row, unit), unit)],
                        sems.at[base + h * blocks + to],
                    )
                )
        base += 2 * blocks
    return copies


def weight_wait(pairs, fulls, sems, parts, part=None):
    base = 0
    for pair, full in zip(pairs, fulls):
        blocks = block_count(pair)
        low = blocks // parts
        unit = full.shape[0] // blocks // 2
        for h in range(2):
            for to in range(blocks):
                if part is None or to // low == part:
                    row = (2 * (to // low) + h) * (low * unit) + to % low * unit
                    source = pair[h][0] if isinstance(pair[h], list) else pair[h].at[0]
                    pltpu.make_async_copy(
                        source.at[:, pl.ds(0, full.shape[1])],
                        full.at[pl.ds(row, unit)],
                        sems.at[base + h * blocks + to],
                    ).wait()
        base += 2 * blocks


def full_weight(pair, n=None):
    unit, width = (pair[0][0] if isinstance(pair[0], list) else pair[0]).shape[-2:]
    return pltpu.VMEM((2 * block_count(pair) * unit, n or width), BF16)


def weight_sems(*pairs):
    return pltpu.SemaphoreType.DMA((sum(2 * block_count(pair) for pair in pairs),))


def flat_pair(pair):
    return [a for half in pair for a in (half if isinstance(half, list) else [half])]


def taken(refs, pair):
    halves = []
    for half in pair:
        if isinstance(half, list):
            halves.append(list(refs[: len(half)]))
            refs = refs[len(half) :]
        else:
            halves.append(refs[0])
            refs = refs[1:]
    return tuple(halves), refs


def rms_scale(pieces, width):
    total = sum(jnp.sum(piece * piece, axis=1, keepdims=True) for piece in pieces)
    return lax.rsqrt(total / width + EPS)


def prepare(at, lengths, order, choices, frequency, gains, low, hidden, experts):
    micro, rows, tok = order.shape
    tokens, top = choices.shape
    _, cols, part = gains.shape
    unit = part // 2 // low
    outer, seqs, size = rows // 2, lengths.shape[1], frequency.shape[1]

    def kernel(at_ref, len_ref, order_ref, choice_ref, freq_ref, gain_ref, bias, angles, chosen, spread, *ordered):
        outer_at, core, col = at_ref[1], at_ref[3], at_ref[4]
        for b in range(micro):

            def seq_of(value):
                seq, start, end = jnp.zeros_like(value), jnp.zeros_like(value), 0
                for i in range(seqs):
                    end = end + len_ref[b, i]
                    passed = value >= end
                    seq = seq + jnp.where(passed, 1, 0)
                    start = start + jnp.where(passed, len_ref[b, i], 0)
                return seq, start

            def row(at):
                return order_ref[b, pl.ds(at, 1), :]

            own = row(2 * outer_at + core)
            own_seq, own_start = seq_of(own)
            keys = jnp.concatenate(
                [row(2 * (outer_at ^ j) + (core ^ h)) for h in range(2) for j in range(outer)], axis=0
            )
            key_seq, _ = seq_of(keys)
            lines = [keys, key_seq, own - own_start]
            lines.append(jnp.zeros((tok - 2 * rows - 1, tok), jnp.int32))
            turned = jnp.concatenate(lines, axis=0).astype(F32).T
            own, own_seq = own.astype(F32), own_seq.astype(F32)
            for i in range(rows):
                allowed = (turned[:, rows + i : rows + i + 1] == own_seq) & (
                    turned[:, i : i + 1] <= own
                )
                bias[b, i * tok : (i + 1) * tok] = jnp.where(allowed, 0.0, NEGATIVE)
            angles[b * tok : (b + 1) * tok] = turned[:, 2 * rows : 2 * rows + 1] * freq_ref[...]
        lanes = lax.broadcasted_iota(jnp.int32, (tokens, LANES), 1)
        hits = jnp.zeros((tokens, LANES), F32)
        for i in range(top):
            hits = hits + jnp.where(choice_ref[:, i : i + 1] == lanes, 1.0, 0.0)
        chosen[...] = hits.astype(BF16)
        units = lax.broadcasted_iota(jnp.int32, (LANES, hidden), 1)
        owners = lax.broadcasted_iota(jnp.int32, (LANES, hidden), 0)
        spread[...] = jnp.where(lax.rem(units, experts) == owners, 1.0, 0.0).astype(BF16)
        for i, out in enumerate(ordered):
            for k in range(cols):
                line = gain_ref[i, pl.ds(col ^ k, 1), :]
                for n in range(low):
                    first = line[:, 2 * n * unit : (2 * n + 1) * unit]
                    second = line[:, (2 * n + 1) * unit : (2 * n + 2) * unit]
                    start = k * part + n * unit
                    out[:, start : start + unit] = jnp.where(core == 0, first, second)
                    start = start + part // 2
                    out[:, start : start + unit] = jnp.where(core == 0, second, first)

    outs = (
        struct((micro, rows * tok, tok), F32),
        struct((tokens, size), F32),
        struct((tokens, LANES), BF16),
        struct((LANES, hidden), BF16),
        struct((1, cols * part), F32),
        struct((1, cols * part), F32),
    )
    ins = (order, choices, frequency, gains)
    return pl.pallas_call(
        kernel,
        out_shape=outs,
        grid=(1,),
        in_specs=[SMEM, SMEM] + [whole(a.shape) for a in ins],
        out_specs=[whole(o.shape) for o in outs],
        compiler_params=params(),
        cost_estimate=cost(1, 1),
        name="prepare",
    )(at, lengths, *ins)


def project(at, pieces, part, gain, pair, query_gain, key_gain, cosine, sine, heads, kv_heads):
    parts = len(pieces)
    tokens = cosine.shape[0]
    width = parts * part
    n = flat_pair(pair)[0].shape[-1]
    size = query_gain.shape[1]

    def kernel(at_ref, *refs):
        ins, refs = refs[:parts], refs[parts:]
        weights, refs = taken(refs, pair)
        gain_ref, qg, kg, cos_ref, sin_ref, normed, pre, ready, kv, full, sems = refs
        for copy in weight_copies(at_ref, [weights], [full], sems, parts):
            copy.start()
        values = [ref[...].astype(F32) for ref in ins]
        scale = rms_scale(values, width)
        for k, value in enumerate(values):
            cut = slice(k * part, (k + 1) * part)
            normed[:, cut] = (value * scale * gain_ref[:, cut]).astype(BF16)
        weight_wait([weights], [full], sems, parts)
        pre[...] = dot(normed[...], full[...])
        cosine, sine = cos_ref[...], sin_ref[...]
        for i in range(n // size):
            cut = slice(i * size, (i + 1) * size)
            head = pre[:, cut]
            if i < heads + kv_heads:
                head_gain = qg[...] if i < heads else kg[...]
                head = (
                    head
                    * lax.rsqrt(jnp.mean(head * head, axis=1, keepdims=True) + EPS)
                    * head_gain
                )
                head = head * cosine + pltpu.roll(head, size // 2, 1) * sine
            if i < heads:
                ready[:, cut] = head.astype(BF16)
            else:
                kv[:, (i - heads) * size : (i - heads + 1) * size] = head.astype(BF16)

    outs = (
        struct((tokens, width), BF16),
        struct((tokens, n), F32),
        struct((tokens, heads * size), BF16),
        struct((tokens, n - heads * size), BF16),
    )
    ins = (*pieces, *flat_pair(pair), gain, query_gain, key_gain, cosine, sine)
    return pl.pallas_call(
        kernel,
        out_shape=outs,
        in_specs=[SMEM]
        + [whole((tokens, part)) for _ in pieces]
        + [ANY] * len(flat_pair(pair))
        + [whole(a.shape) for a in (gain, query_gain, key_gain, cosine, sine)],
        out_specs=[whole(o.shape) for o in outs],
        scratch_shapes=[full_weight(pair), weight_sems(pair)],
        grid=(1,),
        compiler_params=params(),
        cost_estimate=cost(9e11, 1),
        name="project",
    )(at, *ins)


def attend(ready, own, other, bias, heads, kv_heads, size):
    micro, keys, tok = bias.shape
    group = heads // kv_heads
    outer = own.shape[0]
    scale = 1.0 / math.sqrt(size)

    def kernel(q_ref, k0, k1, v0, v1, bias_ref, out_ref, lse_ref):
        key = jnp.concatenate([r[...].reshape(outer * tok, size) for r in (k0, k1)], axis=0)
        value = jnp.concatenate([r[...].reshape(outer * tok, size) for r in (v0, v1)], axis=0)
        scores = dot_bt(key, q_ref[...]) * scale + bias_ref[0]
        peak = jnp.max(scores, axis=0, keepdims=True)
        powers = jnp.exp(scores - peak)
        total = jnp.sum(powers, axis=0, keepdims=True)
        probs = (powers * (1.0 / total)).astype(BF16)
        out_ref[...] = dot_at(probs, value).astype(BF16)
        lse_ref[0, 0] = peak + jnp.log(total)

    def kv_spec(first):
        return pl.BlockSpec((outer, tok, size), lambda m, h: (0, m, first + h // group))

    head_spec = pl.BlockSpec((tok, size), lambda m, h: (m, h))
    outs = (struct((micro * tok, heads * size), BF16), struct((micro, heads, 1, tok), F32))
    return pl.pallas_call(
        kernel,
        out_shape=outs,
        grid=(micro, heads),
        in_specs=[
            head_spec,
            kv_spec(0),
            kv_spec(0),
            kv_spec(kv_heads),
            kv_spec(kv_heads),
            pl.BlockSpec((1, keys, tok), lambda m, h: (m, 0, 0)),
        ],
        out_specs=[head_spec, pl.BlockSpec((1, 1, 1, tok), lambda m, h: (m, h, 0, 0))],
        compiler_params=params(2),
        cost_estimate=cost(4 * micro * heads * keys * tok * size, nbytes((own, other, bias))),
        name="attend",
    )(ready, own, other, own, other, bias)


def attend_back(ready, own, other, bias, lse, grad, heads, kv_heads, size):
    micro, keys, tok = bias.shape
    group = heads // kv_heads
    outer = own.shape[0]
    scale = 1.0 / math.sqrt(size)
    mid = keys // 2

    def kernel(q_ref, k0, k1, v0, v1, bias_ref, lse_ref, g_ref, gq, mine, theirs, gk, gv):
        head = pl.program_id(1)
        place = head % group
        key = jnp.concatenate([r[...].reshape(outer * tok, size) for r in (k0, k1)], axis=0)
        value = jnp.concatenate([r[...].reshape(outer * tok, size) for r in (v0, v1)], axis=0)
        query, out_grad = q_ref[...], g_ref[...]
        scores = dot_bt(key, query) * scale + bias_ref[0]
        probs = jnp.exp(scores - lse_ref[0, 0])
        back = dot_bt(value, out_grad)
        centre = jnp.sum(probs * back, axis=0, keepdims=True)
        slope = (probs * (back - centre)).astype(BF16)
        gq[...] = dot_at(slope, key) * scale
        key_part = dot(slope, query) * scale
        value_part = dot(probs.astype(BF16), out_grad)

        @pl.when(place == 0)
        def _():
            gk[...] = key_part
            gv[...] = value_part

        @pl.when(place > 0)
        def _():
            gk[...] += key_part
            gv[...] += value_part

        for g in range(kv_heads):

            @pl.when(head == (g + 1) * group - 1)
            def _(g=g):
                for i, ref in enumerate((gk, gv)):
                    at = (i * kv_heads + g) * size
                    cut = slice(at, at + size)
                    mine[:, :, cut] = ref[:mid].reshape(outer, tok, size)
                    theirs[:, :, cut] = ref[mid:].reshape(outer, tok, size).astype(BF16)

    def kv_spec(start):
        return pl.BlockSpec((outer, tok, size), lambda m, h: (0, m, start + h // group))

    head_spec = pl.BlockSpec((tok, size), lambda m, h: (m, h))
    kv_shape = (outer, micro * tok, 2 * kv_heads * size)
    outs = (
        struct((micro * tok, heads * size), F32),
        struct(kv_shape, F32),
        struct(kv_shape, BF16),
    )
    out_spec = pl.BlockSpec((outer, tok, kv_shape[2]), lambda m, h: (0, m, 0))
    return pl.pallas_call(
        kernel,
        out_shape=outs,
        grid=(micro, heads),
        in_specs=[
            head_spec,
            kv_spec(0),
            kv_spec(0),
            kv_spec(kv_heads),
            kv_spec(kv_heads),
            pl.BlockSpec((1, keys, tok), lambda m, h: (m, 0, 0)),
            pl.BlockSpec((1, 1, 1, tok), lambda m, h: (m, h, 0, 0)),
            head_spec,
        ],
        out_specs=[head_spec, out_spec, out_spec],
        scratch_shapes=[pltpu.VMEM((keys, size), F32)] * 2,
        compiler_params=params(2),
        cost_estimate=cost(10 * micro * heads * keys * tok * size, nbytes((own, other, bias))),
        name="attend_back",
    )(ready, own, other, own, other, bias, lse, grad)


def sum_cores(mine, theirs):
    outer, tokens, n = mine.shape

    def kernel(mine, theirs, *outs):
        for j, out in enumerate(outs):
            out[...] = (mine[j] + theirs[j].astype(F32)).astype(BF16)

    outs = [struct((tokens, n), BF16)] * outer
    return pl.pallas_call(
        kernel,
        out_shape=outs,
        grid=(1,),
        in_specs=[whole(mine.shape)] * 2,
        out_specs=[whole(o.shape) for o in outs],
        compiler_params=params(),
        cost_estimate=cost(1, 1),
        name="sum_cores",
    )(mine, theirs)


def expand(at, a, pair, part, parts):
    tokens, n = a.shape
    outs = [struct((tokens, part), F32 if k == 0 else BF16) for k in range(parts)]

    def kernel(at_ref, a_ref, *refs):
        weights, refs = taken(refs, pair)
        outs, (full, sems) = refs[:parts], refs[parts:]
        for copy in weight_copies(at_ref, [weights], [full], sems, parts):
            copy.start()
        for k, out in enumerate(outs):
            weight_wait([weights], [full], sems, parts, k)
            out[...] = dot_bt(a_ref[...], full[k * part : (k + 1) * part]).astype(out.dtype)

    ins = (a, *flat_pair(pair))
    return pl.pallas_call(
        kernel,
        out_shape=outs,
        in_specs=[SMEM, whole(a.shape)] + [ANY] * len(flat_pair(pair)),
        out_specs=[whole(o.shape) for o in outs],
        scratch_shapes=[full_weight(pair, n), weight_sems(pair)],
        grid=(1,),
        compiler_params=params(),
        cost_estimate=cost(2 * tokens * n * part * parts, nbytes(ins)),
        name="expand",
    )(at, *ins)


def contract(at, pieces, pair, n):
    parts = len(pieces)
    tokens, part = pieces[0].shape
    outs = struct((tokens, n), BF16)

    def kernel(at_ref, *refs):
        ins, refs = refs[:parts], refs[parts:]
        weights, (out, full, sems) = taken(refs, pair)
        for copy in weight_copies(at_ref, [weights], [full], sems, parts):
            copy.start()
        total = 0.0
        for k, ref in enumerate(ins):
            weight_wait([weights], [full], sems, parts, k)
            total = total + dot(ref[...], full[k * part : (k + 1) * part])
        out[...] = total.astype(BF16)

    ins = (*pieces, *flat_pair(pair))
    return pl.pallas_call(
        kernel,
        out_shape=outs,
        in_specs=[SMEM] + [whole(a.shape) for a in pieces] + [ANY] * len(flat_pair(pair)),
        out_specs=whole(outs.shape),
        scratch_shapes=[full_weight(pair, n), weight_sems(pair)],
        grid=(1,),
        compiler_params=params(),
        cost_estimate=cost(2 * tokens * n * part * parts, nbytes(ins)),
        name="contract",
    )(at, *ins)


def second_norm(pieces, gain):
    parts = len(pieces)
    tokens, part = pieces[0].shape
    width = parts * part
    out = struct((tokens, width), BF16)

    def kernel(*refs):
        ins, (gain_ref, out_ref) = refs[:parts], refs[parts:]
        values = [ref[...].astype(F32) for ref in ins]
        scale = rms_scale(values, width)
        for k, value in enumerate(values):
            cut = slice(k * part, (k + 1) * part)
            out_ref[:, cut] = (value * scale * gain_ref[:, cut]).astype(BF16)

    return pl.pallas_call(
        kernel,
        out_shape=out,
        in_specs=[whole(a.shape) for a in pieces] + [whole(gain.shape)],
        out_specs=whole(out.shape),
        grid=(1,),
        compiler_params=params(),
        cost_estimate=cost(tokens * width * 4, nbytes((*pieces, out))),
        name="second_norm",
    )(*pieces, gain)


def run_experts(at, tokens_in, grads, spread, pair, router, router_at, parts, by_part):
    count = len(tokens_in)
    tok, width = tokens_in[0].shape
    hidden = flat_pair(pair)[0].shape[-1] // 3
    part = width // parts

    def kernel(at_ref, s_ref, *refs):
        x_refs, refs = refs[:count], refs[count:]
        g_refs, refs = refs[:count], refs[count:]
        weights, refs = taken(refs, pair)
        routers, refs = taken(refs, router)
        weighted, d_high, logit, *refs = refs
        dxs, refs = refs[:count], refs[count:]
        los, (full, r_ref, x_now, g_now, sems, x_sems) = refs[:count], refs[count:]
        pairs, fulls = [weights, routers], [full, r_ref]
        high, low = slice(0, 2 * hidden), slice(2 * hidden, 3 * hidden)
        step = pl.program_id(0)
        arrivals = [
            [
                pltpu.make_async_copy(x_refs[i], x_now.at[i % 2], x_sems.at[0, i % 2]),
                pltpu.make_async_copy(g_refs[i], g_now.at[i % 2], x_sems.at[1, i % 2]),
            ]
            for i in range(count)
        ]

        @pl.when(step == 0)
        def _():
            for copy in arrivals[0]:
                copy.start()
            for copy in weight_copies(at_ref, pairs, fulls, sems, parts, (0, router_at)):
                copy.start()

        for i in range(count):

            @pl.when(step == i)
            def _(i=i):
                for copy in arrivals[i]:
                    copy.wait()
                if i + 1 < count:
                    for copy in arrivals[i + 1]:
                        copy.start()

        slot = lax.rem(step, 2)
        pre, back, logits = 0.0, 0.0, 0.0
        for k in range(parts):

            @pl.when(step == 0)
            def _(k=k):
                weight_wait(pairs, fulls, sems, parts, k)

            cut = slice(k * part, (k + 1) * part)
            x = x_now[slot, :, cut]
            pre = pre + dot(x, full[cut, high])
            back = back + dot(g_now[slot, :, cut], full[cut, low])
            logits = logits + dot(x, r_ref[cut])
        logits = jnp.where(g_now[slot, :, width:] > 0, logits, NEGATIVE)
        peak = jnp.max(logits, axis=1, keepdims=True)
        powers = jnp.exp(logits - peak)
        gate_probs = powers / jnp.sum(powers, axis=1, keepdims=True)
        spread = s_ref[...]
        one, two = two_parts(gate_probs)
        probs_wide = dot(one, spread) + dot(two, spread)
        gate_pre, up_pre = pre[:, :hidden], pre[:, hidden:]
        sigmoid = 0.5 + 0.5 * jnp.tanh(0.5 * gate_pre)
        swish = gate_pre * sigmoid
        active = swish * up_pre
        weighted_now = (probs_wide * active).astype(BF16)
        weighted[...] = weighted_now
        gate_grad = dot_bt((active * back).astype(BF16), spread)
        logit_low = (
            gate_probs * (gate_grad - jnp.sum(gate_probs * gate_grad, axis=1, keepdims=True))
        ).astype(BF16)
        logit[...] = logit_low
        back = probs_wide * back
        d_high[:, :hidden] = (back * up_pre * (sigmoid + swish * (1.0 - sigmoid))).astype(BF16)
        d_high[:, hidden:] = (back * swish).astype(BF16)
        dx = dot_bt(d_high[...], full[:, high]) + dot_bt(logit_low, r_ref[...])
        total = dot_bt(weighted_now, full[:, low])
        for i, ref in enumerate(dxs):

            @pl.when(step == i)
            def _(i=i, ref=ref):
                ref[...] = dx.astype(BF16)
                for k in range(parts if by_part else 0):
                    los[i][at_ref[4] ^ k] = total[:, k * part : (k + 1) * part].astype(BF16)
                if not by_part:
                    los[i][...] = total.astype(BF16)

    def rows(n):
        return pl.BlockSpec((tok, n), lambda i, at_ref: (i, 0))

    outs = [struct((count * tok, n), BF16) for n in (hidden, 2 * hidden, LANES)]
    outs += [struct((tok, width), BF16)] * count
    outs += [struct((parts, tok, part) if by_part else (tok, width), BF16)] * count
    all_weights = flat_pair(pair) + flat_pair(router)
    ins = (spread, *tokens_in, *grads, *all_weights)
    weighted, d_high, logit, *rest = pl.pallas_call(
        kernel,
        out_shape=outs,
        grid_spec=pltpu.PrefetchScalarGridSpec(
            num_scalar_prefetch=1,
            grid=(count,),
            in_specs=[whole(spread.shape)] + [ANY] * (2 * count + len(all_weights)),
            out_specs=[rows(hidden), rows(2 * hidden), rows(LANES)]
            + [whole(o.shape) for o in outs[3:]],
            scratch_shapes=[
                full_weight(pair),
                full_weight(router, LANES),
                pltpu.VMEM((2, tok, width), BF16),
                pltpu.VMEM((2, tok, grads[0].shape[1]), BF16),
                weight_sems(pair, router),
                pltpu.SemaphoreType.DMA((2, 2)),
            ],
        ),
        compiler_params=params(),
        cost_estimate=cost(12 * count * tok * width * hidden, nbytes([*all_weights, *outs])),
        name="run_experts",
    )(at, *ins)
    return weighted, d_high, logit, rest[:count], rest[count:]


def weight_grads(at, place, outer_at, half_at, lefts, rights, parts, blocks, part, add=None, by_device=False, joined=False):
    unit = part * parts // blocks // 2
    stacks = [stack for group in rights for stack in group]
    left_flat = [a if isinstance(a, tuple) else (a, None) for runs in lefts for a in runs]
    if blocks != parts:
        width = part * parts
        totals = []
        for runs, group in zip(lefts, rights):
            runs = [
                lax.dynamic_index_in_dim(a[0], outer_at ^ a[1], 0, keepdims=False)
                if isinstance(a, tuple)
                else a
                for a in runs
            ]
            left = jnp.concatenate([a[:, :width] for a in runs], axis=0)
            left = left.reshape(left.shape[0], parts, 2, -1)[:, :, half_at].reshape(left.shape[0], -1)
            total = jnp.concatenate([dot_at(left, jnp.concatenate(x, axis=0)) for x in group], axis=1)
            total = total.reshape(blocks, unit, -1)
            order = [place ^ j for j in range(blocks)]
            out = jnp.stack([lax.dynamic_index_in_dim(total, i, 0, keepdims=False) for i in order])
            if add is not None and len(add) == 1:
                start = sum(a.shape[2] for a in totals)
                out = out + add[0][:, :, start : start + out.shape[2]].astype(F32)
            elif add is not None:
                out = out + add[len(totals)].astype(F32)
            order = [outer_at ^ j if by_device else j for j in range(blocks)]
            out = [lax.dynamic_index_in_dim(out, i, 0, keepdims=False) for i in order]
            totals.append(jnp.stack(out).astype(BF16))
        return [jnp.concatenate(totals, axis=2)] if joined else totals
    flat = [r for stack in stacks for r in stack]
    tokens = sum(r.shape[0] for r in stacks[0])
    sizes = [sum(stack[0].shape[1] for stack in group) for group in rights]
    n = sum(sizes)
    outs = [struct((blocks, unit, size), BF16) for size in ([n] if joined else sizes)]
    joins = [stack for stack in stacks if len(stack) > 1]
    extra = [] if add is None else add
    counts = [len(runs) for runs in lefts]

    def kernel(at_ref, *refs):
        left_refs, refs = refs[: len(left_flat)], refs[len(left_flat) :]
        right_refs, refs = refs[: len(flat)], refs[len(flat) :]
        added, refs = refs[: len(extra)], refs[len(extra) :]
        out_refs, fulls = refs[: len(outs)], refs[len(outs) :]
        step = pl.program_id(0)
        stacked = []
        for stack in stacks:
            stack_refs, right_refs = right_refs[: len(stack)], right_refs[len(stack) :]
            if len(stack) == 1:
                stacked.append(stack_refs[0])
            else:
                full, fulls = fulls[0], fulls[1:]
                stacked.append(full)

                @pl.when(step == 0)
                def _(full=full, stack_refs=stack_refs):
                    row = 0
                    for ref in stack_refs:
                        full[row : row + ref.shape[0]] = ref[...]
                        row += ref.shape[0]

        column, rest, more = 0, stacked, left_refs
        for i, (count, group) in enumerate(zip(counts, rights)):
            run_refs, more = more[:count], more[count:]
            now, rest = rest[: len(group)], rest[len(group) :]
            left = jnp.concatenate([ref[...].reshape(-1, unit) for ref in run_refs], axis=0).T
            column = column if joined else 0
            own = 0
            for right in now:
                cut = slice(column, column + right.shape[1])
                value = dot(left, right[...])
                if extra:
                    source, start = (added[0], column) if len(extra) == 1 else (added[i], own)
                    value = value + source[0, :, start : start + right.shape[1]].astype(F32)
                out_refs[0 if joined else i][0, :, cut] = value.astype(BF16)
                column, own = cut.stop, own + right.shape[1]

    def left_spec(a, i):
        if a.ndim == 3:
            return pl.BlockSpec(
                (1, a.shape[1], unit),
                lambda j, at_ref: (at_ref[1] ^ i, 0, 2 * (j ^ at_ref[0]) + half_at),
            )
        return pl.BlockSpec((a.shape[0], unit), lambda j, at_ref: (0, 2 * (j ^ at_ref[0]) + half_at))

    ins = (*[a for a, _ in left_flat], *flat, *extra)
    return pl.pallas_call(
        kernel,
        out_shape=outs,
        grid_spec=pltpu.PrefetchScalarGridSpec(
            num_scalar_prefetch=1,
            grid=(blocks,),
            in_specs=[left_spec(a, i) for a, i in left_flat]
            + [whole(a.shape) for a in flat]
            + [pl.BlockSpec((1,) + a.shape[1:], lambda j, at_ref: (j, 0, 0)) for a in extra],
            out_specs=[
                pl.BlockSpec(
                    (1,) + o.shape[1:], lambda j, at_ref: (at_ref[1] ^ j if by_device else j, 0, 0)
                )
                for o in outs
            ],
            scratch_shapes=[
                pltpu.VMEM((sum(a.shape[0] for a in stack), stack[0].shape[1]), BF16)
                for stack in joins
            ],
        ),
        compiler_params=params(),
        cost_estimate=cost(2 * tokens * blocks * unit * n, nbytes(ins)),
        name="weight_grads",
    )(at, *ins)


def by_owner(weights, blocks):
    unit, hidden = weights[0].shape[0], weights[0].shape[1] // blocks
    if hidden % LANES:
        return jnp.concatenate(
            [w.reshape(unit, blocks, hidden).transpose(1, 0, 2) for w in weights], axis=2
        )

    def kernel(*refs):
        for i, ref in enumerate(refs[:-1]):
            refs[-1][0, :, i * hidden : (i + 1) * hidden] = ref[...]

    out = struct((blocks, unit, hidden * len(weights)), BF16)
    return pl.pallas_call(
        kernel,
        out_shape=out,
        grid=(blocks,),
        in_specs=[pl.BlockSpec((unit, hidden), lambda i: (0, i)) for _ in weights],
        out_specs=pl.BlockSpec((1,) + out.shape[1:], lambda i: (i, 0, 0)),
        compiler_params=params(),
        cost_estimate=cost(1, 1),
        name="by_owner",
    )(*weights)


def by_columns(grads, hidden):
    blocks, unit, n = grads.shape
    starts = (0, hidden, 2 * hidden + LANES)
    if hidden % LANES:
        return [
            grads[:, :, start : start + hidden]
            .transpose(1, 0, 2)
            .reshape(unit, blocks * hidden)
            .astype(F32)
            for start in starts
        ]

    def kernel(ref, *outs):
        for start, out in zip(starts, outs):
            out[...] = ref[0, :, start : start + hidden].astype(F32)

    outs = [struct((unit, blocks * hidden), F32) for _ in starts]
    return pl.pallas_call(
        kernel,
        out_shape=outs,
        grid=(blocks,),
        in_specs=[pl.BlockSpec((1, unit, n), lambda i: (i, 0, 0))],
        out_specs=[pl.BlockSpec((unit, hidden), lambda i: (0, i)) for _ in starts],
        compiler_params=params(),
        cost_estimate=cost(0, nbytes([grads, *outs])),
        name="by_columns",
    )(grads)


def norm_back(values, pieces, scale, gain, gain_grad, outs, width):
    part = pieces[0].shape[1]
    cuts = [slice(k * part, (k + 1) * part) for k in range(len(pieces))]
    inner = 0.0
    for value, piece, cut in zip(values, pieces, cuts):
        gain_grad[:, cut] = jnp.sum(value * (piece * scale), axis=0, keepdims=True)
        inner = inner + jnp.sum(value * gain[:, cut] * piece, axis=1, keepdims=True)
    inner = inner * (scale * scale * scale / width)
    for value, piece, cut, out in zip(values, pieces, cuts, outs):
        out[...] = (value * gain[:, cut] * scale - piece * inner).astype(out.dtype)


def second_norm_back(received, pieces, gain):
    parts, blocks = len(pieces), len(received)
    tokens, width = received[0].shape
    part = width // parts
    outs = [struct((tokens, part), F32 if k == 0 else BF16) for k in range(parts)]
    outs.append(struct((1, width), F32))

    def kernel(*refs):
        got, refs = refs[:blocks], refs[blocks:]
        ins, (gain_ref, *outs, gain_grad) = refs[:parts], refs[parts:]
        values = []
        for k in range(parts):
            cut = slice(k * part, (k + 1) * part)
            values.append(sum(ref[:, cut].astype(F32) for ref in got))
        pieces = [ref[...].astype(F32) for ref in ins]
        scale = rms_scale(pieces, width)
        norm_back(values, pieces, scale, gain_ref, gain_grad, outs, width)

    ins = (*received, *pieces, gain)
    return pl.pallas_call(
        kernel,
        out_shape=outs,
        in_specs=[whole(a.shape) for a in ins],
        out_specs=[whole(o.shape) for o in outs],
        grid=(1,),
        compiler_params=params(),
        cost_estimate=cost(tokens * width * 20, nbytes(ins)),
        name="second_norm_back",
    )(*ins)


def project_back(
    at, grad_q, grad_kv, pre, pieces, gain, pair, query_gain, key_gain, cosine, sine, heads, kv_heads, gain_grad_two, router, experts
):
    parts, runs, blocks = len(pieces), len(grad_q), len(grad_kv)
    tokens, n = pre.shape
    width = gain.shape[1]
    part = width // parts
    size = query_gain.shape[1]
    gain_lines = -(-(2 * parts + 1) // 16) * 16
    lines = gain_lines + -(-experts // 16) * 16
    router_rows = router.shape[0]
    outs = [struct((tokens, part), F32)] + [struct((tokens + 2 * lines, part), BF16)] * (parts - 1)
    outs += [struct((tokens, n), BF16), struct((lines, part), F32)]

    def kernel(at_ref, pre_ref, two_ref, router_ref, *refs):
        gq, refs = refs[:runs], refs[runs:]
        gkv, refs = refs[:blocks], refs[blocks:]
        ins, refs = refs[:parts], refs[parts:]
        weights, refs = taken(refs, pair)
        gain_ref, qg, kg, cos_ref, sin_ref, *refs = refs
        outs, (d_wide, sums, gain_grad, full, sems) = refs[:parts], refs[parts:]
        for copy in weight_copies(at_ref, [weights], [full], sems, parts):
            copy.start()
        cosine, sine = cos_ref[...], sin_ref[...]
        totals = [jnp.zeros((1, size), F32), jnp.zeros((1, size), F32)]
        for i in range(n // size):
            cut = slice(i * size, (i + 1) * size)
            if i < heads:
                grad = jnp.concatenate([ref[:, cut] for ref in gq], axis=0)
            else:
                kv_cut = slice((i - heads) * size, (i - heads + 1) * size)
                grad = sum(ref[:, kv_cut].astype(F32) for ref in gkv)
            if i < heads + kv_heads:
                which = 0 if i < heads else 1
                gain_row = (qg, kg)[which][...]
                grad = grad * cosine + pltpu.roll(grad * sine, size // 2, 1)
                head = pre_ref[:, cut]
                scale = lax.rsqrt(jnp.mean(head * head, axis=1, keepdims=True) + EPS)
                unit = head * scale
                totals[which] = totals[which] + jnp.sum(grad * unit, axis=0, keepdims=True)
                grad = grad * gain_row
                grad = scale * (grad - unit * jnp.mean(grad * unit, axis=1, keepdims=True))
            d_wide[:, cut] = grad.astype(BF16)
        weight_wait([weights], [full], sems, parts)
        values = [
            dot_bt(d_wide[...], full[k * part : (k + 1) * part]) for k in range(parts)
        ]
        pieces = [ref[...].astype(F32) for ref in ins]
        scale = rms_scale(pieces, width)
        cut_outs = [outs[0]] + [out.at[:tokens] for out in outs[1:]]
        norm_back(values, pieces, scale, gain_ref, gain_grad, cut_outs, width)
        sums[...] = jnp.zeros_like(sums)
        for i, ref in enumerate((gain_grad, two_ref)):
            for k in range(parts):
                sums[i * parts + k : i * parts + k + 1] = ref[:, k * part : (k + 1) * part]
        for i, total in enumerate(totals):
            sums[2 * parts : 2 * parts + 1, i * size : (i + 1) * size] = total
        sums[gain_lines : gain_lines + experts, :router_rows] = router_ref[...].T[:experts]
        for out in outs[1:]:
            one, two = two_parts(sums[...])
            out[tokens : tokens + lines] = one
            out[tokens + lines :] = two

    ins = (pre, gain_grad_two, router, *grad_q, *grad_kv, *pieces, *flat_pair(pair))
    ins = (*ins, gain, query_gain, key_gain, cosine, sine)
    return pl.pallas_call(
        kernel,
        out_shape=outs,
        in_specs=[SMEM]
        + [whole(a.shape) for a in (pre, gain_grad_two, router, *grad_q, *grad_kv)]
        + [whole((tokens, part)) for _ in pieces]
        + [ANY] * len(flat_pair(pair))
        + [whole(a.shape) for a in (gain, query_gain, key_gain, cosine, sine)],
        out_specs=[whole(o.shape) for o in outs],
        scratch_shapes=[pltpu.VMEM((1, width), F32), full_weight(pair), weight_sems(pair)],
        grid=(1,),
        compiler_params=params(),
        cost_estimate=cost(2 * tokens * width * n, nbytes(ins)),
        name="project_back",
    )(at, *ins)


def sum_blocks(grads, widths, first=0):
    blocks = len(grads)
    unit = grads[0].shape[-2]

    def kernel(*refs):
        ins, outs = refs[:blocks], refs[blocks:]
        start = first
        for out in outs:
            cut = slice(start, start + out.shape[1])
            parts = [ref[:, cut] if len(ref.shape) == 2 else ref[0, :, cut] for ref in ins]
            out[...] = sum(a.astype(F32) for a in parts)
            start = cut.stop

    def spec(i, a):
        if a.ndim == 2:
            return whole(a.shape)
        return pl.BlockSpec((1,) + a.shape[1:], lambda _: (i, 0, 0))

    outs = [struct((unit, width), F32) for width in widths]
    return pl.pallas_call(
        kernel,
        out_shape=outs,
        grid=(1,),
        in_specs=[spec(i, a) for i, a in enumerate(grads)],
        out_specs=[whole(o.shape) for o in outs],
        compiler_params=params(),
        cost_estimate=cost(1, 1),
        name="sum_blocks",
    )(*grads)


def finish(at, residual, own, arrived, own_sums, low, unit_rows, experts):
    others = len(arrived)
    tokens, part = own.shape
    parts, half = others + 1, part // 2
    unit = half // low
    lines = own_sums.shape[0]
    gain_lines = -(-(2 * parts + 1) // 16) * 16

    def kernel(at_ref, residual, own, *refs):
        arrived, refs = refs[:others], refs[others:]
        own_sums, out, sums, router = refs
        even, col = at_ref[3] == 0, at_ref[4]

        def put(ref, rows, value):
            first = jnp.where(even, value[:, :half], value[:, half:])
            second = jnp.where(even, value[:, half:], value[:, :half])
            for i in range(low):
                cut = slice(i * unit, (i + 1) * unit)
                ref[rows, 2 * i * unit : (2 * i + 1) * unit] = first[:, cut].astype(ref.dtype)
                ref[rows, (2 * i + 1) * unit : (2 * i + 2) * unit] = second[:, cut].astype(ref.dtype)

        value = residual[...] + own[...]
        for ref in arrived:
            value = value + ref[:tokens].astype(F32)
        put(out, slice(0, tokens), value)
        got = [ref[tokens : tokens + lines].astype(F32) for ref in arrived]
        got = [a + ref[tokens + lines :].astype(F32) for a, ref in zip(got, arrived)]
        total = own_sums[...]
        for a in got:
            total = total + a
        sums[...] = total[:gain_lines]
        router[...] = total[gain_lines : gain_lines + experts, :unit_rows].T
        for i in range(2):
            for k in range(parts):
                line = own_sums[i * parts + k : i * parts + k + 1]
                for mask, a in enumerate(got, 1):
                    row = i * parts + (k ^ mask)
                    line = line + a[row : row + 1]
                for to in range(parts):

                    @pl.when(col ^ k == to)
                    def _(i=i, to=to, line=line):
                        put(sums, slice(i * parts + to, i * parts + to + 1), line)

    outs = (
        struct((tokens, part), BF16),
        struct((gain_lines, part), F32),
        struct((unit_rows, experts), F32),
    )
    ins = (residual, own, *arrived, own_sums)
    return pl.pallas_call(
        kernel,
        out_shape=outs,
        grid=(1,),
        in_specs=[SMEM] + [whole(a.shape) for a in ins],
        out_specs=[whole(o.shape) for o in outs],
        compiler_params=params(),
        cost_estimate=cost(1, 1),
        name="finish",
    )(at, *ins)


def per_device(
    layer_in,
    out_grad,
    lengths,
    token_order,
    choices,
    norm_gain,
    w_query,
    w_key,
    w_value,
    query_gain,
    key_gain,
    w_out,
    ffn_gain,
    w_router,
    w_gate,
    w_up,
    w_down,
):
    micro, tok, part = layer_in.shape
    outer, cols = lax.axis_size("outer"), lax.axis_size("col")
    rows = 2 * outer
    tokens = micro * tok
    width = part * cols
    outer_at, core_at, col_at = (lax.axis_index(name) for name in ("outer", "core", "col"))
    row_at = outer_at * 2 + core_at
    low = outer // cols
    unit = width // rows
    half = part // 2
    size = query_gain.shape[0]
    heads = w_query.shape[1] // size
    kv_heads = w_key.shape[1] // size
    experts = w_router.shape[1]
    hidden = w_gate.shape[1] // outer
    repeats = hidden // experts

    place = outer_at ^ (col_at * low)
    at = jnp.stack([place, outer_at, col_at * low, core_at, col_at]).astype(jnp.int32)

    def core_swap(a):
        return lax.ppermute(a, "core", [(0, 1), (1, 0)])

    def col_swap(a, mask):
        return lax.ppermute(a, "col", [(i, i ^ mask) for i in range(cols)])

    def exchange(a):
        return lax.all_to_all(a, "outer", 0, 0, tiled=True)

    def col_exchange(a):
        return lax.all_to_all(a, "col", 0, 0, tiled=True)

    def for_all(a):
        return jnp.broadcast_to(a[None], (outer,) + a.shape)

    def after(a, b):
        return lax.optimization_barrier((a, b))[0]

    def to_halves(a):
        blocks = a.reshape(a.shape[:-1] + (low, 2, unit))
        first = blocks[..., 0, :].reshape(a.shape[:-1] + (half,))
        second = blocks[..., 1, :].reshape(a.shape[:-1] + (half,))
        even = core_at == 0
        return jnp.concatenate(
            [jnp.where(even, first, second), jnp.where(even, second, first)], axis=-1
        )

    def from_halves(a):
        even = core_at == 0
        first = jnp.where(even, a[..., :half], a[..., half:]).reshape(a.shape[:-1] + (low, unit))
        second = jnp.where(even, a[..., half:], a[..., :half]).reshape(a.shape[:-1] + (low, unit))
        return jnp.stack([first, second], axis=-2).reshape(a.shape)

    def col_gather(a):
        return [a] + [col_swap(a, k) for k in range(1, cols)]

    def col_total(pieces):
        total = pieces[0]
        for k in range(1, cols):
            total = total + col_swap(pieces[k], k).astype(F32)
        return total

    def swap(a, mask):
        return lax.ppermute(a, "outer", [(i, i ^ mask) for i in range(outer)])

    def gather(a):
        return [a] + [swap(a, j) for j in range(1, outer)]

    def scatter(blocks):
        return [blocks[0]] + [swap(blocks[j], j) for j in range(1, outer)]

    def swap(a, mask):
        return lax.ppermute(a, "outer", [(i, i ^ mask) for i in range(outer)])

    def gather(a):
        return [a] + [swap(a, j) for j in range(1, outer)]

    def scatter(blocks):
        return [blocks[0]] + [swap(blocks[j], j) for j in range(1, outer)]

    def both(*arrays):
        return lax.optimization_barrier(arrays)

    def both_cores(a):
        return a, [core_swap(b) for b in a] if isinstance(a, list) else core_swap(a)

    own_in = to_halves(layer_in).reshape(tokens, part)
    own_grad = to_halves(out_grad).reshape(tokens, part)
    w_in = gather(jnp.concatenate([w_query, w_key, w_value], axis=1))
    arrived = col_gather(own_in)
    w_back = jnp.concatenate([w_out, jnp.pad(w_router, ((0, 0), (0, LANES - experts)))], axis=1)
    w_back = for_all(w_back)
    weights = by_owner([w_gate, w_up, w_down], outer)
    q_gain, k_gain = query_gain[None, :], key_gain[None, :]
    frequency = jnp.exp(jnp.arange(size // 2, dtype=F32) * (-2.0 * math.log(THETA) / size))
    bias, angles, chosen, spread, gain_one, gain_two = prepare(
        at,
        lengths,
        token_order.reshape(micro, rows, tok),
        choices.reshape(tokens, -1),
        jnp.concatenate([frequency, frequency])[None, :],
        jnp.stack([norm_gain, ffn_gain]).reshape(2, cols, part),
        low,
        hidden,
        experts,
    )
    cosine = jnp.cos(angles)
    sine = jnp.sin(angles) * jnp.where(jnp.arange(size) < size // 2, -1.0, 1.0)

    w_back, weights, bias = both(w_back, weights, bias)
    w_back = exchange(w_back)
    w_in, arrived, weights, chosen, bias, cosine, sine, gain_one, gain_two, spread = both(
        w_in, arrived, weights, chosen, bias, cosine, sine, gain_one, gain_two, spread
    )
    own_grads = col_gather(after(own_grad, w_in))
    w_in = both_cores(w_in)
    normed_one, pre, ready, kv = project(
        at, arrived, part, gain_one, w_in, q_gain, k_gain, cosine, sine, heads, kv_heads
    )
    near = [j for j in range(1, outer) if not j & (j - 1)]
    far = [j for j in range(1, outer) if j & (j - 1)]
    far_grads, _ = both(jnp.concatenate([own_grad, chosen], axis=1), w_in[0])
    far_grads = [swap(far_grads, j) for j in far]
    kv_own = jnp.stack(gather(kv))
    kv_own, w_back, far_grads = both(kv_own, w_back, far_grads)
    weights = exchange(after(weights, w_back))
    kv_other = core_swap(kv_own)
    w_back = both_cores(w_back)
    attended, lse = attend(ready, kv_own, kv_other, bias, heads, kv_heads, size)
    attn_parts = expand(at, attended, w_back, part, cols)
    attn_parts, own_grads = both(attn_parts, own_grads)

    grads = [jnp.concatenate(own_grads + [chosen], axis=1)] + [None] * (outer - 1)
    near_grads = [swap(grads[0], j) for j in near]

    residual = own_in.astype(F32) + col_total(attn_parts)
    residual, weights = both(residual, weights)
    full_res = col_gather(residual.astype(BF16))
    full_res, near_grads, weights = both(full_res, near_grads, weights)
    for j, a in zip(near, near_grads):
        grads[j] = a
    weights = both_cores(weights)
    normed_two = second_norm(full_res, gain_two)
    expert_in = gather(normed_two)
    far_grads, _ = both(far_grads, normed_two)
    for j, a in zip(far, far_grads):
        grads[j] = jnp.concatenate(col_gather(a[:, :part]) + [a[:, part:]], axis=1)

    results, dx, lo = [], [None] * outer, [None] * outer
    order = [0] + far + near
    for group in [[0]] + [far[i : i + 4] for i in range(0, len(far), 4)] + [near]:
        *result, dx_now, lo_now = run_experts(
            at,
            [expert_in[j] for j in group],
            [grads[j] for j in group],
            spread,
            weights,
            w_back,
            heads * size,
            cols,
            group != near,
        )
        for j, a, b in zip(group, dx_now, lo_now):
            dx[j], lo[j] = a, b
        if group == [0]:
            expert_in, lo[0] = both(expert_in, lo[0])
        elif group != near:
            for j in group:
                dx[j] = swap(dx[j], j)
            if group[-1] == far[-1]:
                lo_sums = col_exchange(jnp.concatenate([lo[j] for j in [0] + far], axis=1))
        results.append(result)
    far_dx, results[-1] = both([dx[j] for j in far], results[-1])
    weighted, d_high, logit_low = [list(arrays) for arrays in zip(*results)]
    for j in near:
        dx[j] = swap(dx[j], j)
    sizes = (cols, outer, part)
    expert_sides = (
        [[expert_in[j] for j in order], [grads[j] for j in order]],
        [[d_high, logit_low], [weighted]],
    )
    (other,) = weight_grads(at, place, outer_at, 1, *expert_sides, *sizes, joined=True)
    other, near_dx, lo_sums = both(other, [dx[j] for j in near], lo_sums)
    lo_sums = jnp.sum(lo_sums.astype(F32), axis=0)
    lo[0] = lo_sums[:tokens]
    lo_far = [lo_sums[i * tokens : (i + 1) * tokens].astype(BF16) for i in range(1, len(far) + 1)]
    other = core_swap(other)
    *spread_two, gain_grad_two = second_norm_back([dx[0]] + near_dx + far_dx, full_res, gain_two)
    lo_near, _ = both([lo[j] for j in near], spread_two)
    lo_near = [swap(a, j) for j, a in zip(near, lo_near)]
    (expert_grads,) = weight_grads(
        at, place, outer_at, 0, *expert_sides, *sizes, [other], True, True
    )
    spread_two[0], expert_grads = both(spread_two[0], expert_grads)
    grad_residual = own_grad.astype(F32) + col_total(spread_two)
    grad_residual, lo_near, expert_grads = both(grad_residual, lo_near, expert_grads)
    expert_grads = exchange(expert_grads)
    grad_feats = col_gather(grad_residual.astype(BF16))

    lo_near = sum(a.astype(F32) for a in lo_near)
    lo_near = [
        lo_near[:, k * part : (k + 1) * part].astype(F32 if k == 0 else BF16) for k in range(cols)
    ]
    grad_feats, lo_near = both(grad_feats, lo_near)
    back_attended = contract(at, grad_feats, w_back, heads * size)
    lo_near = col_total(after(lo_near, back_attended))
    grad_q, kv_mine, kv_theirs = attend_back(
        ready, kv_own, kv_other, bias, lse, back_attended, heads, kv_heads, size
    )
    kv_theirs, expert_grads, lo_near = both(kv_theirs, expert_grads, lo_near)
    kv_sums = sum_cores(kv_mine, core_swap(kv_theirs))
    grad_kv = scatter(kv_sums)
    router_part = jnp.sum(
        expert_grads[:, :, 2 * hidden : 2 * hidden + LANES].astype(F32), axis=0
    )
    feats, lo_far, _ = both(grad_feats, lo_far, kv_sums)
    lo_far = [swap(a, j) for j, a in zip(far, lo_far)]
    feats = [jnp.concatenate(feats, axis=1)]
    (other,) = weight_grads(at, place, outer_at, 1, [feats], [[[attended]]], *sizes)
    (out_grads,) = weight_grads(
        at, place, outer_at, 0, [feats], [[[attended]]], *sizes, [core_swap(other)], True
    )
    grad_kv, out_grads = both(grad_kv, out_grads)
    out_grads = exchange(out_grads)
    *spread_one, d_wide, sums = project_back(
        at,
        [grad_q],
        grad_kv,
        pre,
        arrived,
        gain_one,
        w_in,
        q_gain,
        k_gain,
        cosine,
        sine,
        heads,
        kv_heads,
        gain_grad_two,
        router_part,
        experts,
    )
    (other,) = weight_grads(at, place, outer_at, 1, [[normed_one]], [[[d_wide]]], *sizes)
    other, expert_grads, lo_far = both(other, expert_grads, lo_far)
    grad_gate_w, grad_up_w, grad_down_w = by_columns(expert_grads, hidden)
    other = jnp.stack([core_swap(other[j]) for j in range(outer)])
    other, grad_gate_w, out_grads = both(other, grad_gate_w, out_grads)
    (wide_grads,) = weight_grads(
        at, place, outer_at, 0, [[normed_one]], [[[d_wide]]], *sizes, [other], True
    )
    spread_one, wide_grads = both(spread_one, wide_grads)
    wide_grads = exchange(wide_grads)

    got = [col_swap(spread_one[k], k) for k in range(1, cols)]
    layer_out = residual + lo[0] + lo_near + sum(a.astype(F32) for a in lo_far)
    layer_out = from_halves(layer_out.astype(BF16)).reshape(micro, tok, part)
    input_grad, sums, grad_router = finish(
        at, grad_residual, spread_one[0], got, sums, low, unit, experts
    )
    input_grad = input_grad.reshape(micro, tok, part)
    sums = sums + core_swap(sums)
    sums = sum(gather(sums))
    (grad_out_w,) = sum_blocks([out_grads] * outer, [heads * size])
    wide_grads, input_grad, layer_out, grad_out_w, sums, grad_router = both(
        wide_grads, input_grad, layer_out, grad_out_w, sums, grad_router
    )
    head_sums = sums[2 * cols, : 2 * size]
    grad_query_w, grad_key_w, grad_value_w = sum_blocks(
        [wide_grads] * outer, [w.shape[1] for w in (w_query, w_key, w_value)]
    )
    return (
        layer_out,
        input_grad,
        sums[:cols].reshape(width),
        grad_query_w,
        grad_key_w,
        grad_value_w,
        head_sums[:size],
        head_sums[size:],
        grad_out_w,
        sums[cols : 2 * cols].reshape(width),
        grad_router,
        grad_gate_w,
        grad_up_w,
        grad_down_w,
    )


def solution(mesh):
    rows, cols = mesh.devices.shape
    split = Mesh(mesh.devices.reshape(rows // 2, 2, cols), ("outer", "core", "col"))
    tokens_placed = P(None, ROW, "col")
    weight_placed = P(ROW, "col")
    return jax.shard_map(
        per_device,
        mesh=split,
        in_specs=(
            tokens_placed,
            tokens_placed,
            P(),
            P(),
            P(None, ROW, None),
            P(),
            weight_placed,
            weight_placed,
            weight_placed,
            P(),
            P(),
            weight_placed,
            P(),
            P(ROW, None),
            weight_placed,
            weight_placed,
            weight_placed,
        ),
        out_specs=(
            tokens_placed,
            tokens_placed,
            P(),
            weight_placed,
            weight_placed,
            weight_placed,
            P(),
            P(),
            weight_placed,
            P(),
            P(ROW, None),
            weight_placed,
            weight_placed,
            weight_placed,
        ),
        check_vma=False,
    )
```

time: 592 us -> 524 us (0.89)
  the two profiles are of different devices: /device:TPU:0 before, /device:TPU:10 now
where the time goes in v2:
time: 524 us; the launch traced here: 516 us
  Pallas kernels  193 us (37%)
  waiting for transfers between devices  178 us (34%)
  starting transfers between devices  96.6 us (18%)
  local copies, waits for them, and re-layouts  29.4 us (6%)
  other arithmetic  17.4 us (3%)
    ppermute x27, waiting for transfers between devices, col_swap(): return lax.ppermute(a, 'col', [(i, i ^ mask) for i in range(cols)])  121 us
    ppermute x24, waiting for transfers between devices, swap(): return lax.ppermute(a, 'outer', [(i, i ^ mask) for i in range(outer)])  54.3 us
    pallas_call x3, Pallas kernels, run_experts(): pl.pallas_call(kernel, out_shape=outs, grid_spec=pltpu.PrefetchScalarGrid...  52.8 us
    pallas_call x6, Pallas kernels, weight_grads(): pl.pallas_call(kernel, out_shape=outs, grid_spec=pltpu.PrefetchScalarGrid...  45.8 us
    ppermute x27, starting transfers between devices, col_swap(): return lax.ppermute(a, 'col', [(i, i ^ mask) for i in range(cols)])  37.3 us
    ppermute x24, starting transfers between devices, swap(): return lax.ppermute(a, 'outer', [(i, i ^ mask) for i in range(outer)])  28.6 us
    all_to_all x5, starting transfers between devices, exchange(): return lax.all_to_all(a, 'outer', 0, 0, tiled=True)  24.7 us
    unnamed x157, local copies, waits for them, and re-layouts  18.8 us
  transfers between devices with their start and end apart: 72, of which 23 were waited for; matrix products, arithmetic and copies ran while one was open for 5% of the time, Pallas kernels for 31%

profile of v2, /device:TPU:10, one launch (start us, length us, event | category | flops | bytes accessed | tf_op | source)
XLA Modules:
  0.0 515.8 jit_solution(5301898527719777645)
XLA Ops:
  11.1 12.9 %collective-permute-done.5.refs_3_.refs_8_ = bf16[256,512]{1,0:T(8,128)(2,1)S(1)} collective-permute-done((bf16[256,512]{1,0:T(8,128)(2,1)S(1)}, bf16[256,512]{1,0:T(8,128)(2,1)S(1)}, u32[]{:S(2)}, u32[]{:S(2)}) %collective-permute-start.5) | collective-permute-done | bytes 262176 | tf_op jit(solution)/shard_map/ppermute | solution.py:1046
  45.0 6.7 %project.1 = (bf16[256,2048]{1,0:T(8,128)(2,1)}, f32[256,1280]{1,0:T(8,128)}, bf16[256,1024]{1,0:T(8,128)(2,1)}, bf16[256,256]{1,0:T(8,128)(2,1)}) custom-call(s32[5]{0:T(128)} %stack.62.at_ref, bf16[256,512]{1,0:T(8,128)(2,1)} %copy-done.28, bf16[256,512]{1,0:T(8,128)(2,1)} %copy-done.48, bf16[256,512]{1,0:T(8,128)(2,1)} %collective-permute-done.4.refs_2_.refs_7_, ...), custom_call_target="tpu_custom_call" | custom-call | flops 14062499840 | tf_op jit(solution)/shard_map/project/pallas_call | solution.py:265
  55.2 26.5 %collective-permute-done.12 = bf16[256,256]{1,0:T(8,128)(2,1)S(1)} collective-permute-done((bf16[256,256]{1,0:T(8,128)(2,1)}, bf16[256,256]{1,0:T(8,128)(2,1)S(1)}, u32[]{:S(2)}, u32[]{:S(2)}) %collective-permute-start.12) | collective-permute-done | bytes 131104 | tf_op jit(solution)/shard_map/ppermute | solution.py:1094
  97.2 16.1 %attend.1 = (bf16[256,1024]{1,0:T(8,128)(2,1)}, f32[2,8,1,128]{3,2,1,0:T(1,128)}) custom-call(bf16[256,1024]{1,0:T(8,128)(2,1)} %get-tuple-element.201.q_ref, bf16[4,256,256]{2,1,0:T(8,128)(2,1)} %copy-done.4, bf16[4,256,256]{2,1,0:T(8,128)(2,1)} %copy-done.10, bf16[4,256,256]{2,1,0:T(8,128)(2,1)} %copy-done.4, bf16[4,256,256]{2,1,0:T(8,128)(2,1)} %copy-done.10, ...), custom_call_target="tpu_custom_call" | custom-call | flops 16777216 | bytes 32768 | tf_op jit(solution)/shard_map/attend/pallas_call | solution.py:303
  125.1 7.1 %collective-permute-done.19 = bf16[256,512]{1,0:T(8,128)(2,1)S(1)} collective-permute-done((bf16[256,512]{1,0:T(8,128)(2,1)S(1)}, bf16[256,512]{1,0:T(8,128)(2,1)S(1)}, u32[]{:S(2)}, u32[]{:S(2)}) %collective-permute-start.19) | collective-permute-done | bytes 262176 | tf_op jit(solution)/shard_map/ppermute | solution.py:1046
  132.2 10.4 %collective-permute-done.20 = bf16[256,512]{1,0:T(8,128)(2,1)S(1)} collective-permute-done((bf16[256,512]{1,0:T(8,128)(2,1)S(1)}, bf16[256,512]{1,0:T(8,128)(2,1)S(1)}, u32[]{:S(2)}, u32[]{:S(2)}) %collective-permute-start.20) | collective-permute-done | bytes 262176 | tf_op jit(solution)/shard_map/ppermute | solution.py:1046
  152.8 14.6 %collective-permute-done.26.refs_3_.refs_7_ = bf16[256,2176]{1,0:T(8,128)(2,1)S(1)} collective-permute-done((bf16[256,2176]{1,0:T(8,128)(2,1)S(1)}, bf16[256,2176]{1,0:T(8,128)(2,1)S(1)}, u32[]{:S(2)}, u32[]{:S(2)}) %collective-permute-start.26) | collective-permute-done | bytes 1114144 | tf_op jit(solution)/shard_map/ppermute | solution.py:1094
  181.6 6.9 %collective-permute-done.32 = bf16[256,512]{1,0:T(8,128)(2,1)S(1)} collective-permute-done((bf16[256,512]{1,0:T(8,128)(2,1)S(1)}, bf16[256,512]{1,0:T(8,128)(2,1)S(1)}, u32[]{:S(2)}, u32[]{:S(2)}) %collective-permute-start.32) | collective-permute-done | bytes 262176 | tf_op jit(solution)/shard_map/ppermute | solution.py:1046
  192.2 6.5 %collective-permute-done.31 = bf16[256,512]{1,0:T(8,128)(2,1)S(1)} collective-permute-done((bf16[256,512]{1,0:T(8,128)(2,1)S(1)}, bf16[256,512]{1,0:T(8,128)(2,1)S(1)}, u32[]{:S(2)}, u32[]{:S(2)}) %collective-permute-start.31) | collective-permute-done | bytes 262176 | tf_op jit(solution)/shard_map/ppermute | solution.py:1046
  199.1 12.9 %collective-permute-done.33 = bf16[256,512]{1,0:T(8,128)(2,1)S(1)} collective-permute-done((bf16[256,512]{1,0:T(8,128)(2,1)S(1)}, bf16[256,512]{1,0:T(8,128)(2,1)S(1)}, u32[]{:S(2)}, u32[]{:S(2)}) %collective-permute-start.33) | collective-permute-done | bytes 262176 | tf_op jit(solution)/shard_map/ppermute | solution.py:1046
  215.1 14.4 %run_experts.3 = (bf16[256,768]{1,0:T(8,128)(2,1)}, bf16[256,1536]{1,0:T(8,128)(2,1)}, bf16[256,128]{1,0:T(8,128)(2,1)}, bf16[256,2048]{1,0:T(8,128)(2,1)}, bf16[4,256,512]{2,1,0:T(8,128)(2,1)}) custom-call(s32[5]{0:T(128)} %stack.62.at_ref, bf16[128,768]{1,0:T(8,128)(2,1)} %get-tuple-element.200.s_ref, bf16[256,2048]{1,0:T(8,128)(2,1)} %second_norm.1.refs_0_, ...), custom_call_target="tpu_custom_call" | custom-call | flops 75497472 | bytes 273408 | tf_op jit(solution)/shard_map/run_experts/pallas_call | solution.py:596
  230.4 14.9 %run_experts.4 = (bf16[256,768]{1,0:T(8,128)(2,1)}, bf16[256,1536]{1,0:T(8,128)(2,1)}, bf16[256,128]{1,0:T(8,128)(2,1)}, bf16[256,2048]{1,0:T(8,128)(2,1)}, bf16[4,256,512]{2,1,0:T(8,128)(2,1)}) custom-call(s32[5]{0:T(128)} %stack.62.at_ref, bf16[128,768]{1,0:T(8,128)(2,1)} %get-tuple-element.200.s_ref, bf16[256,2048]{1,0:T(8,128)(2,1)} %copy-done.9, ...), custom_call_target="tpu_custom_call" | custom-call | flops 75497472 | bytes 273408 | tf_op jit(solution)/shard_map/run_experts/pallas_call | solution.py:596
  253.3 23.5 %run_experts.5 = (bf16[512,768]{1,0:T(8,128)(2,1)}, bf16[512,1536]{1,0:T(8,128)(2,1)}, bf16[512,128]{1,0:T(8,128)(2,1)}, bf16[256,2048]{1,0:T(8,128)(2,1)}, bf16...) custom-call(s32[5]{0:T(128)} %stack.62.at_ref, ...), custom_call_target="tpu_custom_call" | custom-call | flops 150994944 | bytes 325632 | tf_op jit(solution)/shard_map/run_experts/pallas_call | solution.py:596
  278.8 11.9 %weight_grads.6 = bf16[4,256,2432]{2,1,0:T(8,128)(2,1)} custom-call(s32[5]{0:T(128)} %stack.62.at_ref, bf16[256,2048]{1,0:T(8,128)(2,1)} %second_norm.1.refs_0_, bf16[256,2048]{1,0:T(8,128)(2,1)} %copy-done.9, bf16[256,2048]{1,0:T(8,128)(2,1)} %collective-permute-done.28.refs_0_.refs_2_, bf16[256,2048]{1,0:T(8,128)(2,1)} %collective-permute-done.29.refs_1_.refs_3_, ...), custom_call_target="tpu_custom_call" | custom-call | flops 79691776 | bytes 212992 | tf_op jit(solution)/shard_map/weight_grads/pallas_call | solution.py:706
  290.7 9.8 %collective-permute-done.35.refs_1_ = bf16[256,2048]{1,0:T(8,128)(2,1)S(1)} collective-permute-done((bf16[256,2048]{1,0:T(8,128)(2,1)}, bf16[256,2048]{1,0:T(8,128)(2,1)S(1)}, u32[]{:S(2)}, u32[]{:S(2)}) %collective-permute-start.35) | collective-permute-done | bytes 1048608 | tf_op jit(solution)/shard_map/ppermute | solution.py:1094
  312.2 12.6 %weight_grads.7 = bf16[4,256,2432]{2,1,0:T(8,128)(2,1)} custom-call(s32[5]{0:T(128)} %stack.62.at_ref, bf16[256,2048]{1,0:T(8,128)(2,1)} %second_norm.1.refs_0_, bf16[256,2048]{1,0:T(8,128)(2,1)} %copy-done.9, bf16[256,2048]{1,0:T(8,128)(2,1)} %collective-permute-done.28.refs_0_.refs_2_, bf16[256,2048]{1,0:T(8,128)(2,1)} %collective-permute-done.29.refs_1_.refs_3_, ...), custom_call_target="tpu_custom_call" | custom-call | flops 79691776 | bytes 290816 | tf_op jit(solution)/shard_map/weight_grads/pallas_call | solution.py:706
  329.1 6.1 %collective-permute-done.40 = bf16[256,512]{1,0:T(8,128)(2,1)S(1)} collective-permute-done((bf16[256,512]{1,0:T(8,128)(2,1)}, bf16[256,512]{1,0:T(8,128)(2,1)S(1)}, u32[]{:S(2)}, u32[]{:S(2)}) %collective-permute-start.40) | collective-permute-done | bytes 262176 | tf_op jit(solution)/shard_map/ppermute | solution.py:1046
  347.2 10.3 %collective-permute-done.45.refs_3_ = bf16[256,512]{1,0:T(8,128)(2,1)S(1)} collective-permute-done((bf16[256,512]{1,0:T(8,128)(2,1)S(1)}, bf16[256,512]{1,0:T(8,128)(2,1)S(1)}, u32[]{:S(2)}, u32[]{:S(2)}) %collective-permute-start.45) | collective-permute-done | bytes 262176 | tf_op jit(solution)/shard_map/ppermute | solution.py:1046
  373.5 18.3 %attend_back.1 = (f32[256,1024]{1,0:T(8,128)}, f32[4,256,256]{2,1,0:T(8,128)}, bf16[4,256,256]{2,1,0:T(8,128)(2,1)}) custom-call(bf16[256,1024]{1,0:T(8,128)(2,1)} %get-tuple-element.201.q_ref, bf16[4,256,256]{2,1,0:T(8,128)(2,1)} %copy-done.4, bf16[4,256,256]{2,1,0:T(8,128)(2,1)} %copy-done.10, bf16[4,256,256]{2,1,0:T(8,128)(2,1)} %copy-done.4, ...), custom_call_target="tpu_custom_call" | custom-call | flops 41943040 | bytes 32768 | tf_op jit(solution)/shard_map/attend_back/pallas_call | solution.py:375
  429.1 9.6 %project_back.1 = (f32[256,512]{1,0:T(8,128)}, bf16[320,512]{1,0:T(8,128)(2,1)}, bf16[320,512]{1,0:T(8,128)(2,1)}, bf16[320,512]{1,0:T(8,128)(2,1)}, bf16[256,1280]{1,0:T(8,128)(2,1)}, /*index=5*/f32[32,512]{1,0:T(8,128)}) custom-call(s32[5]{0:T(128)} %stack.62.at_ref, f32[256,1280]{1,0:T(8,128)} %get-tuple-element.199.pre_ref, ...), custom_call_target="tpu_custom_call" | custom-call | flops 20971520 | bytes 149776 | tf_op jit(solution)/shard_map/project_back/pallas_call | solution.py:893
  446.8 6.4 %by_columns.1 = (f32[256,3072]{1,0:T(8,128)}, f32[256,3072]{1,0:T(8,128)}, f32[256,3072]{1,0:T(8,128)}) custom-call(bf16[4,256,2432]{2,1,0:T(8,128)(2,1)} %all-to-all-done.3.ref), custom_call_target="tpu_custom_call" | custom-call | bytes 225280 | tf_op jit(solution)/shard_map/by_columns/pallas_call | solution.py:773
  470.0 8.6 %collective-permute-done.59.refs_0_ = bf16[320,512]{1,0:T(8,128)(2,1)S(1)} collective-permute-done((bf16[320,512]{1,0:T(8,128)(2,1)}, bf16[320,512]{1,0:T(8,128)(2,1)S(1)}, u32[]{:S(2)}, u32[]{:S(2)}) %collective-permute-start.59) | collective-permute-done | bytes 327712 | tf_op jit(solution)/shard_map/ppermute | solution.py:1046
  478.6 12.1 %collective-permute-done.60.refs_1_ = bf16[320,512]{1,0:T(8,128)(2,1)S(1)} collective-permute-done((bf16[320,512]{1,0:T(8,128)(2,1)}, bf16[320,512]{1,0:T(8,128)(2,1)S(1)}, u32[]{:S(2)}, u32[]{:S(2)}) %collective-permute-start.60) | collective-permute-done | bytes 327712 | tf_op jit(solution)/shard_map/ppermute | solution.py:1046
  490.6 6.2 %collective-permute-done.61.refs_2_ = bf16[320,512]{1,0:T(8,128)(2,1)S(1)} collective-permute-done((bf16[320,512]{1,0:T(8,128)(2,1)}, bf16[320,512]{1,0:T(8,128)(2,1)S(1)}, u32[]{:S(2)}, u32[]{:S(2)}) %collective-permute-start.61) | collective-permute-done | bytes 327712 | tf_op jit(solution)/shard_map/ppermute | solution.py:1046
  (347 shorter events, 228.8 us)
Async XLA Ops:
  5.3 32.7 %collective-permute-start.4 = (bf16[256,512]{1,0:T(8,128)(2,1)S(1)}, bf16[256,512]{1,0:T(8,128)(2,1)}, u32[]{:S(2)}, u32[]{:S(2)}) collective-permute-start(bf16[256,512]{1,0:T(8,128)(2,1)S(1)} %pad_maximum_fusion.4.refs_0_.refs_5_), channel_id=1, source_target_pairs={{0,2},{1,3},{2,0},{3,1},{4,6},{5,7},{6,4},{7,5},{8,10},{9,11},{10,... | collective-permute-start | bytes 786440 | tf_op jit(solution)/shard_map/ppermute | solution.py:1046
  6.7 31.3 %collective-permute-start.2 = (bf16[256,1280]{1,0:T(8,128)(2,1)S(1)}, bf16[256,1280]{1,0:T(8,128)(2,1)}, u32[]{:S(2)}, u32[]{:S(2)}) collective-permute-start(bf16[256,1280]{1,0:T(8,128)(2,1)S(1)} %constant_dynamic-update-slice_fusion.refs_4_.refs_9_), channel_id=1, source_target_pairs={{0,24},{8,16},{16,8},{24,0},{1,25},{9,17},{17,9},{25,1},{2,26},{10... | collective-permute-start | bytes 1966088 | tf_op jit(solution)/shard_map/ppermute | solution.py:1094
  8.3 29.8 %collective-permute-start.1 = (bf16[256,1280]{1,0:T(8,128)(2,1)S(1)}, bf16[256,1280]{1,0:T(8,128)(2,1)}, u32[]{:S(2)}, u32[]{:S(2)}) collective-permute-start(bf16[256,1280]{1,0:T(8,128)(2,1)S(1)} %constant_dynamic-update-slice_fusion.refs_4_.refs_9_), channel_id=1, source_target_pairs={{0,16},{8,24},{16,0},{24,8},{1,17},{9,25},{17,1},{25,9},{2,18},{10... | collective-permute-start | bytes 1966088 | tf_op jit(solution)/shard_map/ppermute | solution.py:1094
  8.6 29.4 %collective-permute-start = (bf16[256,1280]{1,0:T(8,128)(2,1)S(1)}, bf16[256,1280]{1,0:T(8,128)(2,1)}, u32[]{:S(2)}, u32[]{:S(2)}) collective-permute-start(bf16[256,1280]{1,0:T(8,128)(2,1)S(1)} %constant_dynamic-update-slice_fusion.refs_4_.refs_9_), channel_id=1, source_target_pairs={{0,8},{8,0},{16,24},{24,16},{1,9},{9,1},{17,25},{25,17},{2,10},{10... | collective-permute-start | bytes 1966088 | tf_op jit(solution)/shard_map/ppermute | solution.py:1094
  39.1 45.4 %all-to-all-start = ((bf16[4,256,1152]{2,1,0:T(8,128)(2,1)}), bf16[4,256,1152]{2,1,0:T(8,128)(2,1)S(1)}, u32[]{:S(2)}, u32[]{:S(2)}) async-start(bf16[4,256,1152]{2,1,0:T(8,128)(2,1)} %broadcast_in_dim.24), calls=%async_computation | async-start | bytes 4718592 | tf_op jit(solution)/shard_map/all_to_all | solution.py:1049
  43.4 41.1 %collective-permute-start.13 = (bf16[256,640]{1,0:T(8,128)(2,1)S(1)}, bf16[256,640]{1,0:T(8,128)(2,1)}, u32[]{:S(2)}, u32[]{:S(2)}) collective-permute-start(bf16[256,640]{1,0:T(8,128)(2,1)S(1)} %pad_maximum_fusion.3), channel_id=1, source_target_pairs={{0,24},{8,16},{16,8},{24,0},{1,25},{9,17},{17,9},{25,1},{2,26},{10... | collective-permute-start | bytes 983048 | tf_op jit(solution)/shard_map/ppermute | solution.py:1094
  51.7 30.1 %collective-permute-start.12 = (bf16[256,256]{1,0:T(8,128)(2,1)}, bf16[256,256]{1,0:T(8,128)(2,1)S(1)}, u32[]{:S(2)}, u32[]{:S(2)}) collective-permute-start(bf16[256,256]{1,0:T(8,128)(2,1)} %get-tuple-element.202), channel_id=1, source_target_pairs={{0,24},{8,16},{16,8},{24,0},{1,25},{9,17},{17,9},{25,1},{2,26},{10... | collective-permute-start | bytes 393224 | tf_op jit(solution)/shard_map/ppermute | solution.py:1094
  53.2 30.3 %collective-permute-start.11 = (bf16[256,256]{1,0:T(8,128)(2,1)}, bf16[256,256]{1,0:T(8,128)(2,1)S(1)}, u32[]{:S(2)}, u32[]{:S(2)}) collective-permute-start(bf16[256,256]{1,0:T(8,128)(2,1)} %get-tuple-element.202), channel_id=1, source_target_pairs={{0,16},{8,24},{16,0},{24,8},{1,17},{9,25},{17,1},{25,9},{2,18},{10... | collective-permute-start | bytes 393224 | tf_op jit(solution)/shard_map/ppermute | solution.py:1094
  54.7 28.8 %collective-permute-start.10 = (bf16[256,256]{1,0:T(8,128)(2,1)}, bf16[256,256]{1,0:T(8,128)(2,1)S(1)}, u32[]{:S(2)}, u32[]{:S(2)}) collective-permute-start(bf16[256,256]{1,0:T(8,128)(2,1)} %get-tuple-element.202), channel_id=1, source_target_pairs={{0,8},{8,0},{16,24},{24,16},{1,9},{9,1},{17,25},{25,17},{2,10},{10... | collective-permute-start | bytes 393224 | tf_op jit(solution)/shard_map/ppermute | solution.py:1094
  84.5 28.8 %collective-permute-start.15 = (bf16[4,256,1152]{2,1,0:T(8,128)(2,1)S(1)}, bf16[4,256,1152]{2,1,0:T(8,128)(2,1)}, u32[]{:S(2)}, u32[]{:S(2)}) collective-permute-start(bf16[4,256,1152]{2,1,0:T(8,128)(2,1)S(1)} %all-to-all-done.refs_0_.refs_4_.refs_6_), channel_id=1, source_target_pairs={{0,4},{4,0},{1,5},{5,1},{2,6},{6,2},{3,7},{7,3},{8,12},{12,8},{9,1... | collective-permute-start | bytes 7077896 | tf_op jit(solution)/shard_map/ppermute | solution.py:1043
  86.0 62.2 %all-to-all-start.1 = ((bf16[4,256,2304]{2,1,0:T(8,128)(2,1)}), bf16[4,256,2304]{2,1,0:T(8,128)(2,1)}, u32[]{:S(2)}, u32[]{:S(2)}) async-start(bf16[4,256,2304]{2,1,0:T(8,128)(2,1)} %by_owner.1), calls=%async_computation.1 | async-start | bytes 9437184 | tf_op jit(solution)/shard_map/all_to_all | solution.py:1049
  119.1 48.3 %collective-permute-start.26 = (bf16[256,2176]{1,0:T(8,128)(2,1)S(1)}, bf16[256,2176]{1,0:T(8,128)(2,1)S(1)}, u32[]{:S(2)}, u32[]{:S(2)}) collective-permute-start(bf16[256,2176]{1,0:T(8,128)(2,1)S(1)} %constant_dynamic-update-slice_fusion.3.refs_1_.refs_4_), channel_id=1, source_target_pairs={{0,16},{8,24},{16,0},{24,8},{1,17},{9,25},{17,1},{25,9},{2,18},{10... | collective-permute-start | bytes 3342344 | tf_op jit(solution)/shard_map/ppermute | solution.py:1094
  120.6 46.7 %collective-permute-start.25 = (bf16[256,2176]{1,0:T(8,128)(2,1)S(1)}, bf16[256,2176]{1,0:T(8,128)(2,1)S(1)}, u32[]{:S(2)}, u32[]{:S(2)}) collective-permute-start(bf16[256,2176]{1,0:T(8,128)(2,1)S(1)} %constant_dynamic-update-slice_fusion.3.refs_1_.refs_4_), channel_id=1, source_target_pairs={{0,8},{8,0},{16,24},{24,16},{1,9},{9,1},{17,25},{25,17},{2,10},{10... | collective-permute-start | bytes 3342344 | tf_op jit(solution)/shard_map/ppermute | solution.py:1094
  171.1 41.7 %collective-permute-start.27 = (bf16[4,256,2304]{2,1,0:T(8,128)(2,1)}, bf16[4,256,2304]{2,1,0:T(8,128)(2,1)S(1)}, u32[]{:S(2)}, u32[]{:S(2)}) collective-permute-start(bf16[4,256,2304]{2,1,0:T(8,128)(2,1)} %all-to-all-done.1.refs_2_.refs_4_), channel_id=1, source_target_pairs={{0,4},{4,0},{1,5},{5,1},{2,6},{6,2},{3,7},{7,3},{8,12},{12,8},{9,1... | collective-permute-start | bytes 14155784 | tf_op jit(solution)/shard_map/ppermute | solution.py:1043
  178.1 51.3 %collective-permute-start.30 = (bf16[256,2048]{1,0:T(8,128)(2,1)}, bf16[256,2048]{1,0:T(8,128)(2,1)S(1)}, u32[]{:S(2)}, u32[]{:S(2)}) collective-permute-start(bf16[256,2048]{1,0:T(8,128)(2,1)} %second_norm.1.refs_0_), channel_id=1, source_target_pairs={{0,24},{8,16},{16,8},{24,0},{1,25},{9,17},{17,9},{25,1},{2,26},{10... | collective-permute-start | bytes 3145736 | tf_op jit(solution)/shard_map/ppermute | solution.py:1094
  179.7 49.8 %collective-permute-start.29 = (bf16[256,2048]{1,0:T(8,128)(2,1)}, bf16[256,2048]{1,0:T(8,128)(2,1)}, u32[]{:S(2)}, u32[]{:S(2)}) collective-permute-start(bf16[256,2048]{1,0:T(8,128)(2,1)} %second_norm.1.refs_0_), channel_id=1, source_target_pairs={{0,16},{8,24},{16,0},{24,8},{1,17},{9,25},{17,1},{25,9},{2,18},{10... | collective-permute-start | bytes 3145736 | tf_op jit(solution)/shard_map/ppermute | solution.py:1094
  180.9 48.5 %collective-permute-start.28 = (bf16[256,2048]{1,0:T(8,128)(2,1)}, bf16[256,2048]{1,0:T(8,128)(2,1)}, u32[]{:S(2)}, u32[]{:S(2)}) collective-permute-start(bf16[256,2048]{1,0:T(8,128)(2,1)} %second_norm.1.refs_0_), channel_id=1, source_target_pairs={{0,8},{8,0},{16,24},{24,16},{1,9},{9,1},{17,25},{25,17},{2,10},{10... | collective-permute-start | bytes 3145736 | tf_op jit(solution)/shard_map/ppermute | solution.py:1094
  248.1 53.4 %all-to-all-start.2 = ((bf16[4,512,512]{2,1,0:T(8,128)(2,1)}), bf16[4,512,512]{2,1,0:T(8,128)(2,1)S(1)}, u32[]{:S(2)}, u32[]{:S(2)}) async-start(bf16[4,512,512]{2,1,0:T(8,128)(2,1)} %pad_maximum_fusion.1), calls=%async_computation.2 | async-start | bytes 4194304 | tf_op jit(solution)/shard_map/all_to_all | solution.py:1052
  306.5 28.8 %collective-permute-start.41 = (bf16[256,2048]{1,0:T(8,128)(2,1)S(1)}, bf16[256,2048]{1,0:T(8,128)(2,1)}, u32[]{:S(2)}, u32[]{:S(2)}) collective-permute-start(bf16[256,2048]{1,0:T(8,128)(2,1)S(1)} %copy-done.62), channel_id=1, source_target_pairs={{0,8},{8,0},{16,24},{24,16},{1,9},{9,1},{17,25},{25,17},{2,10},{10... | collective-permute-start | bytes 3145736 | tf_op jit(solution)/shard_map/ppermute | solution.py:1094
  335.4 62.2 %all-to-all-start.3 = ((bf16[4,256,2432]{2,1,0:T(8,128)(2,1)}), bf16[4,256,2432]{2,1,0:T(8,128)(2,1)}, u32[]{:S(2)}, u32[]{:S(2)}) async-start(bf16[4,256,2432]{2,1,0:T(8,128)(2,1)} %weight_grads.7), calls=%async_computation.3 | async-start | bytes 9961472 | tf_op jit(solution)/shard_map/all_to_all | solution.py:1049
  408.9 35.0 %collective-permute-start.54 = (bf16[256,512]{1,0:T(8,128)(2,1)S(1)}, bf16[256,512]{1,0:T(8,128)(2,1)S(1)}, u32[]{:S(2)}, u32[]{:S(2)}) collective-permute-start(bf16[256,512]{1,0:T(8,128)(2,1)S(1)} %slice.144), channel_id=1, source_target_pairs={{0,24},{8,16},{16,8},{24,0},{1,25},{9,17},{17,9},{25,1},{2,26},{10... | collective-permute-start | bytes 786440 | tf_op jit(solution)/shard_map/ppermute | solution.py:1094
  424.7 30.3 %all-to-all-start.4 = ((bf16[4,256,1024]{2,1,0:T(8,128)(2,1)}), bf16[4,256,1024]{2,1,0:T(8,128)(2,1)S(1)}, u32[]{:S(2)}, u32[]{:S(2)}) async-start(bf16[4,256,1024]{2,1,0:T(8,128)(2,1)} %weight_grads.9), calls=%async_computation.4 | async-start | bytes 4194304 | tf_op jit(solution)/shard_map/all_to_all | solution.py:1049
  460.8 49.1 %all-to-all-start.5 = ((bf16[4,256,1280]{2,1,0:T(8,128)(2,1)}), bf16[4,256,1280]{2,1,0:T(8,128)(2,1)S(1)}, u32[]{:S(2)}, u32[]{:S(2)}) async-start(bf16[4,256,1280]{2,1,0:T(8,128)(2,1)} %weight_grads.11), calls=%async_computation.5 | async-start | bytes 5242880 | tf_op jit(solution)/shard_map/all_to_all | solution.py:1049
  468.1 28.7 %collective-permute-start.61 = (bf16[320,512]{1,0:T(8,128)(2,1)}, bf16[320,512]{1,0:T(8,128)(2,1)S(1)}, u32[]{:S(2)}, u32[]{:S(2)}) collective-permute-start(bf16[320,512]{1,0:T(8,128)(2,1)} %get-tuple-element.326), channel_id=1, source_target_pairs={{0,3},{1,2},{2,1},{3,0},{4,7},{5,6},{6,5},{7,4},{8,11},{9,10},{10,... | collective-permute-start | bytes 983048 | tf_op jit(solution)/shard_map/ppermute | solution.py:1046
  (117 other events, 1439.9 us)

commit v3 on v2

--- a/solution.py
+++ b/solution.py
@@ -44,9 +44,9 @@
     return pl.BlockSpec(shape, lambda *_: (0,) * len(shape))
 
 
-def params(steps=1):
+def params(steps=1, limit=VMEM_BYTES):
     return pltpu.CompilerParams(
-        dimension_semantics=("arbitrary",) * steps, vmem_limit_bytes=VMEM_BYTES
+        dimension_semantics=("arbitrary",) * steps, vmem_limit_bytes=limit
     )
 
 
@@ -273,7 +273,7 @@
         scratch_shapes=[full_weight(pair), weight_sems(pair)],
         grid=(1,),
         compiler_params=params(),
-        cost_estimate=cost(9e11, 1),
+        cost_estimate=cost(4.5e11, 1),
         name="project",
     )(at, *ins)
 
@@ -284,39 +284,45 @@
     outer = own.shape[0]
     scale = 1.0 / math.sqrt(size)
 
-    def kernel(q_ref, k0, k1, v0, v1, bias_ref, out_ref, lse_ref):
-        key = jnp.concatenate([r[...].reshape(outer * tok, size) for r in (k0, k1)], axis=0)
-        value = jnp.concatenate([r[...].reshape(outer * tok, size) for r in (v0, v1)], axis=0)
-        scores = dot_bt(key, q_ref[...]) * scale + bias_ref[0]
-        peak = jnp.max(scores, axis=0, keepdims=True)
-        powers = jnp.exp(scores - peak)
-        total = jnp.sum(powers, axis=0, keepdims=True)
-        probs = (powers * (1.0 / total)).astype(BF16)
-        out_ref[...] = dot_at(probs, value).astype(BF16)
-        lse_ref[0, 0] = peak + jnp.log(total)
-
-    def kv_spec(first):
-        return pl.BlockSpec((outer, tok, size), lambda m, h: (0, m, first + h // group))
-
-    head_spec = pl.BlockSpec((tok, size), lambda m, h: (m, h))
+    def kernel(q_ref, own_ref, other_ref, bias_ref, out_ref, lse_ref):
+        for h in range(heads):
+            key, value = (
+                jnp.concatenate(
+                    [
+                        ref[:, :, i * size : (i + 1) * size].reshape(outer * tok, size)
+                        for ref in (own_ref, other_ref)
+                    ],
+                    axis=0,
+                )
+                for i in (h // group, kv_heads + h // group)
+            )
+            cut = slice(h * size, (h + 1) * size)
+            scores = dot_bt(key, q_ref[:, cut]) * scale + bias_ref[0]
+            peak = jnp.max(scores, axis=0, keepdims=True)
+            powers = jnp.exp(scores - peak)
+            total = jnp.sum(powers, axis=0, keepdims=True)
+            probs = (powers * (1.0 / total)).astype(BF16)
+            out_ref[:, cut] = dot_at(probs, value).astype(BF16)
+            lse_ref[0, h] = peak + jnp.log(total)
+
+    kv_spec = pl.BlockSpec((outer, tok, own.shape[2]), lambda m: (0, m, 0))
+    head_spec = pl.BlockSpec((tok, heads * size), lambda m: (m, 0))
     outs = (struct((micro * tok, heads * size), BF16), struct((micro, heads, 1, tok), F32))
     return pl.pallas_call(
         kernel,
         out_shape=outs,
-        grid=(micro, heads),
+        grid=(micro,),
         in_specs=[
             head_spec,
-            kv_spec(0),
-            kv_spec(0),
-            kv_spec(kv_heads),
-            kv_spec(kv_heads),
-            pl.BlockSpec((1, keys, tok), lambda m, h: (m, 0, 0)),
+            kv_spec,
+            kv_spec,
+            pl.BlockSpec((1, keys, tok), lambda m: (m, 0, 0)),
         ],
-        out_specs=[head_spec, pl.BlockSpec((1, 1, 1, tok), lambda m, h: (m, h, 0, 0))],
-        compiler_params=params(2),
+        out_specs=[head_spec, pl.BlockSpec((1, heads, 1, tok), lambda m: (m, 0, 0, 0))],
+        compiler_params=params(limit=40 * 1024 * 1024),
         cost_estimate=cost(4 * micro * heads * keys * tok * size, nbytes((own, other, bias))),
         name="attend",
-    )(ready, own, other, own, other, bias)
+    )(ready, own, other, bias)
 
 
 def attend_back(ready, own, other, bias, lse, grad, heads, kv_heads, size):
@@ -326,72 +332,67 @@
     scale = 1.0 / math.sqrt(size)
     mid = keys // 2
 
-    def kernel(q_ref, k0, k1, v0, v1, bias_ref, lse_ref, g_ref, gq, mine, theirs, gk, gv):
-        head = pl.program_id(1)
-        place = head % group
-        key = jnp.concatenate([r[...].reshape(outer * tok, size) for r in (k0, k1)], axis=0)
-        value = jnp.concatenate([r[...].reshape(outer * tok, size) for r in (v0, v1)], axis=0)
-        query, out_grad = q_ref[...], g_ref[...]
-        scores = dot_bt(key, query) * scale + bias_ref[0]
-        probs = jnp.exp(scores - lse_ref[0, 0])
-        back = dot_bt(value, out_grad)
-        centre = jnp.sum(probs * back, axis=0, keepdims=True)
-        slope = (probs * (back - centre)).astype(BF16)
-        gq[...] = dot_at(slope, key) * scale
-        key_part = dot(slope, query) * scale
-        value_part = dot(probs.astype(BF16), out_grad)
-
-        @pl.when(place == 0)
-        def _():
-            gk[...] = key_part
-            gv[...] = value_part
-
-        @pl.when(place > 0)
-        def _():
-            gk[...] += key_part
-            gv[...] += value_part
-
-        for g in range(kv_heads):
-
-            @pl.when(head == (g + 1) * group - 1)
-            def _(g=g):
+    def kernel(q_ref, own_ref, other_ref, bias_ref, lse_ref, g_ref, gq, mine, theirs, gk, gv):
+        for h in range(heads):
+            key, value = (
+                jnp.concatenate(
+                    [
+                        ref[:, :, i * size : (i + 1) * size].reshape(outer * tok, size)
+                        for ref in (own_ref, other_ref)
+                    ],
+                    axis=0,
+                )
+                for i in (h // group, kv_heads + h // group)
+            )
+            cut = slice(h * size, (h + 1) * size)
+            query, out_grad = q_ref[:, cut], g_ref[:, cut]
+            scores = dot_bt(key, query) * scale + bias_ref[0]
+            probs = jnp.exp(scores - lse_ref[0, h])
+            back = dot_bt(value, out_grad)
+            centre = jnp.sum(probs * back, axis=0, keepdims=True)
+            slope = (probs * (back - centre)).astype(BF16)
+            gq[:, cut] = dot_at(slope, key) * scale
+            key_part = dot(slope, query) * scale
+            value_part = dot(probs.astype(BF16), out_grad)
+            if h % group == 0:
+                gk[...] = key_part
+                gv[...] = value_part
+            else:
+                gk[...] += key_part
+                gv[...] += value_part
+            if h % group == group - 1:
                 for i, ref in enumerate((gk, gv)):
-                    at = (i * kv_heads + g) * size
+                    at = (i * kv_heads + h // group) * size
                     cut = slice(at, at + size)
                     mine[:, :, cut] = ref[:mid].reshape(outer, tok, size)
                     theirs[:, :, cut] = ref[mid:].reshape(outer, tok, size).astype(BF16)
 
-    def kv_spec(start):
-        return pl.BlockSpec((outer, tok, size), lambda m, h: (0, m, start + h // group))
-
-    head_spec = pl.BlockSpec((tok, size), lambda m, h: (m, h))
+    kv_spec = pl.BlockSpec((outer, tok, own.shape[2]), lambda m: (0, m, 0))
+    head_spec = pl.BlockSpec((tok, heads * size), lambda m: (m, 0))
     kv_shape = (outer, micro * tok, 2 * kv_heads * size)
     outs = (
         struct((micro * tok, heads * size), F32),
         struct(kv_shape, F32),
         struct(kv_shape, BF16),
     )
-    out_spec = pl.BlockSpec((outer, tok, kv_shape[2]), lambda m, h: (0, m, 0))
     return pl.pallas_call(
         kernel,
         out_shape=outs,
-        grid=(micro, heads),
+        grid=(micro,),
         in_specs=[
             head_spec,
-            kv_spec(0),
-            kv_spec(0),
-            kv_spec(kv_heads),
-            kv_spec(kv_heads),
-            pl.BlockSpec((1, keys, tok), lambda m, h: (m, 0, 0)),
-            pl.BlockSpec((1, 1, 1, tok), lambda m, h: (m, h, 0, 0)),
+            kv_spec,
+            kv_spec,
+            pl.BlockSpec((1, keys, tok), lambda m: (m, 0, 0)),
+            pl.BlockSpec((1, heads, 1, tok), lambda m: (m, 0, 0, 0)),
             head_spec,
         ],
-        out_specs=[head_spec, out_spec, out_spec],
+        out_specs=[head_spec, kv_spec, kv_spec],
         scratch_shapes=[pltpu.VMEM((keys, size), F32)] * 2,
-        compiler_params=params(2),
+        compiler_params=params(),
         cost_estimate=cost(10 * micro * heads * keys * tok * size, nbytes((own, other, bias))),
         name="attend_back",
-    )(ready, own, other, own, other, bias, lse, grad)
+    )(ready, own, other, bias, lse, grad)
 
 
 def sum_cores(mine, theirs):
@@ -435,7 +436,7 @@
         out_specs=[whole(o.shape) for o in outs],
         scratch_shapes=[full_weight(pair, n), weight_sems(pair)],
         grid=(1,),
-        compiler_params=params(),
+        compiler_params=params(limit=40 * 1024 * 1024),
         cost_estimate=cost(2 * tokens * n * part * parts, nbytes(ins)),
         name="expand",
     )(at, *ins)
@@ -444,16 +445,17 @@
 def contract(at, pieces, pair, n):
     parts = len(pieces)
     tokens, part = pieces[0].shape
-    outs = struct((tokens, n), BF16)
+    outs = (struct((tokens, n), BF16), struct((tokens, part * parts), BF16))
 
     def kernel(at_ref, *refs):
         ins, refs = refs[:parts], refs[parts:]
-        weights, (out, full, sems) = taken(refs, pair)
+        weights, (out, joined, full, sems) = taken(refs, pair)
         for copy in weight_copies(at_ref, [weights], [full], sems, parts):
             copy.start()
         total = 0.0
         for k, ref in enumerate(ins):
             weight_wait([weights], [full], sems, parts, k)
+            joined[:, k * part : (k + 1) * part] = ref[...]
             total = total + dot(ref[...], full[k * part : (k + 1) * part])
         out[...] = total.astype(BF16)
 
@@ -462,7 +464,7 @@
         kernel,
         out_shape=outs,
         in_specs=[SMEM] + [whole(a.shape) for a in pieces] + [ANY] * len(flat_pair(pair)),
-        out_specs=whole(outs.shape),
+        out_specs=[whole(o.shape) for o in outs],
         scratch_shapes=[full_weight(pair, n), weight_sems(pair)],
         grid=(1,),
         compiler_params=params(),
@@ -502,6 +504,7 @@
     tok, width = tokens_in[0].shape
     hidden = flat_pair(pair)[0].shape[-1] // 3
     part = width // parts
+    lo_count = parts if by_part else 1
 
     def kernel(at_ref, s_ref, *refs):
         x_refs, refs = refs[:count], refs[count:]
@@ -510,7 +513,8 @@
         routers, refs = taken(refs, router)
         weighted, d_high, logit, *refs = refs
         dxs, refs = refs[:count], refs[count:]
-        los, (full, r_ref, x_now, g_now, sems, x_sems) = refs[:count], refs[count:]
+        los, refs = refs[: count * lo_count], refs[count * lo_count :]
+        full, r_ref, x_now, g_now, sems, x_sems = refs
         pairs, fulls = [weights, routers], [full, r_ref]
         high, low = slice(0, 2 * hidden), slice(2 * hidden, 3 * hidden)
         step = pl.program_id(0)
@@ -580,17 +584,16 @@
             @pl.when(step == i)
             def _(i=i, ref=ref):
                 ref[...] = dx.astype(BF16)
-                for k in range(parts if by_part else 0):
-                    los[i][at_ref[4] ^ k] = total[:, k * part : (k + 1) * part].astype(BF16)
-                if not by_part:
-                    los[i][...] = total.astype(BF16)
+                n = width // lo_count
+                for k, lo in enumerate(los[i * lo_count : (i + 1) * lo_count]):
+                    lo[...] = total[:, k * n : (k + 1) * n].astype(BF16)
 
     def rows(n):
         return pl.BlockSpec((tok, n), lambda i, at_ref: (i, 0))
 
     outs = [struct((count * tok, n), BF16) for n in (hidden, 2 * hidden, LANES)]
     outs += [struct((tok, width), BF16)] * count
-    outs += [struct((parts, tok, part) if by_part else (tok, width), BF16)] * count
+    outs += [struct((tok, width // lo_count), BF16)] * (count * lo_count)
     all_weights = flat_pair(pair) + flat_pair(router)
     ins = (spread, *tokens_in, *grads, *all_weights)
     weighted, d_high, logit, *rest = pl.pallas_call(
@@ -611,11 +614,14 @@
                 pltpu.SemaphoreType.DMA((2, 2)),
             ],
         ),
-        compiler_params=params(),
+        compiler_params=params(limit=40 * 1024 * 1024),
         cost_estimate=cost(12 * count * tok * width * hidden, nbytes([*all_weights, *outs])),
         name="run_experts",
     )(at, *ins)
-    return weighted, d_high, logit, rest[:count], rest[count:]
+    dx, los = rest[:count], rest[count:]
+    if by_part:
+        los = [los[i * parts : (i + 1) * parts] for i in range(count)]
+    return weighted, d_high, logit, dx, los
 
 
 def weight_grads(at, place, outer_at, half_at, lefts, rights, parts, blocks, part, add=None, by_device=False, joined=False):
@@ -723,7 +729,7 @@
                 for stack in joins
             ],
         ),
-        compiler_params=params(),
+        compiler_params=params(limit=40 * 1024 * 1024),
         cost_estimate=cost(2 * tokens * blocks * unit * n, nbytes(ins)),
         name="weight_grads",
     )(at, *ins)
@@ -1048,9 +1054,6 @@
     def exchange(a):
         return lax.all_to_all(a, "outer", 0, 0, tiled=True)
 
-    def col_exchange(a):
-        return lax.all_to_all(a, "col", 0, 0, tiled=True)
-
     def for_all(a):
         return jnp.broadcast_to(a[None], (outer,) + a.shape)
 
@@ -1167,7 +1170,7 @@
     for j, a in zip(far, far_grads):
         grads[j] = jnp.concatenate(col_gather(a[:, :part]) + [a[:, part:]], axis=1)
 
-    results, dx, lo = [], [None] * outer, [None] * outer
+    results, dx, lo_far = [], [None] * outer, []
     order = [0] + far + near
     for group in [[0]] + [far[i : i + 4] for i in range(0, len(far), 4)] + [near]:
         *result, dx_now, lo_now = run_experts(
@@ -1179,35 +1182,35 @@
             w_back,
             heads * size,
             cols,
-            group != near,
+            group[0] in far,
         )
-        for j, a, b in zip(group, dx_now, lo_now):
-            dx[j], lo[j] = a, b
+        for j, a in zip(group, dx_now):
+            dx[j] = a
         if group == [0]:
-            expert_in, lo[0] = both(expert_in, lo[0])
+            lo_own = lo_now[0]
+            expert_in, lo_own = both(expert_in, lo_own)
         elif group != near:
+            lo_far += lo_now
             for j in group:
                 dx[j] = swap(dx[j], j)
-            if group[-1] == far[-1]:
-                lo_sums = col_exchange(jnp.concatenate([lo[j] for j in [0] + far], axis=1))
+        else:
+            lo_near = lo_now
         results.append(result)
-    far_dx, results[-1] = both([dx[j] for j in far], results[-1])
+    far_dx, results[-1], lo_far = both([dx[j] for j in far], results[-1], lo_far)
+    lo_far = [col_total([a[0].astype(F32), *a[1:]]).astype(BF16) for a in lo_far]
     weighted, d_high, logit_low = [list(arrays) for arrays in zip(*results)]
-    for j in near:
-        dx[j] = swap(dx[j], j)
+    near_dx, far_dx = both([dx[j] for j in near], far_dx)
+    for j, a in zip(near, near_dx):
+        dx[j] = swap(a, j)
     sizes = (cols, outer, part)
     expert_sides = (
         [[expert_in[j] for j in order], [grads[j] for j in order]],
         [[d_high, logit_low], [weighted]],
     )
     (other,) = weight_grads(at, place, outer_at, 1, *expert_sides, *sizes, joined=True)
-    other, near_dx, lo_sums = both(other, [dx[j] for j in near], lo_sums)
-    lo_sums = jnp.sum(lo_sums.astype(F32), axis=0)
-    lo[0] = lo_sums[:tokens]
-    lo_far = [lo_sums[i * tokens : (i + 1) * tokens].astype(BF16) for i in range(1, len(far) + 1)]
+    other, near_dx, lo_far, lo_near = both(other, [dx[j] for j in near], lo_far, lo_near)
     other = core_swap(other)
     *spread_two, gain_grad_two = second_norm_back([dx[0]] + near_dx + far_dx, full_res, gain_two)
-    lo_near, _ = both([lo[j] for j in near], spread_two)
     lo_near = [swap(a, j) for j, a in zip(near, lo_near)]
     (expert_grads,) = weight_grads(
         at, place, outer_at, 0, *expert_sides, *sizes, [other], True, True
@@ -1218,30 +1221,29 @@
     expert_grads = exchange(expert_grads)
     grad_feats = col_gather(grad_residual.astype(BF16))
 
-    lo_near = sum(a.astype(F32) for a in lo_near)
+    lo_near = lo_own.astype(F32) + sum(a.astype(F32) for a in lo_near)
     lo_near = [
         lo_near[:, k * part : (k + 1) * part].astype(F32 if k == 0 else BF16) for k in range(cols)
     ]
     grad_feats, lo_near = both(grad_feats, lo_near)
-    back_attended = contract(at, grad_feats, w_back, heads * size)
+    back_attended, feats = contract(at, grad_feats, w_back, heads * size)
     lo_near = col_total(after(lo_near, back_attended))
     grad_q, kv_mine, kv_theirs = attend_back(
         ready, kv_own, kv_other, bias, lse, back_attended, heads, kv_heads, size
     )
-    kv_theirs, expert_grads, lo_near = both(kv_theirs, expert_grads, lo_near)
+    kv_theirs, expert_grads = both(kv_theirs, expert_grads)
     kv_sums = sum_cores(kv_mine, core_swap(kv_theirs))
     grad_kv = scatter(kv_sums)
     router_part = jnp.sum(
         expert_grads[:, :, 2 * hidden : 2 * hidden + LANES].astype(F32), axis=0
     )
-    feats, lo_far, _ = both(grad_feats, lo_far, kv_sums)
+    feats, lo_near, _ = both(feats, lo_near, grad_q)
+    (other,) = weight_grads(at, place, outer_at, 1, [[feats]], [[[attended]]], *sizes)
+    (out_grads,) = weight_grads(
+        at, place, outer_at, 0, [[feats]], [[[attended]]], *sizes, [core_swap(other)], True
+    )
+    grad_kv, out_grads, lo_far = both(grad_kv, out_grads, lo_far)
     lo_far = [swap(a, j) for j, a in zip(far, lo_far)]
-    feats = [jnp.concatenate(feats, axis=1)]
-    (other,) = weight_grads(at, place, outer_at, 1, [feats], [[[attended]]], *sizes)
-    (out_grads,) = weight_grads(
-        at, place, outer_at, 0, [feats], [[[attended]]], *sizes, [core_swap(other)], True
-    )
-    grad_kv, out_grads = both(grad_kv, out_grads)
     out_grads = exchange(out_grads)
     *spread_one, d_wide, sums = project_back(
         at,
@@ -1273,7 +1275,7 @@
     wide_grads = exchange(wide_grads)
 
     got = [col_swap(spread_one[k], k) for k in range(1, cols)]
-    layer_out = residual + lo[0] + lo_near + sum(a.astype(F32) for a in lo_far)
+    layer_out = residual + lo_near + sum(a.astype(F32) for a in lo_far)
     layer_out = from_halves(layer_out.astype(BF16)).reshape(micro, tok, part)
     input_grad, sums, grad_router = finish(
         at, grad_residual, spread_one[0], got, sums, low, unit, experts
@@ -1282,24 +1284,31 @@
     sums = sums + core_swap(sums)
     sums = sum(gather(sums))
     (grad_out_w,) = sum_blocks([out_grads] * outer, [heads * size])
-    wide_grads, input_grad, layer_out, grad_out_w, sums, grad_router = both(
-        wide_grads, input_grad, layer_out, grad_out_w, sums, grad_router
-    )
     head_sums = sums[2 * cols, : 2 * size]
+    gain_sums = (
+        sums[:cols].reshape(width),
+        sums[cols : 2 * cols].reshape(width),
+        head_sums[:size],
+        head_sums[size:],
+    )
+    wide_grads, input_grad, layer_out, grad_out_w, gain_sums, grad_router = both(
+        wide_grads, input_grad, layer_out, grad_out_w, gain_sums, grad_router
+    )
+    grad_norm_gain, grad_ffn_gain, grad_query_gain, grad_key_gain = gain_sums
     grad_query_w, grad_key_w, grad_value_w = sum_blocks(
         [wide_grads] * outer, [w.shape[1] for w in (w_query, w_key, w_value)]
     )
     return (
         layer_out,
         input_grad,
-        sums[:cols].reshape(width),
+        grad_norm_gain,
         grad_query_w,
         grad_key_w,
         grad_value_w,
-        head_sums[:size],
-        head_sums[size:],
+        grad_query_gain,
+        grad_key_gain,
         grad_out_w,
-        sums[cols : 2 * cols].reshape(width),
+        grad_ffn_gain,
         grad_router,
         grad_gate_w,
         grad_up_w,

time: 524 us -> 500 us (0.954)
  the two profiles are of different devices: /device:TPU:10 before, /device:TPU:0 now
where the time goes in v3:
time: 500 us; the launch traced here: 490 us
  waiting for transfers between devices  180 us (36%)
  Pallas kernels  156 us (31%)
  starting transfers between devices  107 us (21%)
  local copies, waits for them, and re-layouts  27.7 us (6%)
  other arithmetic  17 us (3%)
    ppermute x30, waiting for transfers between devices, col_swap(): return lax.ppermute(a, 'col', [(i, i ^ mask) for i in range(cols)])  118 us
    ppermute x30, starting transfers between devices, col_swap(): return lax.ppermute(a, 'col', [(i, i ^ mask) for i in range(cols)])  51.4 us
    ppermute x24, waiting for transfers between devices, swap(): return lax.ppermute(a, 'outer', [(i, i ^ mask) for i in range(outer)])  50.8 us
    pallas_call x3, Pallas kernels, run_experts(): pl.pallas_call(kernel, out_shape=outs, grid_spec=pltpu.PrefetchScalarGrid...  45.8 us
    pallas_call x6, Pallas kernels, weight_grads(): pl.pallas_call(kernel, out_shape=outs, grid_spec=pltpu.PrefetchScalarGrid...  34.7 us
    ppermute x24, starting transfers between devices, swap(): return lax.ppermute(a, 'outer', [(i, i ^ mask) for i in range(outer)])  29.9 us
    all_to_all x5, starting transfers between devices, exchange(): return lax.all_to_all(a, 'outer', 0, 0, tiled=True)  22.7 us
    unnamed x192, local copies, waits for them, and re-layouts  18.8 us
  transfers between devices with their start and end apart: 74, of which 30 were waited for; matrix products, arithmetic and copies ran while one was open for 5% of the time, Pallas kernels for 28%

profile of v3, /device:TPU:0, one launch (start us, length us, event | category | flops | bytes accessed | tf_op | source)
XLA Modules:
  0.0 489.9 jit_solution(270827819946194925)
XLA Ops:
  48.5 6.7 %project.1 = (bf16[256,2048]{1,0:T(8,128)(2,1)}, f32[256,1280]{1,0:T(8,128)}, bf16[256,1024]{1,0:T(8,128)(2,1)}, bf16[256,256]{1,0:T(8,128)(2,1)}) custom-call(s32[5]{0:T(128)} %stack.62.at_ref, bf16[256,512]{1,0:T(8,128)(2,1)} %pad_maximum_fusion.3.refs_0_.refs_5_, bf16[256,512]{1,0:T(8,128)(2,1)} %copy-done.70, ...), custom_call_target="tpu_custom_call" | custom-call | flops 7031249920 | tf_op jit(solution)/shard_map/project/pallas_call | solution.py:265
  58.8 18.7 %collective-permute-done.12 = bf16[256,256]{1,0:T(8,128)(2,1)S(1)} collective-permute-done((bf16[256,256]{1,0:T(8,128)(2,1)}, bf16[256,256]{1,0:T(8,128)(2,1)S(1)}, u32[]{:S(2)}, u32[]{:S(2)}) %collective-permute-start.12) | collective-permute-done | bytes 131104 | tf_op jit(solution)/shard_map/ppermute | solution.py:1097
  92.6 5.6 %attend.1 = (bf16[256,1024]{1,0:T(8,128)(2,1)S(1)}, f32[2,8,1,128]{3,2,1,0:T(1,128)S(1)}) custom-call(bf16[256,1024]{1,0:T(8,128)(2,1)S(1)} %copy-done.21, bf16[4,256,256]{2,1,0:T(8,128)(2,1)S(1)} %pad_maximum_fusion.1.own_ref, bf16[4,256,256]{2,1,0:T(8,128)(2,1)S(1)} %collective-permute-done.14.other_ref, f32[2,1024,128]{2,1,0:T(8,128)S(1)} %copy-done.9), custom_call_target="tpu_custom_call" | custom-call | flops 16777216 | bytes 32768 | tf_op jit(solution)/shard_map/attend/pallas_call | solution.py:311
  102.0 10.9 %collective-permute-done.17 = bf16[256,512]{1,0:T(8,128)(2,1)S(1)} collective-permute-done((bf16[256,512]{1,0:T(8,128)(2,1)S(1)}, bf16[256,512]{1,0:T(8,128)(2,1)S(1)}, u32[]{:S(2)}, u32[]{:S(2)}) %collective-permute-start.17) | collective-permute-done | bytes 262176 | tf_op jit(solution)/shard_map/ppermute | solution.py:1052
  121.0 8.1 %collective-permute-done.19 = bf16[256,512]{1,0:T(8,128)(2,1)S(1)} collective-permute-done((bf16[256,512]{1,0:T(8,128)(2,1)S(1)}, bf16[256,512]{1,0:T(8,128)(2,1)S(1)}, u32[]{:S(2)}, u32[]{:S(2)}) %collective-permute-start.19) | collective-permute-done | bytes 262176 | tf_op jit(solution)/shard_map/ppermute | solution.py:1052
  129.0 9.1 %collective-permute-done.20 = bf16[256,512]{1,0:T(8,128)(2,1)S(1)} collective-permute-done((bf16[256,512]{1,0:T(8,128)(2,1)S(1)}, bf16[256,512]{1,0:T(8,128)(2,1)S(1)}, u32[]{:S(2)}, u32[]{:S(2)}) %collective-permute-start.20) | collective-permute-done | bytes 262176 | tf_op jit(solution)/shard_map/ppermute | solution.py:1052
  146.5 16.5 %collective-permute-done.26.refs_3_.refs_7_ = bf16[256,2176]{1,0:T(8,128)(2,1)} collective-permute-done((bf16[256,2176]{1,0:T(8,128)(2,1)S(1)}, bf16[256,2176]{1,0:T(8,128)(2,1)}, u32[]{:S(2)}, u32[]{:S(2)}) %collective-permute-start.26) | collective-permute-done | bytes 1114144 | tf_op jit(solution)/shard_map/ppermute | solution.py:1097
  174.8 10.2 %collective-permute-done.32 = bf16[256,512]{1,0:T(8,128)(2,1)S(1)} collective-permute-done((bf16[256,512]{1,0:T(8,128)(2,1)S(1)}, bf16[256,512]{1,0:T(8,128)(2,1)S(1)}, u32[]{:S(2)}, u32[]{:S(2)}) %collective-permute-start.32) | collective-permute-done | bytes 262176 | tf_op jit(solution)/shard_map/ppermute | solution.py:1052
  185.0 8.2 %collective-permute-done.31 = bf16[256,512]{1,0:T(8,128)(2,1)S(1)} collective-permute-done((bf16[256,512]{1,0:T(8,128)(2,1)S(1)}, bf16[256,512]{1,0:T(8,128)(2,1)S(1)}, u32[]{:S(2)}, u32[]{:S(2)}) %collective-permute-start.31) | collective-permute-done | bytes 262176 | tf_op jit(solution)/shard_map/ppermute | solution.py:1052
  195.4 7.0 %collective-permute-done.33 = bf16[256,512]{1,0:T(8,128)(2,1)S(1)} collective-permute-done((bf16[256,512]{1,0:T(8,128)(2,1)S(1)}, bf16[256,512]{1,0:T(8,128)(2,1)S(1)}, u32[]{:S(2)}, u32[]{:S(2)}) %collective-permute-start.33) | collective-permute-done | bytes 262176 | tf_op jit(solution)/shard_map/ppermute | solution.py:1052
  203.4 12.0 %run_experts.3 = (bf16[256,768]{1,0:T(8,128)(2,1)S(1)}, bf16[256,1536]{1,0:T(8,128)(2,1)S(1)}, bf16[256,128]{1,0:T(8,128)(2,1)S(1)}, bf16[256,2048]{1,0:T(8,128)(2,1)S(1)}, bf16[256,2048]{1,0:T(8,128)(2,1)S(1)}) custom-call(s32[5]{0:T(128)S(1)} %copy-done.35, bf16[128,768]{1,0:T(8,128)(2,1)S(1)} %copy-done.23, bf16[256,2048]{1,0:T(8,128)(2,1)S(1)} %copy-done.1, ...), custom_call_target="tpu_custom_call" | custom-call | flops 75497472 | bytes 273408 | tf_op jit(solution)/shard_map/run_experts/pallas_call | solution.py:599
  220.0 12.8 %run_experts.4 = (bf16[256,768]{1,0:T(8,128)(2,1)S(1)}, bf16[256,1536]{1,0:T(8,128)(2,1)S(1)}, bf16[256,128]{1,0:T(8,128)(2,1)S(1)}, bf16[256,2048]{1,0:T(8,128)...) custom-call(s32[5]{0:T(128)S(1)} %copy-done.35, ...), custom_call_target="tpu_custom_call" | custom-call | flops 75497472 | bytes 273408 | tf_op jit(solution)/shard_map/run_experts/pallas_call | solution.py:599
  234.4 21.0 %run_experts.5 = (bf16[512,768]{1,0:T(8,128)(2,1)S(1)}, bf16[512,1536]{1,0:T(8,128)(2,1)S(1)}, bf16[512,128]{1,0:T(8,128)(2,1)S(1)}, bf16[256,2048]{1,0:T(8,128)...) custom-call(s32[5]{0:T(128)S(1)} %copy-done.35, ...), custom_call_target="tpu_custom_call" | custom-call | flops 150994944 | bytes 325632 | tf_op jit(solution)/shard_map/run_experts/pallas_call | solution.py:599
  265.5 10.1 %weight_grads.6 = bf16[4,256,2432]{2,1,0:T(8,128)(2,1)} custom-call(s32[5]{0:T(128)S(1)} %copy-done.35, bf16[256,2048]{1,0:T(8,128)(2,1)S(1)} %copy-done.1, bf16[256,2048]{1,0:T(8,128)(2,1)S(1)} %collective-permute-done.30.refs_0_.refs_1_, bf16[256,2048]{1,0:T(8,128)(2,1)S(1)} %collective-permute-done.28.refs_0_.refs_2_, ...), custom_call_target="tpu_custom_call" | custom-call | flops 79691776 | bytes 212992 | tf_op jit(solution)/shard_map/weight_grads/pallas_call | solution.py:712
  275.6 8.7 %collective-permute-done.38 = bf16[256,512]{1,0:T(8,128)(2,1)S(1)} collective-permute-done((bf16[256,512]{1,0:T(8,128)(2,1)S(1)}, bf16[256,512]{1,0:T(8,128)(2,1)S(1)}, u32[]{:S(2)}, u32[]{:S(2)}) %collective-permute-start.38) | collective-permute-done | bytes 262176 | tf_op jit(solution)/shard_map/ppermute | solution.py:1052
  303.7 10.8 %weight_grads.7 = bf16[4,256,2432]{2,1,0:T(8,128)(2,1)} custom-call(s32[5]{0:T(128)S(1)} %copy-done.35, bf16[256,2048]{1,0:T(8,128)(2,1)S(1)} %copy-done.1, bf16[256,2048]{1,0:T(8,128)(2,1)S(1)} %collective-permute-done.30.refs_0_.refs_1_, bf16[256,2048]{1,0:T(8,128)(2,1)S(1)} %copy-done.3, bf16[256,2048]{1,0:T(8,128)(2,1)S(1)} %collective-permute-done.29.refs_1_.refs_3_, ...), custom_call_target="tpu_custom_call" | custom-call | flops 79691776 | bytes 290816 | tf_op jit(solution)/shard_map/weight_grads/pallas_call | solution.py:712
  331.9 16.1 %collective-permute-done.47.refs_2_ = bf16[256,512]{1,0:T(8,128)(2,1)S(1)} collective-permute-done((bf16[256,512]{1,0:T(8,128)(2,1)S(1)}, bf16[256,512]{1,0:T(8,128)(2,1)S(1)}, u32[]{:S(2)}, u32[]{:S(2)}) %collective-permute-start.47) | collective-permute-done | bytes 262176 | tf_op jit(solution)/shard_map/ppermute | solution.py:1052
  348.9 5.6 %contract.1 = (bf16[256,1024]{1,0:T(8,128)(2,1)}, bf16[256,2048]{1,0:T(8,128)(2,1)}) custom-call(s32[5]{0:T(128)} %stack.62.at_ref, bf16[256,512]{1,0:T(8,128)(2,1)} %copy-done.55, bf16[256,512]{1,0:T(8,128)(2,1)} %copy-done.74, bf16[256,512]{1,0:T(8,128)(2,1)} %copy-done.73, bf16[256,512]{1,0:T(8,128)(2,1)} %copy-done.72, bf16[4,256,1152]{2,1,0:T(8,128)(2,1)} %copy-done, ...), custom_call_target="tpu_custom_call" | custom-call | flops 16777216 | bytes 90112 | tf_op jit(solution)/shard_map/contract/pallas_call | solution.py:463
  358.9 11.8 %attend_back.1 = (f32[256,1024]{1,0:T(8,128)}, f32[4,256,256]{2,1,0:T(8,128)}, bf16[4,256,256]{2,1,0:T(8,128)(2,1)}) custom-call(bf16[256,1024]{1,0:T(8,128)(2,1)} %get-tuple-element.213.q_ref, bf16[4,256,256]{2,1,0:T(8,128)(2,1)} %copy-done.6, bf16[4,256,256]{2,1,0:T(8,128)(2,1)} %copy-done.22, f32[2,1024,128]{2,1,0:T(8,128)} %get-tuple-element.219.bias_ref, ...), custom_call_target="tpu_custom_call" | custom-call | flops 41943040 | bytes 32768 | tf_op jit(solution)/shard_map/attend_back/pallas_call | solution.py:378
  370.8 5.4 %collective-permute-done.54 = bf16[256,512]{1,0:T(8,128)(2,1)S(1)} collective-permute-done((bf16[256,512]{1,0:T(8,128)(2,1)S(1)}, bf16[256,512]{1,0:T(8,128)(2,1)S(1)}, u32[]{:S(2)}, u32[]{:S(2)}) %collective-permute-start.54) | collective-permute-done | bytes 262176 | tf_op jit(solution)/shard_map/ppermute | solution.py:1052
  406.2 9.6 %project_back.1 = (f32[256,512]{1,0:T(8,128)}, bf16[320,512]{1,0:T(8,128)(2,1)}, bf16[320,512]{1,0:T(8,128)(2,1)}, bf16[320,512]{1,0:T(8,128)(2,1)}, bf16[256,1280]{1,0:T(8,128)(2,1)}, /*index=5*/f32[32,512]{1,0:T(8,128)}) custom-call(s32[5]{0:T(128)} %stack.62.at_ref, f32[256,1280]{1,0:T(8,128)} %get-tuple-element.211.pre_ref, ...), custom_call_target="tpu_custom_call" | custom-call | flops 20971520 | bytes 149776 | tf_op jit(solution)/shard_map/project_back/pallas_call | solution.py:899
  420.4 6.4 %by_columns.1 = (f32[256,3072]{1,0:T(8,128)}, f32[256,3072]{1,0:T(8,128)}, f32[256,3072]{1,0:T(8,128)}) custom-call(bf16[4,256,2432]{2,1,0:T(8,128)(2,1)} %all-to-all-done.2.ref), custom_call_target="tpu_custom_call" | custom-call | bytes 225280 | tf_op jit(solution)/shard_map/by_columns/pallas_call | solution.py:779
  447.9 9.3 %collective-permute-done.62.refs_0_ = bf16[320,512]{1,0:T(8,128)(2,1)S(1)} collective-permute-done((bf16[320,512]{1,0:T(8,128)(2,1)}, bf16[320,512]{1,0:T(8,128)(2,1)S(1)}, u32[]{:S(2)}, u32[]{:S(2)}) %collective-permute-start.62) | collective-permute-done | bytes 327712 | tf_op jit(solution)/shard_map/ppermute | solution.py:1052
  457.3 12.8 %collective-permute-done.63.refs_1_ = bf16[320,512]{1,0:T(8,128)(2,1)S(1)} collective-permute-done((bf16[320,512]{1,0:T(8,128)(2,1)}, bf16[320,512]{1,0:T(8,128)(2,1)S(1)}, u32[]{:S(2)}, u32[]{:S(2)}) %collective-permute-start.63) | collective-permute-done | bytes 327712 | tf_op jit(solution)/shard_map/ppermute | solution.py:1052
  (383 shorter events, 234.3 us)
Async XLA Ops:
  4.4 25.4 %collective-permute-start.5 = (bf16[256,512]{1,0:T(8,128)(2,1)}, bf16[256,512]{1,0:T(8,128)(2,1)}, u32[]{:S(2)}, u32[]{:S(2)}) collective-permute-start(bf16[256,512]{1,0:T(8,128)(2,1)} %pad_maximum_fusion.3.refs_0_.refs_5_), channel_id=1, source_target_pairs={{0,3},{1,2},{2,1},{3,0},{4,7},{5,6},{6,5},{7,4},{8,11},{9,10},{10,... | collective-permute-start | bytes 786440 | tf_op jit(solution)/shard_map/ppermute | solution.py:1052
  9.6 28.0 %collective-permute-start.2 = (bf16[256,1280]{1,0:T(8,128)(2,1)S(1)}, bf16[256,1280]{1,0:T(8,128)(2,1)}, u32[]{:S(2)}, u32[]{:S(2)}) collective-permute-start(bf16[256,1280]{1,0:T(8,128)(2,1)S(1)} %constant_dynamic-update-slice_fusion.refs_4_.refs_9_), channel_id=1, source_target_pairs={{0,24},{8,16},{16,8},{24,0},{1,25},{9,17},{17,9},{25,1},{2,26},{10... | collective-permute-start | bytes 1966088 | tf_op jit(solution)/shard_map/ppermute | solution.py:1097
  12.1 30.4 %collective-permute-start.1 = (bf16[256,1280]{1,0:T(8,128)(2,1)S(1)}, bf16[256,1280]{1,0:T(8,128)(2,1)}, u32[]{:S(2)}, u32[]{:S(2)}) collective-permute-start(bf16[256,1280]{1,0:T(8,128)(2,1)S(1)} %constant_dynamic-update-slice_fusion.refs_4_.refs_9_), channel_id=1, source_target_pairs={{0,16},{8,24},{16,0},{24,8},{1,17},{9,25},{17,1},{25,9},{2,18},{10... | collective-permute-start | bytes 1966088 | tf_op jit(solution)/shard_map/ppermute | solution.py:1097
  12.6 29.9 %collective-permute-start = (bf16[256,1280]{1,0:T(8,128)(2,1)S(1)}, bf16[256,1280]{1,0:T(8,128)(2,1)}, u32[]{:S(2)}, u32[]{:S(2)}) collective-permute-start(bf16[256,1280]{1,0:T(8,128)(2,1)S(1)} %constant_dynamic-update-slice_fusion.refs_4_.refs_9_), channel_id=1, source_target_pairs={{0,8},{8,0},{16,24},{24,16},{1,9},{9,1},{17,25},{25,17},{2,10},{10... | collective-permute-start | bytes 1966088 | tf_op jit(solution)/shard_map/ppermute | solution.py:1097
  26.1 53.8 %all-to-all-start = ((bf16[4,256,1152]{2,1,0:T(8,128)(2,1)}), bf16[4,256,1152]{2,1,0:T(8,128)(2,1)S(1)}, u32[]{:S(2)}, u32[]{:S(2)}) async-start(bf16[4,256,1152]{2,1,0:T(8,128)(2,1)} %broadcast_in_dim.24), calls=%async_computation | async-start | bytes 4718592 | tf_op jit(solution)/shard_map/all_to_all | solution.py:1055
  44.4 35.5 %collective-permute-start.13 = (bf16[256,640]{1,0:T(8,128)(2,1)S(1)}, bf16[256,640]{1,0:T(8,128)(2,1)}, u32[]{:S(2)}, u32[]{:S(2)}) collective-permute-start(bf16[256,640]{1,0:T(8,128)(2,1)S(1)} %pad_maximum_fusion.2), channel_id=1, source_target_pairs={{0,24},{8,16},{16,8},{24,0},{1,25},{9,17},{17,9},{25,1},{2,26},{10... | collective-permute-start | bytes 983048 | tf_op jit(solution)/shard_map/ppermute | solution.py:1097
  80.0 59.7 %all-to-all-start.1 = ((bf16[4,256,2304]{2,1,0:T(8,128)(2,1)}), bf16[4,256,2304]{2,1,0:T(8,128)(2,1)}, u32[]{:S(2)}, u32[]{:S(2)}) async-start(bf16[4,256,2304]{2,1,0:T(8,128)(2,1)} %by_owner.1), calls=%async_computation.1 | async-start | bytes 9437184 | tf_op jit(solution)/shard_map/all_to_all | solution.py:1055
  88.4 24.5 %collective-permute-start.17 = (bf16[256,512]{1,0:T(8,128)(2,1)S(1)}, bf16[256,512]{1,0:T(8,128)(2,1)S(1)}, u32[]{:S(2)}, u32[]{:S(2)}) collective-permute-start(bf16[256,512]{1,0:T(8,128)(2,1)S(1)} %pad_maximum_fusion.4), channel_id=1, source_target_pairs={{0,2},{1,3},{2,0},{3,1},{4,6},{5,7},{6,4},{7,5},{8,10},{9,11},{10,... | collective-permute-start | bytes 786440 | tf_op jit(solution)/shard_map/ppermute | solution.py:1052
  113.0 50.0 %collective-permute-start.26 = (bf16[256,2176]{1,0:T(8,128)(2,1)S(1)}, bf16[256,2176]{1,0:T(8,128)(2,1)}, u32[]{:S(2)}, u32[]{:S(2)}) collective-permute-start(bf16[256,2176]{1,0:T(8,128)(2,1)S(1)} %constant_dynamic-update-slice_fusion.3.refs_1_.refs_4_), channel_id=1, source_target_pairs={{0,16},{8,24},{16,0},{24,8},{1,17},{9,25},{17,1},{25,9},{2,18},{10... | collective-permute-start | bytes 3342344 | tf_op jit(solution)/shard_map/ppermute | solution.py:1097
  115.1 47.9 %collective-permute-start.25 = (bf16[256,2176]{1,0:T(8,128)(2,1)S(1)}, bf16[256,2176]{1,0:T(8,128)(2,1)}, u32[]{:S(2)}, u32[]{:S(2)}) collective-permute-start(bf16[256,2176]{1,0:T(8,128)(2,1)S(1)} %constant_dynamic-update-slice_fusion.3.refs_1_.refs_4_), channel_id=1, source_target_pairs={{0,8},{8,0},{16,24},{24,16},{1,9},{9,1},{17,25},{25,17},{2,10},{10... | collective-permute-start | bytes 3342344 | tf_op jit(solution)/shard_map/ppermute | solution.py:1097
  166.7 36.7 %collective-permute-start.27 = (bf16[4,256,2304]{2,1,0:T(8,128)(2,1)}, bf16[4,256,2304]{2,1,0:T(8,128)(2,1)}, u32[]{:S(2)}, u32[]{:S(2)}) collective-permute-start(bf16[4,256,2304]{2,1,0:T(8,128)(2,1)} %all-to-all-done.1.refs_2_.refs_4_), channel_id=1, source_target_pairs={{0,4},{4,0},{1,5},{5,1},{2,6},{6,2},{3,7},{7,3},{8,12},{12,8},{9,1... | collective-permute-start | bytes 14155784 | tf_op jit(solution)/shard_map/ppermute | solution.py:1049
  171.2 45.1 %collective-permute-start.30 = (bf16[256,2048]{1,0:T(8,128)(2,1)}, bf16[256,2048]{1,0:T(8,128)(2,1)S(1)}, u32[]{:S(2)}, u32[]{:S(2)}) collective-permute-start(bf16[256,2048]{1,0:T(8,128)(2,1)} %second_norm.1.refs_0_), channel_id=1, source_target_pairs={{0,24},{8,16},{16,8},{24,0},{1,25},{9,17},{17,9},{25,1},{2,26},{10... | collective-permute-start | bytes 3145736 | tf_op jit(solution)/shard_map/ppermute | solution.py:1097
  172.8 47.2 %collective-permute-start.29 = (bf16[256,2048]{1,0:T(8,128)(2,1)}, bf16[256,2048]{1,0:T(8,128)(2,1)S(1)}, u32[]{:S(2)}, u32[]{:S(2)}) collective-permute-start(bf16[256,2048]{1,0:T(8,128)(2,1)} %second_norm.1.refs_0_), channel_id=1, source_target_pairs={{0,16},{8,24},{16,0},{24,8},{1,17},{9,25},{17,1},{25,9},{2,18},{10... | collective-permute-start | bytes 3145736 | tf_op jit(solution)/shard_map/ppermute | solution.py:1097
  174.2 45.8 %collective-permute-start.28 = (bf16[256,2048]{1,0:T(8,128)(2,1)}, bf16[256,2048]{1,0:T(8,128)(2,1)S(1)}, u32[]{:S(2)}, u32[]{:S(2)}) collective-permute-start(bf16[256,2048]{1,0:T(8,128)(2,1)} %second_norm.1.refs_0_), channel_id=1, source_target_pairs={{0,8},{8,0},{16,24},{24,16},{1,9},{9,1},{17,25},{25,17},{2,10},{10... | collective-permute-start | bytes 3145736 | tf_op jit(solution)/shard_map/ppermute | solution.py:1097
  232.8 26.2 %collective-permute-start.34 = (bf16[256,2048]{1,0:T(8,128)(2,1)}, bf16[256,2048]{1,0:T(8,128)(2,1)S(1)}, u32[]{:S(2)}, u32[]{:S(2)}) collective-permute-start(bf16[256,2048]{1,0:T(8,128)(2,1)} %get-tuple-element.257), channel_id=1, source_target_pairs={{0,24},{8,16},{16,8},{24,0},{1,25},{9,17},{17,9},{25,1},{2,26},{10... | collective-permute-start | bytes 3145736 | tf_op jit(solution)/shard_map/ppermute | solution.py:1097
  259.1 26.1 %collective-permute-start.35 = (bf16[256,2048]{1,0:T(8,128)(2,1)S(1)}, bf16[256,2048]{1,0:T(8,128)(2,1)S(1)}, u32[]{:S(2)}, u32[]{:S(2)}) collective-permute-start(bf16[256,2048]{1,0:T(8,128)(2,1)S(1)} %get-tuple-element.275), channel_id=1, source_target_pairs={{0,8},{8,0},{16,24},{24,16},{1,9},{9,1},{17,25},{25,17},{2,10},{10... | collective-permute-start | bytes 3145736 | tf_op jit(solution)/shard_map/ppermute | solution.py:1097
  260.5 24.6 %collective-permute-start.36 = (bf16[256,2048]{1,0:T(8,128)(2,1)S(1)}, bf16[256,2048]{1,0:T(8,128)(2,1)S(1)}, u32[]{:S(2)}, u32[]{:S(2)}) collective-permute-start(bf16[256,2048]{1,0:T(8,128)(2,1)S(1)} %get-tuple-element.276), channel_id=1, source_target_pairs={{0,16},{8,24},{16,0},{24,8},{1,17},{9,25},{17,1},{25,9},{2,18},{10... | collective-permute-start | bytes 3145736 | tf_op jit(solution)/shard_map/ppermute | solution.py:1097
  285.2 32.5 %collective-permute-start.44 = (bf16[256,2048]{1,0:T(8,128)(2,1)}, bf16[256,2048]{1,0:T(8,128)(2,1)}, u32[]{:S(2)}, u32[]{:S(2)}) collective-permute-start(bf16[256,2048]{1,0:T(8,128)(2,1)} %get-tuple-element.294), channel_id=1, source_target_pairs={{0,8},{8,0},{16,24},{24,16},{1,9},{9,1},{17,25},{25,17},{2,10},{10... | collective-permute-start | bytes 3145736 | tf_op jit(solution)/shard_map/ppermute | solution.py:1097
  286.8 30.9 %collective-permute-start.45 = (bf16[256,2048]{1,0:T(8,128)(2,1)}, bf16[256,2048]{1,0:T(8,128)(2,1)}, u32[]{:S(2)}, u32[]{:S(2)}) collective-permute-start(bf16[256,2048]{1,0:T(8,128)(2,1)} %get-tuple-element.295), channel_id=1, source_target_pairs={{0,16},{8,24},{16,0},{24,8},{1,17},{9,25},{17,1},{25,9},{2,18},{10... | collective-permute-start | bytes 3145736 | tf_op jit(solution)/shard_map/ppermute | solution.py:1097
  317.7 62.6 %all-to-all-start.2 = ((bf16[4,256,2432]{2,1,0:T(8,128)(2,1)}), bf16[4,256,2432]{2,1,0:T(8,128)(2,1)}, u32[]{:S(2)}, u32[]{:S(2)}) async-start(bf16[4,256,2432]{2,1,0:T(8,128)(2,1)} %weight_grads.7), calls=%async_computation.2 | async-start | bytes 9961472 | tf_op jit(solution)/shard_map/all_to_all | solution.py:1055
  401.4 29.0 %all-to-all-start.3 = ((bf16[4,256,1024]{2,1,0:T(8,128)(2,1)}), bf16[4,256,1024]{2,1,0:T(8,128)(2,1)}, u32[]{:S(2)}, u32[]{:S(2)}) async-start(bf16[4,256,1024]{2,1,0:T(8,128)(2,1)} %weight_grads.9), calls=%async_computation.3 | async-start | bytes 4194304 | tf_op jit(solution)/shard_map/all_to_all | solution.py:1055
  435.2 49.8 %all-to-all-start.4 = ((bf16[4,256,1280]{2,1,0:T(8,128)(2,1)}), bf16[4,256,1280]{2,1,0:T(8,128)(2,1)S(1)}, u32[]{:S(2)}, u32[]{:S(2)}) async-start(bf16[4,256,1280]{2,1,0:T(8,128)(2,1)} %weight_grads.11), calls=%async_computation.4 | async-start | bytes 5242880 | tf_op jit(solution)/shard_map/all_to_all | solution.py:1055
  444.3 25.8 %collective-permute-start.63 = (bf16[320,512]{1,0:T(8,128)(2,1)}, bf16[320,512]{1,0:T(8,128)(2,1)S(1)}, u32[]{:S(2)}, u32[]{:S(2)}) collective-permute-start(bf16[320,512]{1,0:T(8,128)(2,1)} %get-tuple-element.346), channel_id=1, source_target_pairs={{0,2},{1,3},{2,0},{3,1},{4,6},{5,7},{6,4},{7,5},{8,10},{9,11},{10,... | collective-permute-start | bytes 983048 | tf_op jit(solution)/shard_map/ppermute | solution.py:1052
  445.3 24.8 %collective-permute-start.64 = (bf16[320,512]{1,0:T(8,128)(2,1)}, bf16[320,512]{1,0:T(8,128)(2,1)S(1)}, u32[]{:S(2)}, u32[]{:S(2)}) collective-permute-start(bf16[320,512]{1,0:T(8,128)(2,1)} %get-tuple-element.347), channel_id=1, source_target_pairs={{0,3},{1,2},{2,1},{3,0},{4,7},{5,6},{6,5},{7,4},{8,11},{9,10},{10,... | collective-permute-start | bytes 983048 | tf_op jit(solution)/shard_map/ppermute | solution.py:1052
  (138 other events, 1937.0 us)

commit v4 on v3

--- a/solution.py
+++ b/solution.py
@@ -409,7 +409,7 @@
         grid=(1,),
         in_specs=[whole(mine.shape)] * 2,
         out_specs=[whole(o.shape) for o in outs],
-        compiler_params=params(),
+        compiler_params=params(limit=24 * 1024 * 1024),
         cost_estimate=cost(1, 1),
         name="sum_cores",
     )(mine, theirs)
@@ -493,7 +493,7 @@
         in_specs=[whole(a.shape) for a in pieces] + [whole(gain.shape)],
         out_specs=whole(out.shape),
         grid=(1,),
-        compiler_params=params(),
+        compiler_params=params(limit=24 * 1024 * 1024),
         cost_estimate=cost(tokens * width * 4, nbytes((*pieces, out))),
         name="second_norm",
     )(*pieces, gain)
@@ -614,7 +614,7 @@
                 pltpu.SemaphoreType.DMA((2, 2)),
             ],
         ),
-        compiler_params=params(limit=40 * 1024 * 1024),
+        compiler_params=params(limit=32 * 1024 * 1024),
         cost_estimate=cost(12 * count * tok * width * hidden, nbytes([*all_weights, *outs])),
         name="run_experts",
     )(at, *ins)
@@ -782,7 +782,7 @@
         grid=(blocks,),
         in_specs=[pl.BlockSpec((1, unit, n), lambda i: (i, 0, 0))],
         out_specs=[pl.BlockSpec((unit, hidden), lambda i: (0, i)) for _ in starts],
-        compiler_params=params(),
+        compiler_params=params(limit=24 * 1024 * 1024),
         cost_estimate=cost(0, nbytes([grads, *outs])),
         name="by_columns",
     )(grads)
@@ -825,7 +825,7 @@
         in_specs=[whole(a.shape) for a in ins],
         out_specs=[whole(o.shape) for o in outs],
         grid=(1,),
-        compiler_params=params(),
+        compiler_params=params(limit=24 * 1024 * 1024),
         cost_estimate=cost(tokens * width * 20, nbytes(ins)),
         name="second_norm_back",
     )(*ins)
@@ -842,7 +842,7 @@
     gain_lines = -(-(2 * parts + 1) // 16) * 16
     lines = gain_lines + -(-experts // 16) * 16
     router_rows = router.shape[0]
-    outs = [struct((tokens, part), F32)] + [struct((tokens + 2 * lines, part), BF16)] * (parts - 1)
+    outs = [struct((tokens, part), F32)] + [struct((tokens + lines, part), BF16)] * (parts - 1)
     outs += [struct((tokens, n), BF16), struct((lines, part), F32)]
 
     def kernel(at_ref, pre_ref, two_ref, router_ref, *refs):
@@ -890,9 +890,7 @@
             sums[2 * parts : 2 * parts + 1, i * size : (i + 1) * size] = total
         sums[gain_lines : gain_lines + experts, :router_rows] = router_ref[...].T[:experts]
         for out in outs[1:]:
-            one, two = two_parts(sums[...])
-            out[tokens : tokens + lines] = one
-            out[tokens + lines :] = two
+            out[tokens:] = sums[...].astype(BF16)
 
     ins = (pre, gain_grad_two, router, *grad_q, *grad_kv, *pieces, *flat_pair(pair))
     ins = (*ins, gain, query_gain, key_gain, cosine, sine)
@@ -938,7 +936,7 @@
         grid=(1,),
         in_specs=[spec(i, a) for i, a in enumerate(grads)],
         out_specs=[whole(o.shape) for o in outs],
-        compiler_params=params(),
+        compiler_params=params(limit=24 * 1024 * 1024),
         cost_estimate=cost(1, 1),
         name="sum_blocks",
     )(*grads)
@@ -969,8 +967,7 @@
         for ref in arrived:
             value = value + ref[:tokens].astype(F32)
         put(out, slice(0, tokens), value)
-        got = [ref[tokens : tokens + lines].astype(F32) for ref in arrived]
-        got = [a + ref[tokens + lines :].astype(F32) for a, ref in zip(got, arrived)]
+        got = [ref[tokens:].astype(F32) for ref in arrived]
         total = own_sums[...]
         for a in got:
             total = total + a
@@ -1000,7 +997,7 @@
         grid=(1,),
         in_specs=[SMEM] + [whole(a.shape) for a in ins],
         out_specs=[whole(o.shape) for o in outs],
-        compiler_params=params(),
+        compiler_params=params(limit=24 * 1024 * 1024),
         cost_estimate=cost(1, 1),
         name="finish",
     )(at, *ins)
@@ -1143,11 +1140,12 @@
     )
     near = [j for j in range(1, outer) if not j & (j - 1)]
     far = [j for j in range(1, outer) if j & (j - 1)]
-    far_grads, _ = both(jnp.concatenate([own_grad, chosen], axis=1), w_in[0])
+    far_grads, _ = both(jnp.concatenate([own_grad, chosen], axis=1), kv)
     far_grads = [swap(far_grads, j) for j in far]
     kv_own = jnp.stack(gather(kv))
-    kv_own, w_back, far_grads = both(kv_own, w_back, far_grads)
-    weights = exchange(after(weights, w_back))
+    kv_own, w_back = both(kv_own, w_back)
+    weights, far_grads, _ = both(weights, far_grads, w_back)
+    weights = exchange(weights)
     kv_other = core_swap(kv_own)
     w_back = both_cores(w_back)
     attended, lse = attend(ready, kv_own, kv_other, bias, heads, kv_heads, size)
@@ -1267,37 +1265,35 @@
     other, expert_grads, lo_far = both(other, expert_grads, lo_far)
     grad_gate_w, grad_up_w, grad_down_w = by_columns(expert_grads, hidden)
     other = jnp.stack([core_swap(other[j]) for j in range(outer)])
-    other, grad_gate_w, out_grads = both(other, grad_gate_w, out_grads)
+    other, grad_gate_w = both(other, grad_gate_w)
     (wide_grads,) = weight_grads(
         at, place, outer_at, 0, [[normed_one]], [[[d_wide]]], *sizes, [other], True
     )
-    spread_one, wide_grads = both(spread_one, wide_grads)
+    spread_one, wide_grads, out_grads = both(spread_one, wide_grads, out_grads)
     wide_grads = exchange(wide_grads)
 
     got = [col_swap(spread_one[k], k) for k in range(1, cols)]
     layer_out = residual + lo_near + sum(a.astype(F32) for a in lo_far)
     layer_out = from_halves(layer_out.astype(BF16)).reshape(micro, tok, part)
+    (grad_out_w,) = sum_blocks([out_grads] * outer, [heads * size])
+    got, grad_out_w, layer_out = both(got, grad_out_w, layer_out)
     input_grad, sums, grad_router = finish(
         at, grad_residual, spread_one[0], got, sums, low, unit, experts
     )
     input_grad = input_grad.reshape(micro, tok, part)
     sums = sums + core_swap(sums)
-    sums = sum(gather(sums))
-    (grad_out_w,) = sum_blocks([out_grads] * outer, [heads * size])
-    head_sums = sums[2 * cols, : 2 * size]
-    gain_sums = (
-        sums[:cols].reshape(width),
-        sums[cols : 2 * cols].reshape(width),
-        head_sums[:size],
-        head_sums[size:],
-    )
-    wide_grads, input_grad, layer_out, grad_out_w, gain_sums, grad_router = both(
-        wide_grads, input_grad, layer_out, grad_out_w, gain_sums, grad_router
-    )
-    grad_norm_gain, grad_ffn_gain, grad_query_gain, grad_key_gain = gain_sums
+    sums = gather(sums)
+    wide_grads, input_grad, layer_out, grad_out_w, grad_router = both(
+        wide_grads, input_grad, layer_out, grad_out_w, grad_router
+    )
     grad_query_w, grad_key_w, grad_value_w = sum_blocks(
         [wide_grads] * outer, [w.shape[1] for w in (w_query, w_key, w_value)]
     )
+    sums, _ = both(sums, grad_query_w)
+    sums = sum(sums)
+    head_sums = sums[2 * cols, : 2 * size]
+    grad_norm_gain, grad_ffn_gain = sums[:cols].reshape(width), sums[cols : 2 * cols].reshape(width)
+    grad_query_gain, grad_key_gain = head_sums[:size], head_sums[size:]
     return (
         layer_out,
         input_grad,

time: 500 us -> 477 us (0.954)
  Pallas kernels: 156 us -> 140 us
  waiting for transfers between devices: 180 us -> 170 us
    ppermute x24, waiting for transfers between devices: 50.8 us -> 44.4 us  [swap(): return lax.ppermute(a, 'outer', [(i, i ^ mask) for i in range(outer)])]
    unnamed x192 -> x154, local copies, waits for them, and re-layouts: 18.8 us -> 22.1 us
  transfers between devices with their start and end apart: 74 -> 74, of which waited for: 30 -> 34; matrix products, arithmetic and copies ran while one was open for 5% -> 5% of each run, Pallas kernels for 28% -> 27%
where the time goes in v4:
time: 477 us; the launch traced here: 468 us
  waiting for transfers between devices  170 us (36%)
  Pallas kernels  140 us (29%)
  starting transfers between devices  108 us (23%)
  local copies, waits for them, and re-layouts  32.5 us (7%)
  other arithmetic  16.4 us (3%)
    ppermute x30, waiting for transfers between devices, col_swap(): return lax.ppermute(a, 'col', [(i, i ^ mask) for i in range(cols)])  114 us
    ppermute x30, starting transfers between devices, col_swap(): return lax.ppermute(a, 'col', [(i, i ^ mask) for i in range(cols)])  55.2 us
    ppermute x24, waiting for transfers between devices, swap(): return lax.ppermute(a, 'outer', [(i, i ^ mask) for i in range(outer)])  44.4 us
    pallas_call x3, Pallas kernels, run_experts(): pl.pallas_call(kernel, out_shape=outs, grid_spec=pltpu.PrefetchScalarGrid...  43.3 us
    pallas_call x6, Pallas kernels, weight_grads(): pl.pallas_call(kernel, out_shape=outs, grid_spec=pltpu.PrefetchScalarGrid...  32.1 us
    ppermute x24, starting transfers between devices, swap(): return lax.ppermute(a, 'outer', [(i, i ^ mask) for i in range(outer)])  27.6 us
    unnamed x154, local copies, waits for them, and re-layouts  22.1 us
    all_to_all x5, starting transfers between devices, exchange(): return lax.all_to_all(a, 'outer', 0, 0, tiled=True)  21.9 us
  transfers between devices with their start and end apart: 74, of which 34 were waited for; matrix products, arithmetic and copies ran while one was open for 5% of the time, Pallas kernels for 27%

profile of v4, /device:TPU:0, one launch (start us, length us, event | category | flops | bytes accessed | tf_op | source)
XLA Modules:
  0.0 468.5 jit_solution(720405622771094010)
XLA Ops:
  48.5 6.7 %project.1 = (bf16[256,2048]{1,0:T(8,128)(2,1)}, f32[256,1280]{1,0:T(8,128)}, bf16[256,1024]{1,0:T(8,128)(2,1)}, bf16[256,256]{1,0:T(8,128)(2,1)}) custom-call(s32[5]{0:T(128)} %stack.62.at_ref, bf16[256,512]{1,0:T(8,128)(2,1)} %pad_maximum_fusion.3.refs_0_.refs_5_, bf16[256,512]{1,0:T(8,128)(2,1)} %copy-done.52, ...), custom_call_target="tpu_custom_call" | custom-call | flops 7031249920 | tf_op jit(solution)/shard_map/project/pallas_call | solution.py:265
  60.9 9.6 %collective-permute-done.12 = bf16[256,256]{1,0:T(8,128)(2,1)S(1)} collective-permute-done((bf16[256,256]{1,0:T(8,128)(2,1)}, bf16[256,256]{1,0:T(8,128)(2,1)S(1)}, u32[]{:S(2)}, u32[]{:S(2)}) %collective-permute-start.12) | collective-permute-done | bytes 131104 | tf_op jit(solution)/shard_map/ppermute | solution.py:1094
  91.1 5.9 %attend.1 = (bf16[256,1024]{1,0:T(8,128)(2,1)S(1)}, f32[2,8,1,128]{3,2,1,0:T(1,128)S(1)}) custom-call(bf16[256,1024]{1,0:T(8,128)(2,1)S(1)} %copy-done.14, bf16[4,256,256]{2,1,0:T(8,128)(2,1)S(1)} %pad_maximum_fusion.1.own_ref, bf16[4,256,256]{2,1,0:T(8,128)(2,1)S(1)} %collective-permute-done.13.other_ref, f32[2,1024,128]{2,1,0:T(8,128)S(1)} %copy-done.9), custom_call_target="tpu_custom_call" | custom-call | flops 16777216 | bytes 32768 | tf_op jit(solution)/shard_map/attend/pallas_call | solution.py:311
  100.8 10.9 %collective-permute-done.16 = bf16[256,512]{1,0:T(8,128)(2,1)S(1)} collective-permute-done((bf16[256,512]{1,0:T(8,128)(2,1)S(1)}, bf16[256,512]{1,0:T(8,128)(2,1)S(1)}, u32[]{:S(2)}, u32[]{:S(2)}) %collective-permute-start.16) | collective-permute-done | bytes 262176 | tf_op jit(solution)/shard_map/ppermute | solution.py:1049
  119.8 8.1 %collective-permute-done.18 = bf16[256,512]{1,0:T(8,128)(2,1)S(1)} collective-permute-done((bf16[256,512]{1,0:T(8,128)(2,1)S(1)}, bf16[256,512]{1,0:T(8,128)(2,1)S(1)}, u32[]{:S(2)}, u32[]{:S(2)}) %collective-permute-start.18) | collective-permute-done | bytes 262176 | tf_op jit(solution)/shard_map/ppermute | solution.py:1049
  127.9 9.0 %collective-permute-done.19 = bf16[256,512]{1,0:T(8,128)(2,1)S(1)} collective-permute-done((bf16[256,512]{1,0:T(8,128)(2,1)S(1)}, bf16[256,512]{1,0:T(8,128)(2,1)S(1)}, u32[]{:S(2)}, u32[]{:S(2)}) %collective-permute-start.19) | collective-permute-done | bytes 262176 | tf_op jit(solution)/shard_map/ppermute | solution.py:1049
  141.5 6.7 %collective-permute-start.23 = (bf16[256,512]{1,0:T(8,128)(2,1)S(1)}, bf16[256,512]{1,0:T(8,128)(2,1)S(1)}, u32[]{:S(2)}, u32[]{:S(2)}) collective-permute-start(bf16[256,512]{1,0:T(8,128)(2,1)S(1)} %convert_element_type.81.refs_0_.refs_4_), channel_id=1, source_target_pairs={{0,2},{1,3},{2,0},{3,1},{4,6},{5,7},{6,4},{7,5},{8,10},{9,11},{10,... | collective-permute-start | bytes 786440 | tf_op jit(solution)/shard_map/ppermute | solution.py:1049
  148.2 11.9 %collective-permute-done.26.refs_3_.refs_7_ = bf16[256,2176]{1,0:T(8,128)(2,1)} collective-permute-done((bf16[256,2176]{1,0:T(8,128)(2,1)S(1)}, bf16[256,2176]{1,0:T(8,128)(2,1)}, u32[]{:S(2)}, u32[]{:S(2)}) %collective-permute-start.26) | collective-permute-done | bytes 1114144 | tf_op jit(solution)/shard_map/ppermute | solution.py:1094
  169.6 11.0 %collective-permute-done.32 = bf16[256,512]{1,0:T(8,128)(2,1)S(1)} collective-permute-done((bf16[256,512]{1,0:T(8,128)(2,1)S(1)}, bf16[256,512]{1,0:T(8,128)(2,1)S(1)}, u32[]{:S(2)}, u32[]{:S(2)}) %collective-permute-start.32) | collective-permute-done | bytes 262176 | tf_op jit(solution)/shard_map/ppermute | solution.py:1049
  180.6 8.3 %collective-permute-done.31 = bf16[256,512]{1,0:T(8,128)(2,1)S(1)} collective-permute-done((bf16[256,512]{1,0:T(8,128)(2,1)S(1)}, bf16[256,512]{1,0:T(8,128)(2,1)S(1)}, u32[]{:S(2)}, u32[]{:S(2)}) %collective-permute-start.31) | collective-permute-done | bytes 262176 | tf_op jit(solution)/shard_map/ppermute | solution.py:1049
  190.8 7.5 %collective-permute-done.33 = bf16[256,512]{1,0:T(8,128)(2,1)S(1)} collective-permute-done((bf16[256,512]{1,0:T(8,128)(2,1)S(1)}, bf16[256,512]{1,0:T(8,128)(2,1)S(1)}, u32[]{:S(2)}, u32[]{:S(2)}) %collective-permute-start.33) | collective-permute-done | bytes 262176 | tf_op jit(solution)/shard_map/ppermute | solution.py:1049
  199.2 11.4 %run_experts.3 = (bf16[256,768]{1,0:T(8,128)(2,1)S(1)}, bf16[256,1536]{1,0:T(8,128)(2,1)S(1)}, bf16[256,128]{1,0:T(8,128)(2,1)S(1)}, bf16[256,2048]{1,0:T(8,128)(2,1)S(1)}, bf16[256,2048]{1,0:T(8,128)(2,1)S(1)}) custom-call(s32[5]{0:T(128)S(1)} %copy-done.24, bf16[128,768]{1,0:T(8,128)(2,1)S(1)} %copy-done.16, bf16[256,2048]{1,0:T(8,128)(2,1)S(1)} %second_norm.1.refs_0_, ...), custom_call_target="tpu_custom_call" | custom-call | flops 75497472 | bytes 273408 | tf_op jit(solution)/shard_map/run_experts/pallas_call | solution.py:599
  215.4 11.2 %run_experts.4 = (bf16[256,768]{1,0:T(8,128)(2,1)S(1)}, bf16[256,1536]{1,0:T(8,128)(2,1)S(1)}, bf16[256,128]{1,0:T(8,128)(2,1)S(1)}, bf16[256,2048]{1,0:T(8,128)...) custom-call(s32[5]{0:T(128)S(1)} %copy-done.24, ...), custom_call_target="tpu_custom_call" | custom-call | flops 75497472 | bytes 273408 | tf_op jit(solution)/shard_map/run_experts/pallas_call | solution.py:599
  227.0 20.7 %run_experts.5 = (bf16[512,768]{1,0:T(8,128)(2,1)S(1)}, bf16[512,1536]{1,0:T(8,128)(2,1)S(1)}, bf16[512,128]{1,0:T(8,128)(2,1)S(1)}, bf16[256,2048]{1,0:T(8,128)...) custom-call(s32[5]{0:T(128)S(1)} %copy-done.24, ...), custom_call_target="tpu_custom_call" | custom-call | flops 150994944 | bytes 325632 | tf_op jit(solution)/shard_map/run_experts/pallas_call | solution.py:599
  258.6 10.0 %weight_grads.6 = bf16[4,256,2432]{2,1,0:T(8,128)(2,1)} custom-call(s32[5]{0:T(128)S(1)} %copy-done.24, bf16[256,2048]{1,0:T(8,128)(2,1)S(1)} %second_norm.1.refs_0_, bf16[256,2048]{1,0:T(8,128)(2,1)S(1)} %collective-permute-done.30.refs_0_.refs_1_, bf16[256,2048]{1,0:T(8,128)(2,1)S(1)} %collective-permute-done.28.refs_0_.refs_2_, ...), custom_call_target="tpu_custom_call" | custom-call | flops 79691776 | bytes 212992 | tf_op jit(solution)/shard_map/weight_grads/pallas_call | solution.py:712
  268.6 8.8 %collective-permute-done.38 = bf16[256,512]{1,0:T(8,128)(2,1)S(1)} collective-permute-done((bf16[256,512]{1,0:T(8,128)(2,1)S(1)}, bf16[256,512]{1,0:T(8,128)(2,1)S(1)}, u32[]{:S(2)}, u32[]{:S(2)}) %collective-permute-start.38) | collective-permute-done | bytes 262176 | tf_op jit(solution)/shard_map/ppermute | solution.py:1049
  290.8 10.7 %weight_grads.7 = bf16[4,256,2432]{2,1,0:T(8,128)(2,1)} custom-call(s32[5]{0:T(128)S(1)} %copy-done.24, bf16[256,2048]{1,0:T(8,128)(2,1)S(1)} %second_norm.1.refs_0_, bf16[256,2048]{1,0:T(8,128)(2,1)S(1)} %collective-permute-done.30.refs_0_.refs_1_, bf16[256,2048]{1,0:T(8,128)(2,1)S(1)} %collective-permute-done.28.refs_0_.refs_2_, ...), custom_call_target="tpu_custom_call" | custom-call | flops 79691776 | bytes 290816 | tf_op jit(solution)/shard_map/weight_grads/pallas_call | solution.py:712
  313.7 5.5 %collective-permute-start.47 = (bf16[256,512]{1,0:T(8,128)(2,1)S(1)}, bf16[256,512]{1,0:T(8,128)(2,1)S(1)}, u32[]{:S(2)}, u32[]{:S(2)}) collective-permute-start(bf16[256,512]{1,0:T(8,128)(2,1)S(1)} %convert_element_type.91.refs_0_), channel_id=1, source_target_pairs={{0,2},{1,3},{2,0},{3,1},{4,6},{5,7},{6,4},{7,5},{8,10},{9,11},{10,... | collective-permute-start | bytes 786440 | tf_op jit(solution)/shard_map/ppermute | solution.py:1049
  321.5 16.0 %collective-permute-done.47.refs_2_ = bf16[256,512]{1,0:T(8,128)(2,1)S(1)} collective-permute-done((bf16[256,512]{1,0:T(8,128)(2,1)S(1)}, bf16[256,512]{1,0:T(8,128)(2,1)S(1)}, u32[]{:S(2)}, u32[]{:S(2)}) %collective-permute-start.47) | collective-permute-done | bytes 262176 | tf_op jit(solution)/shard_map/ppermute | solution.py:1049
  338.3 5.6 %contract.1 = (bf16[256,1024]{1,0:T(8,128)(2,1)}, bf16[256,2048]{1,0:T(8,128)(2,1)}) custom-call(s32[5]{0:T(128)} %stack.62.at_ref, bf16[256,512]{1,0:T(8,128)(2,1)} %copy-done.44, bf16[256,512]{1,0:T(8,128)(2,1)} %copy-done.56, bf16[256,512]{1,0:T(8,128)(2,1)} %copy-done.55, bf16[256,512]{1,0:T(8,128)(2,1)} %copy-done.54, bf16[4,256,1152]{2,1,0:T(8,128)(2,1)} %copy-done, ...), custom_call_target="tpu_custom_call" | custom-call | flops 16777216 | bytes 90112 | tf_op jit(solution)/shard_map/contract/pallas_call | solution.py:463
  348.4 11.8 %attend_back.1 = (f32[256,1024]{1,0:T(8,128)}, f32[4,256,256]{2,1,0:T(8,128)}, bf16[4,256,256]{2,1,0:T(8,128)(2,1)}) custom-call(bf16[256,1024]{1,0:T(8,128)(2,1)} %get-tuple-element.218.q_ref, bf16[4,256,256]{2,1,0:T(8,128)(2,1)} %copy-done.6, bf16[4,256,256]{2,1,0:T(8,128)(2,1)} %copy-done.15, f32[2,1024,128]{2,1,0:T(8,128)} %get-tuple-element.222.bias_ref, ...), custom_call_target="tpu_custom_call" | custom-call | flops 41943040 | bytes 32768 | tf_op jit(solution)/shard_map/attend_back/pallas_call | solution.py:378
  392.6 9.6 %project_back.1 = (f32[256,512]{1,0:T(8,128)}, bf16[288,512]{1,0:T(8,128)(2,1)}, bf16[288,512]{1,0:T(8,128)(2,1)}, bf16[288,512]{1,0:T(8,128)(2,1)}, bf16[256,1280]{1,0:T(8,128)(2,1)}, /*index=5*/f32[32,512]{1,0:T(8,128)}) custom-call(s32[5]{0:T(128)} %stack.62.at_ref, f32[256,1280]{1,0:T(8,128)} %get-tuple-element.216.pre_ref, f32[1,2048]{1,0:T(1,128)} %copy-done.30, ...), custom_call_target="tpu_custom_call" | custom-call | flops 20971520 | bytes 149776 | tf_op jit(solution)/shard_map/project_back/pallas_call | solution.py:897
  406.8 6.4 %by_columns.1 = (f32[256,3072]{1,0:T(8,128)}, f32[256,3072]{1,0:T(8,128)}, f32[256,3072]{1,0:T(8,128)}) custom-call(bf16[4,256,2432]{2,1,0:T(8,128)(2,1)} %all-to-all-done.2.ref), custom_call_target="tpu_custom_call" | custom-call | bytes 225280 | tf_op jit(solution)/shard_map/by_columns/pallas_call | solution.py:779
  442.5 11.6 %collective-permute-done.63.refs_1_ = bf16[288,512]{1,0:T(8,128)(2,1)} collective-permute-done((bf16[288,512]{1,0:T(8,128)(2,1)}, bf16[288,512]{1,0:T(8,128)(2,1)}, u32[]{:S(2)}, u32[]{:S(2)}) %collective-permute-start.63) | collective-permute-done | bytes 294944 | tf_op jit(solution)/shard_map/ppermute | solution.py:1049
  (345 shorter events, 231.3 us)
Async XLA Ops:
  4.5 25.4 %collective-permute-start.5 = (bf16[256,512]{1,0:T(8,128)(2,1)}, bf16[256,512]{1,0:T(8,128)(2,1)}, u32[]{:S(2)}, u32[]{:S(2)}) collective-permute-start(bf16[256,512]{1,0:T(8,128)(2,1)} %pad_maximum_fusion.3.refs_0_.refs_5_), channel_id=1, source_target_pairs={{0,3},{1,2},{2,1},{3,0},{4,7},{5,6},{6,5},{7,4},{8,11},{9,10},{10,... | collective-permute-start | bytes 786440 | tf_op jit(solution)/shard_map/ppermute | solution.py:1049
  9.6 28.0 %collective-permute-start.2 = (bf16[256,1280]{1,0:T(8,128)(2,1)S(1)}, bf16[256,1280]{1,0:T(8,128)(2,1)}, u32[]{:S(2)}, u32[]{:S(2)}) collective-permute-start(bf16[256,1280]{1,0:T(8,128)(2,1)S(1)} %constant_dynamic-update-slice_fusion.refs_4_.refs_9_), channel_id=1, source_target_pairs={{0,24},{8,16},{16,8},{24,0},{1,25},{9,17},{17,9},{25,1},{2,26},{10... | collective-permute-start | bytes 1966088 | tf_op jit(solution)/shard_map/ppermute | solution.py:1094
  12.1 30.4 %collective-permute-start.1 = (bf16[256,1280]{1,0:T(8,128)(2,1)S(1)}, bf16[256,1280]{1,0:T(8,128)(2,1)}, u32[]{:S(2)}, u32[]{:S(2)}) collective-permute-start(bf16[256,1280]{1,0:T(8,128)(2,1)S(1)} %constant_dynamic-update-slice_fusion.refs_4_.refs_9_), channel_id=1, source_target_pairs={{0,16},{8,24},{16,0},{24,8},{1,17},{9,25},{17,1},{25,9},{2,18},{10... | collective-permute-start | bytes 1966088 | tf_op jit(solution)/shard_map/ppermute | solution.py:1094
  12.7 29.9 %collective-permute-start = (bf16[256,1280]{1,0:T(8,128)(2,1)S(1)}, bf16[256,1280]{1,0:T(8,128)(2,1)}, u32[]{:S(2)}, u32[]{:S(2)}) collective-permute-start(bf16[256,1280]{1,0:T(8,128)(2,1)S(1)} %constant_dynamic-update-slice_fusion.refs_4_.refs_9_), channel_id=1, source_target_pairs={{0,8},{8,0},{16,24},{24,16},{1,9},{9,1},{17,25},{25,17},{2,10},{10... | collective-permute-start | bytes 1966088 | tf_op jit(solution)/shard_map/ppermute | solution.py:1094
  26.1 48.2 %all-to-all-start = ((bf16[4,256,1152]{2,1,0:T(8,128)(2,1)}), bf16[4,256,1152]{2,1,0:T(8,128)(2,1)S(1)}, u32[]{:S(2)}, u32[]{:S(2)}) async-start(bf16[4,256,1152]{2,1,0:T(8,128)(2,1)} %broadcast_in_dim.24), calls=%async_computation | async-start | bytes 4718592 | tf_op jit(solution)/shard_map/all_to_all | solution.py:1052
  78.9 59.7 %all-to-all-start.1 = ((bf16[4,256,2304]{2,1,0:T(8,128)(2,1)}), bf16[4,256,2304]{2,1,0:T(8,128)(2,1)}, u32[]{:S(2)}, u32[]{:S(2)}) async-start(bf16[4,256,2304]{2,1,0:T(8,128)(2,1)} %by_owner.1), calls=%async_computation.1 | async-start | bytes 9437184 | tf_op jit(solution)/shard_map/all_to_all | solution.py:1052
  86.9 24.8 %collective-permute-start.16 = (bf16[256,512]{1,0:T(8,128)(2,1)S(1)}, bf16[256,512]{1,0:T(8,128)(2,1)S(1)}, u32[]{:S(2)}, u32[]{:S(2)}) collective-permute-start(bf16[256,512]{1,0:T(8,128)(2,1)S(1)} %pad_maximum_fusion.4), channel_id=1, source_target_pairs={{0,2},{1,3},{2,0},{3,1},{4,6},{5,7},{6,4},{7,5},{8,10},{9,11},{10,... | collective-permute-start | bytes 786440 | tf_op jit(solution)/shard_map/ppermute | solution.py:1049
  111.9 48.2 %collective-permute-start.26 = (bf16[256,2176]{1,0:T(8,128)(2,1)S(1)}, bf16[256,2176]{1,0:T(8,128)(2,1)}, u32[]{:S(2)}, u32[]{:S(2)}) collective-permute-start(bf16[256,2176]{1,0:T(8,128)(2,1)S(1)} %constant_dynamic-update-slice_fusion.3.refs_1_.refs_4_), channel_id=1, source_target_pairs={{0,16},{8,24},{16,0},{24,8},{1,17},{9,25},{17,1},{25,9},{2,18},{10... | collective-permute-start | bytes 3342344 | tf_op jit(solution)/shard_map/ppermute | solution.py:1094
  113.9 46.2 %collective-permute-start.25 = (bf16[256,2176]{1,0:T(8,128)(2,1)S(1)}, bf16[256,2176]{1,0:T(8,128)(2,1)}, u32[]{:S(2)}, u32[]{:S(2)}) collective-permute-start(bf16[256,2176]{1,0:T(8,128)(2,1)S(1)} %constant_dynamic-update-slice_fusion.3.refs_1_.refs_4_), channel_id=1, source_target_pairs={{0,8},{8,0},{16,24},{24,16},{1,9},{9,1},{17,25},{25,17},{2,10},{10... | collective-permute-start | bytes 3342344 | tf_op jit(solution)/shard_map/ppermute | solution.py:1094
  164.5 34.7 %collective-permute-start.27 = (bf16[4,256,2304]{2,1,0:T(8,128)(2,1)}, bf16[4,256,2304]{2,1,0:T(8,128)(2,1)S(1)}, u32[]{:S(2)}, u32[]{:S(2)}) collective-permute-start(bf16[4,256,2304]{2,1,0:T(8,128)(2,1)} %all-to-all-done.1.refs_2_.refs_4_), channel_id=1, source_target_pairs={{0,4},{4,0},{1,5},{5,1},{2,6},{6,2},{3,7},{7,3},{8,12},{12,8},{9,1... | collective-permute-start | bytes 14155784 | tf_op jit(solution)/shard_map/ppermute | solution.py:1046
  166.0 45.5 %collective-permute-start.30 = (bf16[256,2048]{1,0:T(8,128)(2,1)S(1)}, bf16[256,2048]{1,0:T(8,128)(2,1)S(1)}, u32[]{:S(2)}, u32[]{:S(2)}) collective-permute-start(bf16[256,2048]{1,0:T(8,128)(2,1)S(1)} %second_norm.1.refs_0_), channel_id=1, source_target_pairs={{0,24},{8,16},{16,8},{24,0},{1,25},{9,17},{17,9},{25,1},{2,26},{10... | collective-permute-start | bytes 3145736 | tf_op jit(solution)/shard_map/ppermute | solution.py:1094
  166.8 47.8 %collective-permute-start.29 = (bf16[256,2048]{1,0:T(8,128)(2,1)S(1)}, bf16[256,2048]{1,0:T(8,128)(2,1)S(1)}, u32[]{:S(2)}, u32[]{:S(2)}) collective-permute-start(bf16[256,2048]{1,0:T(8,128)(2,1)S(1)} %second_norm.1.refs_0_), channel_id=1, source_target_pairs={{0,16},{8,24},{16,0},{24,8},{1,17},{9,25},{17,1},{25,9},{2,18},{10... | collective-permute-start | bytes 3145736 | tf_op jit(solution)/shard_map/ppermute | solution.py:1094
  168.1 47.3 %collective-permute-start.28 = (bf16[256,2048]{1,0:T(8,128)(2,1)S(1)}, bf16[256,2048]{1,0:T(8,128)(2,1)S(1)}, u32[]{:S(2)}, u32[]{:S(2)}) collective-permute-start(bf16[256,2048]{1,0:T(8,128)(2,1)S(1)} %second_norm.1.refs_0_), channel_id=1, source_target_pairs={{0,8},{8,0},{16,24},{24,16},{1,9},{9,1},{17,25},{25,17},{2,10},{10... | collective-permute-start | bytes 3145736 | tf_op jit(solution)/shard_map/ppermute | solution.py:1094
  226.6 26.0 %collective-permute-start.34 = (bf16[256,2048]{1,0:T(8,128)(2,1)}, bf16[256,2048]{1,0:T(8,128)(2,1)S(1)}, u32[]{:S(2)}, u32[]{:S(2)}) collective-permute-start(bf16[256,2048]{1,0:T(8,128)(2,1)} %get-tuple-element.262), channel_id=1, source_target_pairs={{0,24},{8,16},{16,8},{24,0},{1,25},{9,17},{17,9},{25,1},{2,26},{10... | collective-permute-start | bytes 3145736 | tf_op jit(solution)/shard_map/ppermute | solution.py:1094
  252.6 25.6 %collective-permute-start.35 = (bf16[256,2048]{1,0:T(8,128)(2,1)}, bf16[256,2048]{1,0:T(8,128)(2,1)S(1)}, u32[]{:S(2)}, u32[]{:S(2)}) collective-permute-start(bf16[256,2048]{1,0:T(8,128)(2,1)} %get-tuple-element.280), channel_id=1, source_target_pairs={{0,8},{8,0},{16,24},{24,16},{1,9},{9,1},{17,25},{25,17},{2,10},{10... | collective-permute-start | bytes 3145736 | tf_op jit(solution)/shard_map/ppermute | solution.py:1094
  253.2 25.1 %collective-permute-start.36 = (bf16[256,2048]{1,0:T(8,128)(2,1)}, bf16[256,2048]{1,0:T(8,128)(2,1)S(1)}, u32[]{:S(2)}, u32[]{:S(2)}) collective-permute-start(bf16[256,2048]{1,0:T(8,128)(2,1)} %copy-done.33), channel_id=1, source_target_pairs={{0,16},{8,24},{16,0},{24,8},{1,17},{9,25},{17,1},{25,9},{2,18},{10... | collective-permute-start | bytes 3145736 | tf_op jit(solution)/shard_map/ppermute | solution.py:1094
  278.3 28.1 %collective-permute-start.44 = (bf16[256,2048]{1,0:T(8,128)(2,1)S(1)}, bf16[256,2048]{1,0:T(8,128)(2,1)S(1)}, u32[]{:S(2)}, u32[]{:S(2)}) collective-permute-start(bf16[256,2048]{1,0:T(8,128)(2,1)S(1)} %copy-done.32), channel_id=1, source_target_pairs={{0,8},{8,0},{16,24},{24,16},{1,9},{9,1},{17,25},{25,17},{2,10},{10... | collective-permute-start | bytes 3145736 | tf_op jit(solution)/shard_map/ppermute | solution.py:1094
  279.0 28.4 %collective-permute-start.45 = (bf16[256,2048]{1,0:T(8,128)(2,1)S(1)}, bf16[256,2048]{1,0:T(8,128)(2,1)}, u32[]{:S(2)}, u32[]{:S(2)}) collective-permute-start(bf16[256,2048]{1,0:T(8,128)(2,1)S(1)} %get-tuple-element.300), channel_id=1, source_target_pairs={{0,16},{8,24},{16,0},{24,8},{1,17},{9,25},{17,1},{25,9},{2,18},{10... | collective-permute-start | bytes 3145736 | tf_op jit(solution)/shard_map/ppermute | solution.py:1094
  307.4 62.2 %all-to-all-start.2 = ((bf16[4,256,2432]{2,1,0:T(8,128)(2,1)}), bf16[4,256,2432]{2,1,0:T(8,128)(2,1)}, u32[]{:S(2)}, u32[]{:S(2)}) async-start(bf16[4,256,2432]{2,1,0:T(8,128)(2,1)} %weight_grads.7), calls=%async_computation.2 | async-start | bytes 9961472 | tf_op jit(solution)/shard_map/all_to_all | solution.py:1052
  313.7 23.8 %collective-permute-start.47 = (bf16[256,512]{1,0:T(8,128)(2,1)S(1)}, bf16[256,512]{1,0:T(8,128)(2,1)S(1)}, u32[]{:S(2)}, u32[]{:S(2)}) collective-permute-start(bf16[256,512]{1,0:T(8,128)(2,1)S(1)} %convert_element_type.91.refs_0_), channel_id=1, source_target_pairs={{0,2},{1,3},{2,0},{3,1},{4,6},{5,7},{6,4},{7,5},{8,10},{9,11},{10,... | collective-permute-start | bytes 786440 | tf_op jit(solution)/shard_map/ppermute | solution.py:1049
  388.7 29.3 %all-to-all-start.3 = ((bf16[4,256,1024]{2,1,0:T(8,128)(2,1)}), bf16[4,256,1024]{2,1,0:T(8,128)(2,1)S(1)}, u32[]{:S(2)}, u32[]{:S(2)}) async-start(bf16[4,256,1024]{2,1,0:T(8,128)(2,1)} %copy-done.5), calls=%async_computation.3 | async-start | bytes 4194304 | tf_op jit(solution)/shard_map/all_to_all | solution.py:1052
  419.4 42.4 %all-to-all-start.4 = ((bf16[4,256,1280]{2,1,0:T(8,128)(2,1)}), bf16[4,256,1280]{2,1,0:T(8,128)(2,1)S(1)}, u32[]{:S(2)}, u32[]{:S(2)}) async-start(bf16[4,256,1280]{2,1,0:T(8,128)(2,1)} %copy-done.4), calls=%async_computation.4 | async-start | bytes 5242880 | tf_op jit(solution)/shard_map/all_to_all | solution.py:1052
  430.3 23.8 %collective-permute-start.63 = (bf16[288,512]{1,0:T(8,128)(2,1)}, bf16[288,512]{1,0:T(8,128)(2,1)}, u32[]{:S(2)}, u32[]{:S(2)}) collective-permute-start(bf16[288,512]{1,0:T(8,128)(2,1)} %get-tuple-element.351), channel_id=1, source_target_pairs={{0,2},{1,3},{2,0},{3,1},{4,6},{5,7},{6,4},{7,5},{8,10},{9,11},{10,... | collective-permute-start | bytes 884744 | tf_op jit(solution)/shard_map/ppermute | solution.py:1049
  430.3 23.8 %collective-permute-start.64 = (bf16[288,512]{1,0:T(8,128)(2,1)}, bf16[288,512]{1,0:T(8,128)(2,1)}, u32[]{:S(2)}, u32[]{:S(2)}) collective-permute-start(bf16[288,512]{1,0:T(8,128)(2,1)} %get-tuple-element.352), channel_id=1, source_target_pairs={{0,3},{1,2},{2,1},{3,0},{4,7},{5,6},{6,5},{7,4},{8,11},{9,10},{10,... | collective-permute-start | bytes 884744 | tf_op jit(solution)/shard_map/ppermute | solution.py:1049
  (119 other events, 1590.2 us)

commit v5 on v4

--- a/solution.py
+++ b/solution.py
@@ -272,7 +272,7 @@
         out_specs=[whole(o.shape) for o in outs],
         scratch_shapes=[full_weight(pair), weight_sems(pair)],
         grid=(1,),
-        compiler_params=params(),
+        compiler_params=params(limit=32 * 1024 * 1024),
         cost_estimate=cost(4.5e11, 1),
         name="project",
     )(at, *ins)
@@ -319,7 +319,7 @@
             pl.BlockSpec((1, keys, tok), lambda m: (m, 0, 0)),
         ],
         out_specs=[head_spec, pl.BlockSpec((1, heads, 1, tok), lambda m: (m, 0, 0, 0))],
-        compiler_params=params(limit=40 * 1024 * 1024),
+        compiler_params=params(limit=32 * 1024 * 1024),
         cost_estimate=cost(4 * micro * heads * keys * tok * size, nbytes((own, other, bias))),
         name="attend",
     )(ready, own, other, bias)
@@ -436,7 +436,7 @@
         out_specs=[whole(o.shape) for o in outs],
         scratch_shapes=[full_weight(pair, n), weight_sems(pair)],
         grid=(1,),
-        compiler_params=params(limit=40 * 1024 * 1024),
+        compiler_params=params(limit=32 * 1024 * 1024),
         cost_estimate=cost(2 * tokens * n * part * parts, nbytes(ins)),
         name="expand",
     )(at, *ins)

time: 477 us -> 477 us (level)
    unnamed x154 -> x176, local copies, waits for them, and re-layouts: 22.1 us -> 25.1 us
where the time goes in v5:
time: 477 us; the launch traced here: 468 us
  waiting for transfers between devices  170 us (36%)
  Pallas kernels  137 us (29%)
  starting transfers between devices  108 us (23%)
  local copies, waits for them, and re-layouts  35.7 us (7%)
  other arithmetic  14.7 us (3%)
    ppermute x30, waiting for transfers between devices, col_swap(): return lax.ppermute(a, 'col', [(i, i ^ mask) for i in range(cols)])  115 us
    ppermute x30, starting transfers between devices, col_swap(): return lax.ppermute(a, 'col', [(i, i ^ mask) for i in range(cols)])  55.4 us
    ppermute x24, waiting for transfers between devices, swap(): return lax.ppermute(a, 'outer', [(i, i ^ mask) for i in range(outer)])  43.9 us
    pallas_call x3, Pallas kernels, run_experts(): pl.pallas_call(kernel, out_shape=outs, grid_spec=pltpu.PrefetchScalarGrid...  43.3 us
    pallas_call x6, Pallas kernels, weight_grads(): pl.pallas_call(kernel, out_shape=outs, grid_spec=pltpu.PrefetchScalarGrid...  32.1 us
    ppermute x24, starting transfers between devices, swap(): return lax.ppermute(a, 'outer', [(i, i ^ mask) for i in range(outer)])  27.6 us
    unnamed x176, local copies, waits for them, and re-layouts  25.1 us
    all_to_all x5, starting transfers between devices, exchange(): return lax.all_to_all(a, 'outer', 0, 0, tiled=True)  22.3 us
  transfers between devices with their start and end apart: 74, of which 34 were waited for; matrix products, arithmetic and copies ran while one was open for 5% of the time, Pallas kernels for 27%

profile of v5, /device:TPU:0, one launch (start us, length us, event | category | flops | bytes accessed | tf_op | source)
XLA Modules:
  0.0 467.5 jit_solution(3840616887842495428)
XLA Ops:
  62.8 7.8 %collective-permute-done.12 = bf16[256,256]{1,0:T(8,128)(2,1)S(1)} collective-permute-done((bf16[256,256]{1,0:T(8,128)(2,1)S(1)}, bf16[256,256]{1,0:T(8,128)(2,1)S(1)}, u32[]{:S(2)}, u32[]{:S(2)}) %collective-permute-start.12) | collective-permute-done | bytes 131104 | tf_op jit(solution)/shard_map/ppermute | solution.py:1094
  73.5 5.4 %collective-permute-done.21 = bf16[256,640]{1,0:T(8,128)(2,1)} collective-permute-done((bf16[256,640]{1,0:T(8,128)(2,1)}, bf16[256,640]{1,0:T(8,128)(2,1)}, u32[]{:S(2)}, u32[]{:S(2)}) %collective-permute-start.21) | collective-permute-done | bytes 327712 | tf_op jit(solution)/shard_map/ppermute | solution.py:1094
  91.1 5.6 %attend.1 = (bf16[256,1024]{1,0:T(8,128)(2,1)S(1)}, f32[2,8,1,128]{3,2,1,0:T(1,128)S(1)}) custom-call(bf16[256,1024]{1,0:T(8,128)(2,1)S(1)} %get-tuple-element.218.q_ref, bf16[4,256,256]{2,1,0:T(8,128)(2,1)S(1)} %pad_maximum_fusion.1.own_ref, bf16[4,256,256]{2,1,0:T(8,128)(2,1)S(1)} %collective-permute-done.13.other_ref, f32[2,1024,128]{2,1,0:T(8,128)S(1)} %copy-done.9), custom_call_target="tpu_custom_call" | custom-call | flops 16777216 | bytes 32768 | tf_op jit(solution)/shard_map/attend/pallas_call | solution.py:311
  100.5 11.2 %collective-permute-done.16 = bf16[256,512]{1,0:T(8,128)(2,1)S(1)} collective-permute-done((bf16[256,512]{1,0:T(8,128)(2,1)S(1)}, bf16[256,512]{1,0:T(8,128)(2,1)S(1)}, u32[]{:S(2)}, u32[]{:S(2)}) %collective-permute-start.16) | collective-permute-done | bytes 262176 | tf_op jit(solution)/shard_map/ppermute | solution.py:1049
  119.8 8.1 %collective-permute-done.18 = bf16[256,512]{1,0:T(8,128)(2,1)S(1)} collective-permute-done((bf16[256,512]{1,0:T(8,128)(2,1)S(1)}, bf16[256,512]{1,0:T(8,128)(2,1)S(1)}, u32[]{:S(2)}, u32[]{:S(2)}) %collective-permute-start.18) | collective-permute-done | bytes 262176 | tf_op jit(solution)/shard_map/ppermute | solution.py:1049
  127.9 9.0 %collective-permute-done.19 = bf16[256,512]{1,0:T(8,128)(2,1)S(1)} collective-permute-done((bf16[256,512]{1,0:T(8,128)(2,1)S(1)}, bf16[256,512]{1,0:T(8,128)(2,1)S(1)}, u32[]{:S(2)}, u32[]{:S(2)}) %collective-permute-start.19) | collective-permute-done | bytes 262176 | tf_op jit(solution)/shard_map/ppermute | solution.py:1049
  141.4 6.7 %collective-permute-start.23 = (bf16[256,512]{1,0:T(8,128)(2,1)S(1)}, bf16[256,512]{1,0:T(8,128)(2,1)S(1)}, u32[]{:S(2)}, u32[]{:S(2)}) collective-permute-start(bf16[256,512]{1,0:T(8,128)(2,1)S(1)} %convert_element_type.81.refs_0_.refs_4_), channel_id=1, source_target_pairs={{0,2},{1,3},{2,0},{3,1},{4,6},{5,7},{6,4},{7,5},{8,10},{9,11},{10,... | collective-permute-start | bytes 786440 | tf_op jit(solution)/shard_map/ppermute | solution.py:1049
  148.1 12.0 %collective-permute-done.26.refs_3_.refs_7_ = bf16[256,2176]{1,0:T(8,128)(2,1)} collective-permute-done((bf16[256,2176]{1,0:T(8,128)(2,1)S(1)}, bf16[256,2176]{1,0:T(8,128)(2,1)}, u32[]{:S(2)}, u32[]{:S(2)}) %collective-permute-start.26) | collective-permute-done | bytes 1114144 | tf_op jit(solution)/shard_map/ppermute | solution.py:1094
  169.5 11.0 %collective-permute-done.32 = bf16[256,512]{1,0:T(8,128)(2,1)S(1)} collective-permute-done((bf16[256,512]{1,0:T(8,128)(2,1)S(1)}, bf16[256,512]{1,0:T(8,128)(2,1)S(1)}, u32[]{:S(2)}, u32[]{:S(2)}) %collective-permute-start.32) | collective-permute-done | bytes 262176 | tf_op jit(solution)/shard_map/ppermute | solution.py:1049
  180.5 8.3 %collective-permute-done.31 = bf16[256,512]{1,0:T(8,128)(2,1)S(1)} collective-permute-done((bf16[256,512]{1,0:T(8,128)(2,1)S(1)}, bf16[256,512]{1,0:T(8,128)(2,1)S(1)}, u32[]{:S(2)}, u32[]{:S(2)}) %collective-permute-start.31) | collective-permute-done | bytes 262176 | tf_op jit(solution)/shard_map/ppermute | solution.py:1049
  190.7 7.5 %collective-permute-done.33 = bf16[256,512]{1,0:T(8,128)(2,1)S(1)} collective-permute-done((bf16[256,512]{1,0:T(8,128)(2,1)S(1)}, bf16[256,512]{1,0:T(8,128)(2,1)S(1)}, u32[]{:S(2)}, u32[]{:S(2)}) %collective-permute-start.33) | collective-permute-done | bytes 262176 | tf_op jit(solution)/shard_map/ppermute | solution.py:1049
  199.1 11.4 %run_experts.3 = (bf16[256,768]{1,0:T(8,128)(2,1)S(1)}, bf16[256,1536]{1,0:T(8,128)(2,1)S(1)}, bf16[256,128]{1,0:T(8,128)(2,1)S(1)}, bf16[256,2048]{1,0:T(8,128)(2,1)S(1)}, bf16[256,2048]{1,0:T(8,128)(2,1)S(1)}) custom-call(s32[5]{0:T(128)S(1)} %copy-done.38, bf16[128,768]{1,0:T(8,128)(2,1)S(1)} %copy-done.18, bf16[256,2048]{1,0:T(8,128)(2,1)S(1)} %second_norm.1.refs_0_, ...), custom_call_target="tpu_custom_call" | custom-call | flops 75497472 | bytes 273408 | tf_op jit(solution)/shard_map/run_experts/pallas_call | solution.py:599
  215.4 11.3 %run_experts.4 = (bf16[256,768]{1,0:T(8,128)(2,1)S(1)}, bf16[256,1536]{1,0:T(8,128)(2,1)S(1)}, bf16[256,128]{1,0:T(8,128)(2,1)S(1)}, bf16[256,2048]{1,0:T(8,128)...) custom-call(s32[5]{0:T(128)S(1)} %copy-done.38, ...), custom_call_target="tpu_custom_call" | custom-call | flops 75497472 | bytes 273408 | tf_op jit(solution)/shard_map/run_experts/pallas_call | solution.py:599
  227.0 20.7 %run_experts.5 = (bf16[512,768]{1,0:T(8,128)(2,1)S(1)}, bf16[512,1536]{1,0:T(8,128)(2,1)S(1)}, bf16[512,128]{1,0:T(8,128)(2,1)S(1)}, bf16[256,2048]{1,0:T(8,128)...) custom-call(s32[5]{0:T(128)S(1)} %copy-done.38, ...), custom_call_target="tpu_custom_call" | custom-call | flops 150994944 | bytes 325632 | tf_op jit(solution)/shard_map/run_experts/pallas_call | solution.py:599
  258.6 10.0 %weight_grads.6 = bf16[4,256,2432]{2,1,0:T(8,128)(2,1)} custom-call(s32[5]{0:T(128)S(1)} %copy-done.38, bf16[256,2048]{1,0:T(8,128)(2,1)S(1)} %second_norm.1.refs_0_, bf16[256,2048]{1,0:T(8,128)(2,1)S(1)} %collective-permute-done.30.refs_0_.refs_1_, bf16[256,2048]{1,0:T(8,128)(2,1)S(1)} %collective-permute-done.28.refs_0_.refs_2_, ...), custom_call_target="tpu_custom_call" | custom-call | flops 79691776 | bytes 212992 | tf_op jit(solution)/shard_map/weight_grads/pallas_call | solution.py:712
  268.6 8.8 %collective-permute-done.38 = bf16[256,512]{1,0:T(8,128)(2,1)S(1)} collective-permute-done((bf16[256,512]{1,0:T(8,128)(2,1)S(1)}, bf16[256,512]{1,0:T(8,128)(2,1)S(1)}, u32[]{:S(2)}, u32[]{:S(2)}) %collective-permute-start.38) | collective-permute-done | bytes 262176 | tf_op jit(solution)/shard_map/ppermute | solution.py:1049
  290.8 10.7 %weight_grads.7 = bf16[4,256,2432]{2,1,0:T(8,128)(2,1)} custom-call(s32[5]{0:T(128)S(1)} %copy-done.38, bf16[256,2048]{1,0:T(8,128)(2,1)S(1)} %second_norm.1.refs_0_, bf16[256,2048]{1,0:T(8,128)(2,1)S(1)} %collective-permute-done.30.refs_0_.refs_1_, bf16[256,2048]{1,0:T(8,128)(2,1)S(1)} %collective-permute-done.28.refs_0_.refs_2_, ...), custom_call_target="tpu_custom_call" | custom-call | flops 79691776 | bytes 290816 | tf_op jit(solution)/shard_map/weight_grads/pallas_call | solution.py:712
  320.7 15.9 %collective-permute-done.47.refs_2_ = bf16[256,512]{1,0:T(8,128)(2,1)S(1)} collective-permute-done((bf16[256,512]{1,0:T(8,128)(2,1)S(1)}, bf16[256,512]{1,0:T(8,128)(2,1)S(1)}, u32[]{:S(2)}, u32[]{:S(2)}) %collective-permute-start.47) | collective-permute-done | bytes 262176 | tf_op jit(solution)/shard_map/ppermute | solution.py:1049
  337.4 5.6 %contract.1 = (bf16[256,1024]{1,0:T(8,128)(2,1)}, bf16[256,2048]{1,0:T(8,128)(2,1)}) custom-call(s32[5]{0:T(128)} %stack.62.at_ref, bf16[256,512]{1,0:T(8,128)(2,1)} %copy-done.61, bf16[256,512]{1,0:T(8,128)(2,1)} %copy-done.67, bf16[256,512]{1,0:T(8,128)(2,1)} %copy-done.66, bf16[256,512]{1,0:T(8,128)(2,1)} %copy-done.65, bf16[4,256,1152]{2,1,0:T(8,128)(2,1)} %copy-done, ...), custom_call_target="tpu_custom_call" | custom-call | flops 16777216 | bytes 90112 | tf_op jit(solution)/shard_map/contract/pallas_call | solution.py:463
  347.4 11.8 %attend_back.1 = (f32[256,1024]{1,0:T(8,128)}, f32[4,256,256]{2,1,0:T(8,128)}, bf16[4,256,256]{2,1,0:T(8,128)(2,1)}) custom-call(bf16[256,1024]{1,0:T(8,128)(2,1)} %copy-done.16, bf16[4,256,256]{2,1,0:T(8,128)(2,1)} %copy-done.6, bf16[4,256,256]{2,1,0:T(8,128)(2,1)} %copy-done.17, f32[2,1024,128]{2,1,0:T(8,128)} %get-tuple-element.222.bias_ref, ...), custom_call_target="tpu_custom_call" | custom-call | flops 41943040 | bytes 32768 | tf_op jit(solution)/shard_map/attend_back/pallas_call | solution.py:378
  391.6 9.6 %project_back.1 = (f32[256,512]{1,0:T(8,128)}, bf16[288,512]{1,0:T(8,128)(2,1)}, bf16[288,512]{1,0:T(8,128)(2,1)}, bf16[288,512]{1,0:T(8,128)(2,1)}, bf16[256,1280]{1,0:T(8,128)(2,1)}, /*index=5*/f32[32,512]{1,0:T(8,128)}) custom-call(s32[5]{0:T(128)} %stack.62.at_ref, f32[256,1280]{1,0:T(8,128)} %copy-done.19, f32[1,2048]{1,0:T(1,128)} %copy-done.45, ...), custom_call_target="tpu_custom_call" | custom-call | flops 20971520 | bytes 149776 | tf_op jit(solution)/shard_map/project_back/pallas_call | solution.py:897
  405.8 6.4 %by_columns.1 = (f32[256,3072]{1,0:T(8,128)}, f32[256,3072]{1,0:T(8,128)}, f32[256,3072]{1,0:T(8,128)}) custom-call(bf16[4,256,2432]{2,1,0:T(8,128)(2,1)} %all-to-all-done.2.ref), custom_call_target="tpu_custom_call" | custom-call | bytes 225280 | tf_op jit(solution)/shard_map/by_columns/pallas_call | solution.py:779
  423.9 5.4 %collective-permute-start.62 = (bf16[288,512]{1,0:T(8,128)(2,1)}, bf16[288,512]{1,0:T(8,128)(2,1)S(1)}, u32[]{:S(2)}, u32[]{:S(2)}) collective-permute-start(bf16[288,512]{1,0:T(8,128)(2,1)} %get-tuple-element.350), channel_id=1, source_target_pairs={{0,1},{1,0},{2,3},{3,2},{4,5},{5,4},{6,7},{7,6},{8,9},{9,8},{10,11... | collective-permute-start | bytes 884744 | tf_op jit(solution)/shard_map/ppermute | solution.py:1049
  441.6 11.5 %collective-permute-done.63.refs_1_ = bf16[288,512]{1,0:T(8,128)(2,1)} collective-permute-done((bf16[288,512]{1,0:T(8,128)(2,1)}, bf16[288,512]{1,0:T(8,128)(2,1)}, u32[]{:S(2)}, u32[]{:S(2)}) %collective-permute-start.63) | collective-permute-done | bytes 294944 | tf_op jit(solution)/shard_map/ppermute | solution.py:1049
  (367 shorter events, 233.7 us)
Async XLA Ops:
  4.3 25.7 %collective-permute-start.5 = (bf16[256,512]{1,0:T(8,128)(2,1)S(1)}, bf16[256,512]{1,0:T(8,128)(2,1)S(1)}, u32[]{:S(2)}, u32[]{:S(2)}) collective-permute-start(bf16[256,512]{1,0:T(8,128)(2,1)S(1)} %pad_maximum_fusion.3.refs_0_.refs_5_), channel_id=1, source_target_pairs={{0,3},{1,2},{2,1},{3,0},{4,7},{5,6},{6,5},{7,4},{8,11},{9,10},{10,... | collective-permute-start | bytes 786440 | tf_op jit(solution)/shard_map/ppermute | solution.py:1049
  9.6 27.8 %collective-permute-start.2 = (bf16[256,1280]{1,0:T(8,128)(2,1)S(1)}, bf16[256,1280]{1,0:T(8,128)(2,1)}, u32[]{:S(2)}, u32[]{:S(2)}) collective-permute-start(bf16[256,1280]{1,0:T(8,128)(2,1)S(1)} %constant_dynamic-update-slice_fusion.refs_4_.refs_9_), channel_id=1, source_target_pairs={{0,24},{8,16},{16,8},{24,0},{1,25},{9,17},{17,9},{25,1},{2,26},{10... | collective-permute-start | bytes 1966088 | tf_op jit(solution)/shard_map/ppermute | solution.py:1094
  12.1 30.4 %collective-permute-start.1 = (bf16[256,1280]{1,0:T(8,128)(2,1)S(1)}, bf16[256,1280]{1,0:T(8,128)(2,1)}, u32[]{:S(2)}, u32[]{:S(2)}) collective-permute-start(bf16[256,1280]{1,0:T(8,128)(2,1)S(1)} %constant_dynamic-update-slice_fusion.refs_4_.refs_9_), channel_id=1, source_target_pairs={{0,16},{8,24},{16,0},{24,8},{1,17},{9,25},{17,1},{25,9},{2,18},{10... | collective-permute-start | bytes 1966088 | tf_op jit(solution)/shard_map/ppermute | solution.py:1094
  12.6 29.9 %collective-permute-start = (bf16[256,1280]{1,0:T(8,128)(2,1)S(1)}, bf16[256,1280]{1,0:T(8,128)(2,1)}, u32[]{:S(2)}, u32[]{:S(2)}) collective-permute-start(bf16[256,1280]{1,0:T(8,128)(2,1)S(1)} %constant_dynamic-update-slice_fusion.refs_4_.refs_9_), channel_id=1, source_target_pairs={{0,8},{8,0},{16,24},{24,16},{1,9},{9,1},{17,25},{25,17},{2,10},{10... | collective-permute-start | bytes 1966088 | tf_op jit(solution)/shard_map/ppermute | solution.py:1094
  26.2 47.2 %all-to-all-start = ((bf16[4,256,1152]{2,1,0:T(8,128)(2,1)}), bf16[4,256,1152]{2,1,0:T(8,128)(2,1)S(1)}, u32[]{:S(2)}, u32[]{:S(2)}) async-start(bf16[4,256,1152]{2,1,0:T(8,128)(2,1)} %broadcast_in_dim.24), calls=%async_computation | async-start | bytes 4718592 | tf_op jit(solution)/shard_map/all_to_all | solution.py:1052
  78.9 59.7 %all-to-all-start.1 = ((bf16[4,256,2304]{2,1,0:T(8,128)(2,1)}), bf16[4,256,2304]{2,1,0:T(8,128)(2,1)}, u32[]{:S(2)}, u32[]{:S(2)}) async-start(bf16[4,256,2304]{2,1,0:T(8,128)(2,1)} %by_owner.1), calls=%async_computation.1 | async-start | bytes 9437184 | tf_op jit(solution)/shard_map/all_to_all | solution.py:1052
  86.9 24.8 %collective-permute-start.16 = (bf16[256,512]{1,0:T(8,128)(2,1)S(1)}, bf16[256,512]{1,0:T(8,128)(2,1)S(1)}, u32[]{:S(2)}, u32[]{:S(2)}) collective-permute-start(bf16[256,512]{1,0:T(8,128)(2,1)S(1)} %pad_maximum_fusion.4), channel_id=1, source_target_pairs={{0,2},{1,3},{2,0},{3,1},{4,6},{5,7},{6,4},{7,5},{8,10},{9,11},{10,... | collective-permute-start | bytes 786440 | tf_op jit(solution)/shard_map/ppermute | solution.py:1049
  88.0 23.7 %collective-permute-start.15 = (bf16[256,512]{1,0:T(8,128)(2,1)S(1)}, bf16[256,512]{1,0:T(8,128)(2,1)S(1)}, u32[]{:S(2)}, u32[]{:S(2)}) collective-permute-start(bf16[256,512]{1,0:T(8,128)(2,1)S(1)} %pad_maximum_fusion.4), channel_id=1, source_target_pairs={{0,1},{1,0},{2,3},{3,2},{4,5},{5,4},{6,7},{7,6},{8,9},{9,8},{10,11... | collective-permute-start | bytes 786440 | tf_op jit(solution)/shard_map/ppermute | solution.py:1049
  111.9 48.3 %collective-permute-start.26 = (bf16[256,2176]{1,0:T(8,128)(2,1)S(1)}, bf16[256,2176]{1,0:T(8,128)(2,1)}, u32[]{:S(2)}, u32[]{:S(2)}) collective-permute-start(bf16[256,2176]{1,0:T(8,128)(2,1)S(1)} %constant_dynamic-update-slice_fusion.3.refs_1_.refs_4_), channel_id=1, source_target_pairs={{0,16},{8,24},{16,0},{24,8},{1,17},{9,25},{17,1},{25,9},{2,18},{10... | collective-permute-start | bytes 3342344 | tf_op jit(solution)/shard_map/ppermute | solution.py:1094
  113.9 46.2 %collective-permute-start.25 = (bf16[256,2176]{1,0:T(8,128)(2,1)S(1)}, bf16[256,2176]{1,0:T(8,128)(2,1)}, u32[]{:S(2)}, u32[]{:S(2)}) collective-permute-start(bf16[256,2176]{1,0:T(8,128)(2,1)S(1)} %constant_dynamic-update-slice_fusion.3.refs_1_.refs_4_), channel_id=1, source_target_pairs={{0,8},{8,0},{16,24},{24,16},{1,9},{9,1},{17,25},{25,17},{2,10},{10... | collective-permute-start | bytes 3342344 | tf_op jit(solution)/shard_map/ppermute | solution.py:1094
  164.4 34.7 %collective-permute-start.27 = (bf16[4,256,2304]{2,1,0:T(8,128)(2,1)}, bf16[4,256,2304]{2,1,0:T(8,128)(2,1)S(1)}, u32[]{:S(2)}, u32[]{:S(2)}) collective-permute-start(bf16[4,256,2304]{2,1,0:T(8,128)(2,1)} %all-to-all-done.1.refs_2_.refs_4_), channel_id=1, source_target_pairs={{0,4},{4,0},{1,5},{5,1},{2,6},{6,2},{3,7},{7,3},{8,12},{12,8},{9,1... | collective-permute-start | bytes 14155784 | tf_op jit(solution)/shard_map/ppermute | solution.py:1046
  166.0 45.5 %collective-permute-start.30 = (bf16[256,2048]{1,0:T(8,128)(2,1)S(1)}, bf16[256,2048]{1,0:T(8,128)(2,1)S(1)}, u32[]{:S(2)}, u32[]{:S(2)}) collective-permute-start(bf16[256,2048]{1,0:T(8,128)(2,1)S(1)} %second_norm.1.refs_0_), channel_id=1, source_target_pairs={{0,24},{8,16},{16,8},{24,0},{1,25},{9,17},{17,9},{25,1},{2,26},{10... | collective-permute-start | bytes 3145736 | tf_op jit(solution)/shard_map/ppermute | solution.py:1094
  166.7 47.8 %collective-permute-start.29 = (bf16[256,2048]{1,0:T(8,128)(2,1)S(1)}, bf16[256,2048]{1,0:T(8,128)(2,1)S(1)}, u32[]{:S(2)}, u32[]{:S(2)}) collective-permute-start(bf16[256,2048]{1,0:T(8,128)(2,1)S(1)} %second_norm.1.refs_0_), channel_id=1, source_target_pairs={{0,16},{8,24},{16,0},{24,8},{1,17},{9,25},{17,1},{25,9},{2,18},{10... | collective-permute-start | bytes 3145736 | tf_op jit(solution)/shard_map/ppermute | solution.py:1094
  168.0 47.3 %collective-permute-start.28 = (bf16[256,2048]{1,0:T(8,128)(2,1)S(1)}, bf16[256,2048]{1,0:T(8,128)(2,1)S(1)}, u32[]{:S(2)}, u32[]{:S(2)}) collective-permute-start(bf16[256,2048]{1,0:T(8,128)(2,1)S(1)} %second_norm.1.refs_0_), channel_id=1, source_target_pairs={{0,8},{8,0},{16,24},{24,16},{1,9},{9,1},{17,25},{25,17},{2,10},{10... | collective-permute-start | bytes 3145736 | tf_op jit(solution)/shard_map/ppermute | solution.py:1094
  226.6 26.0 %collective-permute-start.34 = (bf16[256,2048]{1,0:T(8,128)(2,1)}, bf16[256,2048]{1,0:T(8,128)(2,1)S(1)}, u32[]{:S(2)}, u32[]{:S(2)}) collective-permute-start(bf16[256,2048]{1,0:T(8,128)(2,1)} %get-tuple-element.262), channel_id=1, source_target_pairs={{0,24},{8,16},{16,8},{24,0},{1,25},{9,17},{17,9},{25,1},{2,26},{10... | collective-permute-start | bytes 3145736 | tf_op jit(solution)/shard_map/ppermute | solution.py:1094
  252.6 25.6 %collective-permute-start.35 = (bf16[256,2048]{1,0:T(8,128)(2,1)}, bf16[256,2048]{1,0:T(8,128)(2,1)S(1)}, u32[]{:S(2)}, u32[]{:S(2)}) collective-permute-start(bf16[256,2048]{1,0:T(8,128)(2,1)} %get-tuple-element.280), channel_id=1, source_target_pairs={{0,8},{8,0},{16,24},{24,16},{1,9},{9,1},{17,25},{25,17},{2,10},{10... | collective-permute-start | bytes 3145736 | tf_op jit(solution)/shard_map/ppermute | solution.py:1094
  253.2 25.0 %collective-permute-start.36 = (bf16[256,2048]{1,0:T(8,128)(2,1)}, bf16[256,2048]{1,0:T(8,128)(2,1)S(1)}, u32[]{:S(2)}, u32[]{:S(2)}) collective-permute-start(bf16[256,2048]{1,0:T(8,128)(2,1)} %copy-done.50), channel_id=1, source_target_pairs={{0,16},{8,24},{16,0},{24,8},{1,17},{9,25},{17,1},{25,9},{2,18},{10... | collective-permute-start | bytes 3145736 | tf_op jit(solution)/shard_map/ppermute | solution.py:1094
  278.2 28.0 %collective-permute-start.44 = (bf16[256,2048]{1,0:T(8,128)(2,1)S(1)}, bf16[256,2048]{1,0:T(8,128)(2,1)}, u32[]{:S(2)}, u32[]{:S(2)}) collective-permute-start(bf16[256,2048]{1,0:T(8,128)(2,1)S(1)} %copy-done.49), channel_id=1, source_target_pairs={{0,8},{8,0},{16,24},{24,16},{1,9},{9,1},{17,25},{25,17},{2,10},{10... | collective-permute-start | bytes 3145736 | tf_op jit(solution)/shard_map/ppermute | solution.py:1094
  278.8 27.4 %collective-permute-start.45 = (bf16[256,2048]{1,0:T(8,128)(2,1)S(1)}, bf16[256,2048]{1,0:T(8,128)(2,1)}, u32[]{:S(2)}, u32[]{:S(2)}) collective-permute-start(bf16[256,2048]{1,0:T(8,128)(2,1)S(1)} %get-tuple-element.300), channel_id=1, source_target_pairs={{0,16},{8,24},{16,0},{24,8},{1,17},{9,25},{17,1},{25,9},{2,18},{10... | collective-permute-start | bytes 3145736 | tf_op jit(solution)/shard_map/ppermute | solution.py:1094
  306.3 62.3 %all-to-all-start.2 = ((bf16[4,256,2432]{2,1,0:T(8,128)(2,1)}), bf16[4,256,2432]{2,1,0:T(8,128)(2,1)}, u32[]{:S(2)}, u32[]{:S(2)}) async-start(bf16[4,256,2432]{2,1,0:T(8,128)(2,1)} %weight_grads.7), calls=%async_computation.2 | async-start | bytes 9961472 | tf_op jit(solution)/shard_map/all_to_all | solution.py:1052
  387.7 29.4 %all-to-all-start.3 = ((bf16[4,256,1024]{2,1,0:T(8,128)(2,1)}), bf16[4,256,1024]{2,1,0:T(8,128)(2,1)S(1)}, u32[]{:S(2)}, u32[]{:S(2)}) async-start(bf16[4,256,1024]{2,1,0:T(8,128)(2,1)} %copy-done.5), calls=%async_computation.3 | async-start | bytes 4194304 | tf_op jit(solution)/shard_map/all_to_all | solution.py:1052
  418.4 42.4 %all-to-all-start.4 = ((bf16[4,256,1280]{2,1,0:T(8,128)(2,1)}), bf16[4,256,1280]{2,1,0:T(8,128)(2,1)S(1)}, u32[]{:S(2)}, u32[]{:S(2)}) async-start(bf16[4,256,1280]{2,1,0:T(8,128)(2,1)} %copy-done.4), calls=%async_computation.4 | async-start | bytes 5242880 | tf_op jit(solution)/shard_map/all_to_all | solution.py:1052
  429.3 23.8 %collective-permute-start.63 = (bf16[288,512]{1,0:T(8,128)(2,1)}, bf16[288,512]{1,0:T(8,128)(2,1)}, u32[]{:S(2)}, u32[]{:S(2)}) collective-permute-start(bf16[288,512]{1,0:T(8,128)(2,1)} %get-tuple-element.351), channel_id=1, source_target_pairs={{0,2},{1,3},{2,0},{3,1},{4,6},{5,7},{6,4},{7,5},{8,10},{9,11},{10,... | collective-permute-start | bytes 884744 | tf_op jit(solution)/shard_map/ppermute | solution.py:1049
  429.5 23.6 %collective-permute-start.64 = (bf16[288,512]{1,0:T(8,128)(2,1)}, bf16[288,512]{1,0:T(8,128)(2,1)}, u32[]{:S(2)}, u32[]{:S(2)}) collective-permute-start(bf16[288,512]{1,0:T(8,128)(2,1)} %get-tuple-element.352), channel_id=1, source_target_pairs={{0,3},{1,2},{2,1},{3,0},{4,7},{5,6},{6,5},{7,4},{8,11},{9,10},{10,... | collective-permute-start | bytes 884744 | tf_op jit(solution)/shard_map/ppermute | solution.py:1049
  (130 other events, 1661.5 us)
